TPU v7x, 32 devices: a whole 2x2x4 slice. The times are simulated.
32 devices in a mesh: groups: 2 (over y), tensor: 4 (over z), request: 4 (over x, core).
Axes of the slice: x: 2, y: 2, z: 4, core: 2. Of those that a mesh axis runs over, the one named last changes fastest.
Arguments:
- q_nope: bfloat16 [1536, 16384], P(('groups', 'request'), 'tensor'), parts along dimension 0, may hold values from -6 to 6
- q_rope: bfloat16 [1536, 8192], P(('groups', 'request'), 'tensor'), parts along dimension 0, may hold values from -8 to 8
- latent_keys: bfloat16 [32, 512, 576], P(('groups', 'request'), 'tensor'), parts along dimension 0, may hold values from -8 to 8
- w_key: bfloat16 [128, 512, 128], P('tensor'), may hold values from -0.25 to 0.25
- w_value: bfloat16 [128, 512, 128], P('tensor'), may hold values from -4 to 4
- w_out: bfloat16 [16384, 7168], P('tensor', 'request'), may hold values from -0.046875 to 0.046875
- prefix_len: int32 [32], P(('groups', 'request')), parts along dimension 0, may hold values from 256 to 464
- stretch_len: int32 [32], P(('groups', 'request')), parts along dimension 0, may hold values from 12 to 48
- finished: int32 [32], P(('groups', 'request')), parts along dimension 0, may hold values 0 or 1
- owners: int32 [32, 4], P(('groups', 'request'), 'tensor'), parts along dimension 0, may hold values from 0 to 3, as said below
Outputs:
- mixed: bfloat16 [8, 192, 7168], P(('groups', 'request'), 'tensor'), parts along dimension 0
- handed: bfloat16 [8, 4, 512, 576], P(('groups', 'request'), None, 'tensor'), parts along dimension 0
There are 2 independent parts, one for each index of `groups`. A program takes and returns all parts, laid end to end along the dimension named above; an argument that names none is the same for every part. Nothing has to cross between parts.
Inputs may be any that keep to these rules, and one draw needn't show every extreme that they name: For each block index, the 4 requests of one request rank name distinct owners.
All inputs are finite; a program needn't handle non-finite values. No bound on the sum of `finished` on one device may be relied on, other than what follows from the above.
Results may differ from a plain program's by a relative error of at most 0.012.
Values may be sent and summed in bfloat16 or wider, within the bound.
No kernel may reach another device: no remote copies, remote signals or barrier semaphores. Data moves between devices by JAX's collectives and lax.ppermute only.
A program may use at most 256 MiB of HBM per device.

v0:
```python
import jax
import jax.numpy as jnp
from jax import lax
from jax.sharding import PartitionSpec as P


def local(
    q_nope, q_rope, latent_keys, w_key, w_value, w_out, prefix_len, stretch_len, finished, owners
):
    request_count = prefix_len.shape[0]
    row_count = q_nope.shape[0]
    stretch_size = row_count // request_count
    head_count = w_key.shape[0]
    latent_width = w_key.shape[1]
    nope_width = w_key.shape[2]
    value_width = w_value.shape[2]
    rotary_width = q_rope.shape[1] // head_count
    block_size = latent_keys.shape[1]
    key_width = latent_keys.shape[2]
    score_scale = (nope_width + rotary_width) ** (-0.5)
    queries = q_nope.reshape(request_count, stretch_size, head_count, nope_width)
    absorbed = jnp.einsum(
        "kihd,hcd->kihc", queries, w_key, preferred_element_type=jnp.float32
    ).astype(jnp.bfloat16)
    rotary = q_rope.reshape(request_count, stretch_size, head_count, rotary_width)
    full_query = jnp.concatenate([absorbed, rotary], axis=3)
    query_pos = prefix_len[:, None] + jnp.arange(stretch_size, dtype=jnp.int32)[None, :]
    key_piece = lax.all_gather(latent_keys, "tensor", axis=1, tiled=True)
    running_max = jnp.full((request_count, stretch_size, head_count), -1e30, jnp.float32)
    scores = (
        jnp.einsum("kihc,kjc->kihj", full_query, key_piece, preferred_element_type=jnp.float32)
        * score_scale
    )
    key_pos = jnp.arange(key_piece.shape[1], dtype=jnp.int32)
    visible = key_pos[None, None, :] <= query_pos[:, :, None]
    scores = jnp.where(visible[:, :, None, :], scores, -1e30)
    new_max = jnp.maximum(running_max, jnp.max(scores, axis=3))
    weights = jnp.exp(scores - new_max[:, :, :, None])
    denom_sum = jnp.sum(weights, axis=3)
    added = jnp.einsum(
        "kihj,kjc->kihc",
        weights.astype(jnp.bfloat16),
        key_piece[:, :, :latent_width],
        preferred_element_type=jnp.float32,
    )
    accum = added
    running_max, denom_sum, accum = (new_max, denom_sum, accum)
    latent_out = (accum / denom_sum[:, :, :, None]).astype(jnp.bfloat16)
    head_out = jnp.einsum(
        "kihc,hcv->kihv", latent_out, w_value, preferred_element_type=jnp.float32
    ).astype(jnp.bfloat16)
    live_rows = jnp.arange(stretch_size, dtype=jnp.int32)[None, :] < stretch_len[:, None]
    head_out = jnp.where(live_rows[:, :, None, None], head_out, jnp.zeros_like(head_out))
    head_rows = head_out.reshape(row_count, head_count * value_width)
    rank_count = lax.axis_size("request")
    tensor_count = lax.axis_size("tensor")
    share_rows = row_count // tensor_count
    terms = jnp.dot(
        head_rows,
        lax.all_gather(w_out, "request", axis=1, tiled=True),
        preferred_element_type=jnp.float32,
    )
    summed = lax.psum_scatter(terms.astype(jnp.bfloat16), "tensor", scatter_dimension=0, tiled=True)
    mixed = summed.reshape(1, share_rows, summed.shape[1])
    block_index = lax.axis_index("tensor")
    seq_ends = prefix_len + stretch_len
    positions = block_index * block_size + jnp.arange(block_size, dtype=jnp.int32)
    live_keys = (positions[None, :] < seq_ends[:, None]) & (finished[:, None] > 0)
    kept = jnp.where(live_keys[:, :, None], latent_keys, jnp.zeros_like(latent_keys))
    owner_here = owners[:, 0]
    routing = (owner_here[:, None] == jnp.arange(rank_count, dtype=jnp.int32)[None, :]).astype(
        jnp.bfloat16
    )
    outgoing = jnp.einsum("ko,kjc->ojc", routing, kept, preferred_element_type=jnp.float32).astype(
        jnp.bfloat16
    )
    arrived = lax.all_to_all(outgoing, "request", split_axis=0, concat_axis=0, tiled=True)
    handed = arrived.reshape(1, rank_count, block_size, key_width)
    return (mixed, handed)


def solution(mesh):
    placed = (
        P(("groups", "request"), "tensor"),
        P(("groups", "request"), "tensor"),
        P(("groups", "request"), "tensor", None),
        P("tensor", None, None),
        P("tensor", None, None),
        P("tensor", "request"),
        P(("groups", "request")),
        P(("groups", "request")),
        P(("groups", "request")),
        P(("groups", "request"), "tensor"),
    )
    return jax.shard_map(
        local,
        mesh=mesh,
        in_specs=placed,
        out_specs=(
            P(("groups", "request"), "tensor", None),
            P(("groups", "request"), None, "tensor", None),
        ),
        check_vma=False,
    )
```

profile of v0, /device:TPU:0, one launch (start us, length us, event | category | flops | bytes accessed | tf_op | source)
XLA Modules:
  0.0 493.8 jit_solution(15584289638832569570)
XLA Ops:
  7.2 0.0 all-gather.3.cloned.1.call-start
  7.2 0.7 all-gather.3.cloned.1.call-update
  7.9 0.0 all-gather.5.cloned.1.call-start
  8.0 0.7 all-gather.5.cloned.1.call-update
  8.7 0.0 reduce-scatter.2.cloned.1.call-start
  8.7 0.6 copy-done.1
  9.3 0.3 copy.38
  9.6 0.6 copy.25
  10.3 2.7 reshape.118
  13.0 1.8 copy.26
  14.7 0.1 iota_compare_fusion.2
  14.8 0.1 iota_add_fusion
  14.9 0.1 iota_compare_fusion
  15.0 8.5 %fusion.29 = f32[32,512,192]{1,2,0} fusion(bf16[32,512,128]{2,1,0:T(8,128)(2,1)} %param.13, bf16[32,128,192]{1,2,0:T(8,128)(2,1)S(1)} %bitcast.50), kind=kOutput, calls=%fused_computation.34 | convolution fusion | flops 805306368 | bytes 18350080
  23.5 5.6 %convert_bitcast_fusion = bf16[4,48,32,512]{3,1,0,2:T(8,128)(2,1)S(1)} fusion(f32[32,512,4,48]{1,3,2,0:T(8,128)} %bitcast.49), kind=kLoop, calls=%fused_computation.12 | loop fusion | flops 3145728 | bytes 18874368 | tf_op jit(solution)/shard_map/convert_element_type | solution.py:24
  29.1 5.8 %pad_maximum_fusion = bf16[4,48,32,576]{3,1,0,2:T(8,128)(2,1)} fusion(bf16[4,48,32,64]{3,1,0,2:T(8,128)(2,1)} %copy.26, bf16[4,48,32,512]{3,1,0,2:T(8,128)(2,1)S(1)} %convert_bitcast_fusion), kind=kLoop, calls=%fused_computation.7 | loop fusion | flops 14155776 | bytes 14155776 | tf_op jit(solution)/shard_map/concatenate | solution.py:26
  34.9 27.9 %all-gather.3.cloned.1.call-done = bf16[4,512,576]{1,2,0:T(8,128)(2,1)} async-done(((bf16[4,128,576]{1,2,0:T(8,128)(2,1)}), bf16[4,512,576]{1,2,0:T(8,128)(2,1)}) %all-gather.3.cloned.1.call-update) | async-done | bytes 2359312 | tf_op jit(solution)/shard_map/all_gather | solution.py:28
  62.9 13.0 %fusion = (f32[4,48,32]{2,1,0:T(8,128)S(1)}, f32[4,48,32,512]{3,2,1,0:T(8,128)S(1)}) fusion(pred[4,48,512]{2,1,0:T(8,128)(4,1)S(1)} %iota_compare_fusion, bf16[4,512,576]{1,2,0:T(8,128)(2,1)} %all-gather.3.cloned.1.call-done, bf16[4,48,32,576]{3,1,0,2:T(8,128)(2,1)} %pad_maximum_fusion), kind=kOutput, calls=%fused_computation.3 | convolution fusion | flops 3633309696 | bytes 22142976 | tf_op jit(solution)/shard_map/kihc,kjc->kihj/dot_general | solution.py:31
  75.9 6.2 %fusion.2 = (bf16[4,48,32,512]{3,2,1,0:T(8,128)(2,1)}, f32[4,48,32]{2,1,0:T(8,128)S(1)}) fusion(f32[4,48,32,512]{3,2,1,0:T(8,128)S(1)} %get-tuple-element.9, f32[4,48,32]{2,1,0:T(8,128)S(1)} %broadcast_maximum_fusion, pred[4,48,512]{2,1,0:T(8,128)(4,1)S(1)} %iota_compare_fusion), kind=kLoop, calls=%fused_computation.5 | loop fusion | flops 15722496 | bytes 19021824 | tf_op jit(solution)/shard_map/convert_element_type | solution.py:42
  82.1 0.1 copy.30
  82.1 0.0 copy-done.3
  82.2 13.3 %select_bitcast_fusion = bf16[4,48,32,128]{3,1,0,2:T(8,128)(2,1)} fusion(pred[4,48]{1,0:T(4,128)(4,1)S(1)} %iota_compare_fusion.2, bf16[32,512,128]{2,1,0:T(8,128)(2,1)} %param.14, f32[4,48,32]{1,0,2:T(4,128)S(1)} %copy.30, bf16[4,48,32,512]{3,2,1,0:T(8,128)(2,1)} %get-tuple-element.6, bf16[4,512,576]{1,2,0:T(8,128)(2,1)S(1)} %copy-done.3), kind=kOutput, calls=%fused_computation.20 | convolution fusion | flops 4034396160 | bytes 14221824 | tf_op jit(solution)/shard_map/kihc,hcv->kihv/dot_general | solution.py:49
  95.5 2.6 copy.31
  98.1 310.6 %all-gather.5.cloned.1.call-done = bf16[4096,7168]{1,0:T(8,128)(2,1)} async-done(((bf16[4096,1792]{1,0:T(8,128)(2,1)}), bf16[4096,7168]{1,0:T(8,128)(2,1)}) %all-gather.5.cloned.1.call-update) | async-done | bytes 58720272 | tf_op jit(solution)/shard_map/all_gather | solution.py:60
  408.6 23.4 %convolution_convert_fusion = bf16[192,7168]{1,0:T(8,128)(2,1)} fusion(bf16[4096,7168]{1,0:T(8,128)(2,1)} %all-gather.5.cloned.1.call-done, bf16[24,8,32,128]{3,2,1,0:T(8,128)(2,1)S(1)} %bitcast.54), kind=kOutput, calls=%fused_computation.6 | convolution fusion | flops 11275665408 | bytes 63045632 | tf_op jit(solution)/shard_map/dot_general | solution.py:58
  432.1 0.0 reduce-scatter.2.cloned.1.call-update
  432.1 0.1 compare_and_fusion
  432.3 0.5 convolution_convert_fusion.1
  432.8 0.1 copy.33
  432.9 11.9 %all_to_all.5 = bf16[4,128,576]{1,2,0:T(8,128)(2,1)S(1)} all-to-all(bf16[4,128,576]{1,2,0:T(8,128)(2,1)S(1)} %copy.33), channel_id=1, replica_groups=mesh['groups'=2,'tensor'=4,'request'=4] {'request'}, dimensions={0} | all-to-all | bytes 1179648 | tf_op jit(solution)/shard_map/all_to_all | solution.py:77
  444.8 41.6 %reduce-scatter.2.cloned.1.call-done = bf16[48,7168]{1,0:T(8,128)(2,1)} async-done(((bf16[192,7168]{1,0:T(8,128)(2,1)}), bf16[48,7168]{1,0:T(8,128)(2,1)}) %reduce-scatter.2.cloned.1.call-update) | async-done | bytes 688144 | tf_op jit(solution)/shard_map/reduce_scatter | solution.py:63
  486.4 0.8 copy.61
  (17 shorter events, 0.1 us)
Async XLA Ops:
  7.2 55.7 %all-gather.3.cloned.1.call-start = ((), (), s32[]{:S(2)}) async-start(), calls=%async_computation.2 | async-start | bytes 2949120 | tf_op jit(solution)/shard_map/all_gather | solution.py:28
  7.9 1.4 copy-start.1
  7.9 400.7 %all-gather.5.cloned.1.call-start = ((), (), s32[]{:S(2)}) async-start(), calls=%async_computation.3 | async-start | bytes 73400320 | tf_op jit(solution)/shard_map/all_gather | solution.py:60
  8.7 6.1 %copy-start.4 = (s32[4]{0:T(128)S(1)}, s32[4]{0:T(128)}, u32[]{:S(2)}) copy-start(s32[4]{0:T(128)} %param.17) | copy-start | bytes 52
  8.7 6.1 %copy-start.2 = (s32[4]{0:T(128)S(1)}, s32[4]{0:T(128)}, u32[]{:S(2)}) copy-start(s32[4]{0:T(128)} %param.16) | copy-start | bytes 52
  8.7 477.7 %reduce-scatter.2.cloned.1.call-start = ((), (), s32[]{:S(2)}) async-start(), calls=%async_computation.4 | async-start | bytes 3440640 | tf_op jit(solution)/shard_map/reduce_scatter | solution.py:63
  75.9 6.3 %copy-start.3 = (bf16[4,512,576]{1,2,0:T(8,128)(2,1)S(1)}, bf16[4,512,576]{1,2,0:T(8,128)(2,1)}, u32[]{:S(2)}) copy-start(bf16[4,512,576]{1,2,0:T(8,128)(2,1)} %all-gather.3.cloned.1.call-done) | copy-start | bytes 7077892
  408.6 23.5 %copy-start.5 = (s32[4]{0:T(128)S(1)}, s32[4]{0:T(128)}, u32[]{:S(2)}) copy-start(s32[4]{0:T(128)} %param.18) | copy-start | bytes 52
  408.6 23.6 %copy-start = (bf16[4,128,576]{1,2,0:T(8,128)(2,1)S(1)}, bf16[4,128,576]{1,2,0:T(8,128)(2,1)}, u32[]{:S(2)}) copy-start(bf16[4,128,576]{1,2,0:T(8,128)(2,1)} %param.12) | copy-start | bytes 1769476
  408.6 23.6 %copy-start.6 = (s32[4,1]{0,1:T(1,128)S(1)}, s32[4,1]{0,1:T(1,128)}, u32[]{:S(2)}) copy-start(s32[4,1]{0,1:T(1,128)} %param.19) | copy-start | bytes 52
Sparse Core Ops, SparseCore 0:
  9.6 53.2 all-gather.2
  64.4 344.1 all-gather.4
  432.2 54.1 reduce-scatter.1
where the time goes:
time: 494 us
  waiting for transfers between devices  381 us (77%)
  matrix products  58.8 us (12%)
  other arithmetic  18 us (4%)
  between operations  13.9 us (3%)
  blocking collectives  11.9 us (2%)
  local copies, waits for them, and re-layouts  9.55 us (2%)
    all_gather x1, waiting for transfers between devices, local(): lax.all_gather(w_out, 'request', axis=1, tiled=True)  311 us
    reduce_scatter x1, waiting for transfers between devices, local(): lax.psum_scatter(terms.astype(jnp.bfloat16), 'tensor', scatter_dimension=...  41.6 us
    all_gather x1, waiting for transfers between devices, local(): key_piece = lax.all_gather(latent_keys, 'tensor', axis=1, tiled=True)  27.9 us
    dot_general x1, matrix products, local(): jnp.dot(head_rows, lax.all_gather(w_out, 'request', axis=1, tiled=True),...  23.4 us
    dot_general x1, matrix products, local(): jnp.einsum('kihc,hcv->kihv', latent_out, w_value, preferred_element_type=...  13.3 us
    dot_general x1, matrix products, local(): jnp.einsum('kihc,kjc->kihj', full_query, key_piece, preferred_element_typ...  13 us
    all_to_all x1, blocking collectives, local(): lax.all_to_all(outgoing, 'request', split_axis=0, concat_axis=0, tiled=True)  11.9 us
  transfers between devices with their start and end apart: 3, of which 3 were waited for; matrix products, arithmetic and copies ran while one was open for 12% of the time, Pallas kernels for 0%

commit v1 on v0

--- a/solution.py
+++ b/solution.py
@@ -51,17 +51,24 @@
     ).astype(jnp.bfloat16)
     live_rows = jnp.arange(stretch_size, dtype=jnp.int32)[None, :] < stretch_len[:, None]
     head_out = jnp.where(live_rows[:, :, None, None], head_out, jnp.zeros_like(head_out))
-    head_rows = head_out.reshape(row_count, head_count * value_width)
     rank_count = lax.axis_size("request")
     tensor_count = lax.axis_size("tensor")
     share_rows = row_count // tensor_count
+    head_rows = head_out.reshape(tensor_count, share_rows, head_count * value_width)
+    all_rows = lax.all_gather(head_rows, "request", axis=1, tiled=True)
     terms = jnp.dot(
-        head_rows,
-        lax.all_gather(w_out, "request", axis=1, tiled=True),
+        all_rows.reshape(rank_count * row_count, head_count * value_width),
+        w_out,
         preferred_element_type=jnp.float32,
+    ).astype(jnp.bfloat16)
+    summed = lax.psum_scatter(terms, "tensor", scatter_dimension=0, tiled=True)
+    mixed = lax.all_to_all(
+        summed.reshape(rank_count, share_rows, w_out.shape[1]),
+        "request",
+        split_axis=0,
+        concat_axis=2,
+        tiled=True,
     )
-    summed = lax.psum_scatter(terms.astype(jnp.bfloat16), "tensor", scatter_dimension=0, tiled=True)
-    mixed = summed.reshape(1, share_rows, summed.shape[1])
     block_index = lax.axis_index("tensor")
     seq_ends = prefix_len + stretch_len
     positions = block_index * block_size + jnp.arange(block_size, dtype=jnp.int32)

time: 494 us -> 236 us (0.48)
  waiting for transfers between devices: 381 us -> 125 us
  matrix products: 58.8 us -> 53 us
    all_gather x1, waiting for transfers between devices: 311 us -> 44.7 us  [local(): all_rows = lax.all_gather(head_rows, 'request', axis=1, tiled=True)]
    all_to_all x0 -> x1, waiting for transfers between devices: none -> 10.6 us  [local(): lax.all_to_all(summed.reshape(rank_count, share_rows, w_out.shape[1]), 'r...]
  transfers between devices with their start and end apart: 3 -> 4, of which waited for: 3 -> 4; matrix products, arithmetic and copies ran while one was open for 12% -> 12% of each run, Pallas kernels for 0% -> 0%
where the time goes in v1:
time: 236 us
  waiting for transfers between devices  125 us (53%)
  matrix products  53 us (22%)
  other arithmetic  17.8 us (8%)
  between operations  13.9 us (6%)
  blocking collectives  11.9 us (5%)
  local copies, waits for them, and re-layouts  10.3 us (4%)
  starting transfers between devices  3.6 us (2%)
    all_gather x1, waiting for transfers between devices, local(): all_rows = lax.all_gather(head_rows, 'request', axis=1, tiled=True)  44.7 us
    reduce_scatter x1, waiting for transfers between devices, local(): summed = lax.psum_scatter(terms, 'tensor', scatter_dimension=0, tiled=True)  41.5 us
    all_gather x1, waiting for transfers between devices, local(): key_piece = lax.all_gather(latent_keys, 'tensor', axis=1, tiled=True)  27.9 us
    dot_general x1, matrix products, local(): jnp.dot(all_rows.reshape(rank_count * row_count, head_count * value_width...  18.7 us
    dot_general x1, matrix products, local(): jnp.einsum('kihc,kjc->kihj', full_query, key_piece, preferred_element_typ...  13 us
    dot_general x1, matrix products, local(): jnp.einsum('kihc,hcv->kihv', latent_out, w_value, preferred_element_type=...  12.2 us
    all_to_all x1, blocking collectives, local(): lax.all_to_all(outgoing, 'request', split_axis=0, concat_axis=0, tiled=True)  11.9 us
    all_to_all x1, waiting for transfers between devices, local(): lax.all_to_all(summed.reshape(rank_count, share_rows, w_out.shape[1]), 'r...  10.6 us
  transfers between devices with their start and end apart: 4, of which 4 were waited for; matrix products, arithmetic and copies ran while one was open for 12% of the time, Pallas kernels for 0%

profile of v1, /device:TPU:0, one launch (start us, length us, event | category | flops | bytes accessed | tf_op | source)
XLA Modules:
  0.0 235.9 jit_solution(4812377859305305313)
XLA Ops:
  7.2 0.0 all-gather.3.cloned.1.call-start
  7.2 0.7 all-gather.3.cloned.1.call-update
  7.9 0.0 all-gather.5.cloned.1.call-start
  8.0 1.7 copy.44
  9.7 0.6 copy.28
  10.3 2.7 %reshape.121 = bf16[4,48,32,64]{3,2,1,0:T(8,128)(2,1)S(1)} reshape(bf16[192,2048]{1,0:T(8,128)(2,1)} %param.11) | data formatting | bytes 1572864 | tf_op jit(solution)/shard_map/reshape | solution.py:25
  13.0 1.8 copy.29
  14.8 0.1 iota_compare_fusion.2
  14.9 0.1 iota_add_fusion
  15.0 0.1 iota_compare_fusion
  15.1 8.5 %fusion.27 = f32[32,512,192]{1,2,0} fusion(bf16[32,512,128]{2,1,0:T(8,128)(2,1)} %param.13, bf16[32,128,192]{1,2,0:T(8,128)(2,1)S(1)} %bitcast.57), kind=kOutput, calls=%fused_computation.33 | convolution fusion | flops 805306368 | bytes 18350080
  23.6 5.6 %convert_bitcast_fusion = bf16[4,48,32,512]{3,1,0,2:T(8,128)(2,1)S(1)} fusion(f32[32,512,4,48]{1,3,2,0:T(8,128)} %bitcast.55), kind=kLoop, calls=%fused_computation.11 | loop fusion | flops 3145728 | bytes 18874368 | tf_op jit(solution)/shard_map/convert_element_type | solution.py:24
  29.2 5.8 %pad_maximum_fusion = bf16[4,48,32,576]{3,1,0,2:T(8,128)(2,1)} fusion(bf16[4,48,32,64]{3,1,0,2:T(8,128)(2,1)} %copy.29, bf16[4,48,32,512]{3,1,0,2:T(8,128)(2,1)S(1)} %convert_bitcast_fusion), kind=kLoop, calls=%fused_computation.6 | loop fusion | flops 14155776 | bytes 14155776 | tf_op jit(solution)/shard_map/concatenate | solution.py:26
  35.0 27.9 %all-gather.3.cloned.1.call-done = bf16[4,512,576]{1,2,0:T(8,128)(2,1)} async-done(((bf16[4,128,576]{1,2,0:T(8,128)(2,1)}), bf16[4,512,576]{1,2,0:T(8,128)(2,1)}) %all-gather.3.cloned.1.call-update) | async-done | bytes 2359312 | tf_op jit(solution)/shard_map/all_gather | solution.py:28
  62.9 13.0 %fusion = (f32[4,48,32]{2,1,0:T(8,128)S(1)}, f32[4,48,32,512]{3,2,1,0:T(8,128)S(1)}) fusion(pred[4,48,512]{2,1,0:T(8,128)(4,1)S(1)} %iota_compare_fusion, bf16[4,512,576]{1,2,0:T(8,128)(2,1)} %all-gather.3.cloned.1.call-done, bf16[4,48,32,576]{3,1,0,2:T(8,128)(2,1)} %pad_maximum_fusion), kind=kOutput, calls=%fused_computation.3 | convolution fusion | flops 3633309696 | bytes 22142976 | tf_op jit(solution)/shard_map/kihc,kjc->kihj/dot_general | solution.py:31
  75.9 6.0 %fusion.2 = (bf16[4,48,32,512]{3,2,1,0:T(8,128)(2,1)}, f32[4,48,32]{2,1,0:T(8,128)S(1)}) fusion(f32[4,48,32,512]{3,2,1,0:T(8,128)S(1)} %get-tuple-element.9, f32[4,48,32]{2,1,0:T(8,128)S(1)} %broadcast_maximum_fusion, pred[4,48,512]{2,1,0:T(8,128)(4,1)S(1)} %iota_compare_fusion), kind=kLoop, calls=%fused_computation.5 | loop fusion | flops 15722496 | bytes 19021824 | tf_op jit(solution)/shard_map/convert_element_type | solution.py:42
  81.9 0.1 copy.33
  82.0 12.2 %select_bitcast_fusion = bf16[32,4,6,8,128]{4,3,2,1,0:T(8,128)(2,1)S(1)} fusion(pred[4,48]{1,0:T(4,128)(4,1)S(1)} %iota_compare_fusion.2, bf16[32,512,128]{2,1,0:T(8,128)(2,1)} %param.14, f32[4,48,32]{1,0,2:T(4,128)S(1)} %copy.33, bf16[4,48,32,512]{3,2,1,0:T(8,128)(2,1)} %get-tuple-element.6, bf16[4,512,576]{1,2,0:T(8,128)(2,1)} %all-gather.3.cloned.1.call-done), kind=kOutput, calls=%fused_computation.19 | convolution fusion | flops 4034396160 | bytes 14180544 | tf_op jit(solution)/shard_map/kihc,hcv->kihv/dot_general | solution.py:49
  94.2 1.6 copy.62
  95.8 0.0 all-gather.5.cloned.1.call-update
  95.8 0.0 reduce-scatter.2.cloned.1.call-start
  95.9 44.7 %all-gather.5.cloned.1.call-done = bf16[4,192,4096]{2,1,0:T(8,128)(2,1)} async-done(((bf16[4,48,4096]{2,1,0:T(8,128)(2,1)}), bf16[4,192,4096]{2,1,0:T(8,128)(2,1)}) %all-gather.5.cloned.1.call-update) | async-done | bytes 6291472 | tf_op jit(solution)/shard_map/all_gather | solution.py:58
  140.5 18.7 %convolution_convert_fusion = bf16[768,1792]{1,0:T(8,128)(2,1)} fusion(bf16[768,4096]{1,0:T(8,128)(2,1)} %bitcast.64, bf16[4096,1792]{1,0:T(8,128)(2,1)} %param.15), kind=kOutput, calls=%fused_computation.14 | convolution fusion | flops 11275665408 | bytes 23724032 | tf_op jit(solution)/shard_map/dot_general | solution.py:59
  159.4 0.1 compare_and_fusion
  159.5 0.5 convolution_convert_fusion.1
  160.0 0.1 copy.37
  160.1 11.9 %all_to_all.23 = bf16[4,128,576]{1,2,0:T(8,128)(2,1)S(1)} all-to-all(bf16[4,128,576]{1,2,0:T(8,128)(2,1)S(1)} %copy.37), channel_id=1, replica_groups=mesh['groups'=2,'tensor'=4,'request'=4] {'request'}, dimensions={0} | all-to-all | bytes 1179648 | tf_op jit(solution)/shard_map/all_to_all | solution.py:84
  172.1 41.5 %reduce-scatter.2.cloned.1.call-done = bf16[192,1792]{1,0:T(8,128)(2,1)} async-done(((bf16[768,1792]{1,0:T(8,128)(2,1)}), bf16[192,1792]{1,0:T(8,128)(2,1)}) %reduce-scatter.2.cloned.1.call-update) | async-done | bytes 688144 | tf_op jit(solution)/shard_map/reduce_scatter | solution.py:64
  213.6 3.5 %all-to-all-start = ((bf16[4,48,1792]{2,1,0:T(8,128)(2,1)}), bf16[4,48,1792]{2,1,0:T(8,128)(2,1)S(1)}, u32[]{:S(2)}, u32[]{:S(2)}) async-start(bf16[4,48,1792]{2,1,0:T(8,128)(2,1)} %bitcast.62), calls=%async_computation.1 | async-start | bytes 1376256 | tf_op jit(solution)/shard_map/all_to_all | solution.py:65
  217.1 10.6 %all-to-all-done = bf16[4,48,1792]{2,1,0:T(8,128)(2,1)S(1)} async-done(((bf16[4,48,1792]{2,1,0:T(8,128)(2,1)}), bf16[4,48,1792]{2,1,0:T(8,128)(2,1)S(1)}, u32[]{:S(2)}, u32[]{:S(2)}) %all-to-all-start) | async-done | bytes 688160 | tf_op jit(solution)/shard_map/all_to_all | solution.py:65
  227.7 0.9 copy.43
  228.6 0.8 copy.64
  (16 shorter events, 0.1 us)
Async XLA Ops:
  7.2 7.7 %copy-start.2 = (s32[4]{0:T(128)S(1)}, s32[4]{0:T(128)}, u32[]{:S(2)}) copy-start(s32[4]{0:T(128)} %param.17) | copy-start | bytes 52
  7.2 7.7 %copy-start.1 = (s32[4]{0:T(128)S(1)}, s32[4]{0:T(128)}, u32[]{:S(2)}) copy-start(s32[4]{0:T(128)} %param.16) | copy-start | bytes 52
  7.2 55.7 %all-gather.3.cloned.1.call-start = ((), (), s32[]{:S(2)}) async-start(), calls=%async_computation.3 | async-start | bytes 2949120 | tf_op jit(solution)/shard_map/all_gather | solution.py:28
  7.9 132.6 %all-gather.5.cloned.1.call-start = ((), (), s32[]{:S(2)}) async-start(), calls=%async_computation.4 | async-start | bytes 7864320 | tf_op jit(solution)/shard_map/all_gather | solution.py:58
  95.8 117.8 %reduce-scatter.2.cloned.1.call-start = ((), (), s32[]{:S(2)}) async-start(), calls=%async_computation.5 | async-start | bytes 3440640 | tf_op jit(solution)/shard_map/reduce_scatter | solution.py:64
  140.5 18.8 %copy-start.3 = (s32[4]{0:T(128)S(1)}, s32[4]{0:T(128)}, u32[]{:S(2)}) copy-start(s32[4]{0:T(128)} %param.18) | copy-start | bytes 52
  140.5 18.9 %copy-start = (bf16[4,128,576]{1,2,0:T(8,128)(2,1)S(1)}, bf16[4,128,576]{1,2,0:T(8,128)(2,1)}, u32[]{:S(2)}) copy-start(bf16[4,128,576]{1,2,0:T(8,128)(2,1)} %param.12) | copy-start | bytes 1769476
  140.5 18.9 %copy-start.4 = (s32[4,1]{0,1:T(1,128)S(1)}, s32[4,1]{0,1:T(1,128)}, u32[]{:S(2)}) copy-start(s32[4,1]{0,1:T(1,128)} %param.19) | copy-start | bytes 52
  213.6 14.1 %all-to-all-start = ((bf16[4,48,1792]{2,1,0:T(8,128)(2,1)}), bf16[4,48,1792]{2,1,0:T(8,128)(2,1)S(1)}, u32[]{:S(2)}, u32[]{:S(2)}) async-start(bf16[4,48,1792]{2,1,0:T(8,128)(2,1)} %bitcast.62), calls=%async_computation.1 | async-start | bytes 1376256 | tf_op jit(solution)/shard_map/all_to_all | solution.py:65
Sparse Core Ops, SparseCore 0:
  9.6 53.2 all-gather.2
  95.9 44.5 all-gather.4
  159.4 54.1 reduce-scatter.1

commit v2 on v0

v2 whole, which is shorter than its diff:
```python
import jax
import jax.numpy as jnp
from jax import lax
from jax.sharding import PartitionSpec as P


def swap(value, axis, distance, inner=1):
    size = lax.axis_size(axis)
    pairs = [(i, ((i // inner) ^ distance) * inner + i % inner) for i in range(size)]
    return lax.ppermute(value, axis, pairs)


def by_rank(pieces, rank):
    distance = 1
    while distance < len(pieces):
        flip = (rank & distance) > 0
        pieces = [jnp.where(flip, pieces[k ^ distance], pieces[k]) for k in range(len(pieces))]
        distance *= 2
    return pieces


def gather_ranks(value, axis):
    size = lax.axis_size(axis)
    pieces = {0: value}
    distance = size // 2
    while distance:
        for k in list(pieces):
            pieces[k ^ distance] = swap(pieces[k], axis, distance)
        distance //= 2
    return [pieces[k] for k in range(size)]


def local(
    q_nope, q_rope, latent_keys, w_key, w_value, w_out, prefix_len, stretch_len, finished, owners
):
    request_count = prefix_len.shape[0]
    row_count = q_nope.shape[0]
    stretch_size = row_count // request_count
    head_count = w_key.shape[0]
    latent_width = w_key.shape[1]
    nope_width = w_key.shape[2]
    value_width = w_value.shape[2]
    rotary_width = q_rope.shape[1] // head_count
    block_size = latent_keys.shape[1]
    key_width = latent_keys.shape[2]
    score_scale = (nope_width + rotary_width) ** (-0.5)
    rank_count = lax.axis_size("request")
    tensor_count = lax.axis_size("tensor")
    inner = tensor_count // request_count
    share_rows = row_count // tensor_count
    rank = lax.axis_index("request")
    place = lax.axis_index("tensor")
    outer_place = place // inner

    seq_ends = prefix_len + stretch_len
    positions = place * block_size + jnp.arange(block_size, dtype=jnp.int32)
    live_keys = (positions[None, :] < seq_ends[:, None]) & (finished[:, None] > 0)
    kept = jnp.where(live_keys[:, :, None], latent_keys, jnp.zeros_like(latent_keys))
    targets = rank ^ jnp.arange(rank_count, dtype=jnp.int32)
    routing = (owners[:, :1] == targets[None, :]).astype(jnp.bfloat16)
    outgoing = jnp.einsum("ko,kjc->ojc", routing, kept, preferred_element_type=jnp.float32).astype(
        jnp.bfloat16
    )
    arrived = [outgoing[0]] + [swap(outgoing[k], "request", k) for k in range(1, rank_count)]
    handed = jnp.stack(by_rank(arrived, rank))[None]

    if inner > 1:
        groups = [[o * inner + i for i in range(inner)] for o in range(request_count)]
        own_keys = lax.all_gather(
            latent_keys, "tensor", axis=1, tiled=True, axis_index_groups=groups
        )
    else:
        own_keys = latent_keys
    near = (outer_place // 2) * 2
    far = near ^ 2
    near_keys = lax.dynamic_slice_in_dim(own_keys, near, 2, 0)
    far_keys = lax.dynamic_slice_in_dim(own_keys, far, 2, 0)
    far_two = swap(near_keys, "tensor", 2, inner)
    far_one = swap(far_keys, "tensor", 1, inner)
    far_three = swap(far_two, "tensor", 1, inner)
    near_two = swap(far_keys, "tensor", 2, inner)
    near_one = swap(near_keys, "tensor", 1, inner)
    near_three = swap(near_two, "tensor", 1, inner)
    far_blocks = [far_keys, far_one, far_two, far_three]
    near_blocks = [near_keys, near_one, near_two, near_three]

    queries = q_nope.reshape(row_count, head_count, nope_width)
    absorbed = jnp.einsum(
        "ihd,hcd->hic", queries, w_key, preferred_element_type=jnp.float32
    ).astype(jnp.bfloat16)
    rotary = q_rope.reshape(row_count, head_count, rotary_width).transpose(1, 0, 2)
    full_query = jnp.concatenate([absorbed, rotary], axis=2)
    span = own_keys.shape[1]
    key_pos = jnp.concatenate(
        [(outer_place ^ k) * span + jnp.arange(span, dtype=jnp.int32) for k in range(4)]
    )

    def stage(distance):
        request = outer_place ^ distance
        blocks = far_blocks if distance >= 2 else near_blocks
        keys = jnp.concatenate(
            [lax.dynamic_index_in_dim(b, request % 2, 0, False) for b in blocks], axis=0
        )
        query = lax.dynamic_slice_in_dim(full_query, request * stretch_size, stretch_size, 1)
        scores = (
            jnp.einsum("hic,jc->hij", query, keys, preferred_element_type=jnp.float32)
            * score_scale
        )
        query_pos = prefix_len[request] + jnp.arange(stretch_size, dtype=jnp.int32)
        visible = key_pos[None, :] <= query_pos[:, None]
        scores = jnp.where(visible[None], scores, -1e30)
        weights = jnp.exp(scores - jnp.max(scores, axis=2, keepdims=True))
        denom = jnp.sum(weights, axis=2, keepdims=True)
        added = jnp.einsum(
            "hij,jc->hic",
            weights.astype(jnp.bfloat16),
            keys[:, :latent_width],
            preferred_element_type=jnp.float32,
        )
        latent_out = (added / denom).astype(jnp.bfloat16)
        head_out = jnp.einsum(
            "hic,hcv->ihv", latent_out, w_value, preferred_element_type=jnp.float32
        ).astype(jnp.bfloat16)
        live = jnp.arange(stretch_size, dtype=jnp.int32) < stretch_len[request]
        head_out = jnp.where(live[:, None, None], head_out, jnp.zeros_like(head_out))
        head_rows = head_out.reshape(stretch_size, head_count * value_width)
        rows = jnp.stack(gather_ranks(head_rows, "request"))
        return jnp.dot(
            rows.reshape(rank_count * stretch_size, head_count * value_width),
            w_out,
            preferred_element_type=jnp.float32,
        )

    opposite = swap(stage(3).astype(jnp.bfloat16), "tensor", 1, inner)
    across = swap((stage(2) + opposite).astype(jnp.bfloat16), "tensor", 2, inner)
    beside = swap(stage(1).astype(jnp.bfloat16), "tensor", 1, inner)
    summed = (stage(0) + beside + across).astype(jnp.bfloat16)
    if inner > 1:
        summed = summed.reshape(rank_count, inner, share_rows, summed.shape[1]).swapaxes(0, 1)
        summed = lax.psum_scatter(
            summed, "tensor", scatter_dimension=0, axis_index_groups=groups, tiled=True
        )
    summed = summed.reshape(rank_count, share_rows, w_out.shape[1])
    columns = [summed[0]] + [swap(summed[k], "request", k) for k in range(1, rank_count)]
    mixed = jnp.concatenate(by_rank(columns, rank), axis=1)[None]
    return (mixed, handed)


def solution(mesh):
    placed = (
        P(("groups", "request"), "tensor"),
        P(("groups", "request"), "tensor"),
        P(("groups", "request"), "tensor", None),
        P("tensor", None, None),
        P("tensor", None, None),
        P("tensor", "request"),
        P(("groups", "request")),
        P(("groups", "request")),
        P(("groups", "request")),
        P(("groups", "request"), "tensor"),
    )
    return jax.shard_map(
        local,
        mesh=mesh,
        in_specs=placed,
        out_specs=(
            P(("groups", "request"), "tensor", None),
            P(("groups", "request"), None, "tensor", None),
        ),
        check_vma=False,
    )
```

time: 494 us -> 187 us (0.38)
  waiting for transfers between devices: 381 us -> 50.7 us
  starting transfers between devices: 0.11 us -> 21.2 us
  local copies, waits for them, and re-layouts: 9.55 us -> 25.3 us
  between operations: 13.9 us -> 1.36 us
  blocking collectives: 11.9 us -> 0 us
  matrix products: 58.8 us -> 66.1 us
    all_gather x2 -> x0, waiting for transfers between devices: 339 us -> none  [the longest x1 311 us: local(): lax.all_gather(w_out, 'request', axis=1, tiled=True)]
    ppermute x0 -> x27, waiting for transfers between devices: none -> 50.7 us  [swap(): return lax.ppermute(value, axis, pairs)]
    reduce_scatter x1 -> x0, waiting for transfers between devices: 41.6 us -> none  [local(): lax.psum_scatter(terms.astype(jnp.bfloat16), 'tensor', scatter_dimension=...]
    ppermute x0 -> x27, starting transfers between devices: none -> 21.2 us  [swap(): return lax.ppermute(value, axis, pairs)]
    dot_general x3 -> x13, matrix products: 49.8 us -> 64.8 us  [the longest x4 25.4 us: stage(): jnp.dot(rows.reshape(rank_count * stretch_size, head_count * value_width)...]
    all_to_all x1 -> x0, blocking collectives: 11.9 us -> none  [local(): lax.all_to_all(outgoing, 'request', split_axis=0, concat_axis=0, tiled=True)]
    convert_element_type x2 -> x0, other arithmetic: 11.7 us -> none  [the longest x1 6.16 us: local(): weights.astype(jnp.bfloat16)]
    unnamed x1 -> x0, matrix products: 8.52 us -> none
  transfers between devices with their start and end apart: 3 -> 27, of which waited for: 3 -> 8; matrix products, arithmetic and copies ran while one was open for 12% -> 51% of each run, Pallas kernels for 0% -> 0%
where the time goes in v2:
time: 187 us; the launch traced here: 186 us
  matrix products  66.1 us (35%)
  waiting for transfers between devices  50.7 us (27%)
  local copies, waits for them, and re-layouts  25.3 us (14%)
  other arithmetic  21.5 us (11%)
  starting transfers between devices  21.2 us (11%)
    ppermute x27, waiting for transfers between devices, swap(): return lax.ppermute(value, axis, pairs)  50.7 us
    dot_general x4, matrix products, stage(): jnp.dot(rows.reshape(rank_count * stretch_size, head_count * value_width)...  25.4 us
    ppermute x27, starting transfers between devices, swap(): return lax.ppermute(value, axis, pairs)  21.2 us
    dot_general x4, matrix products, stage(): jnp.einsum('hic,hcv->ihv', latent_out, w_value, preferred_element_type=jn...  20.5 us
    dot_general x4, matrix products, stage(): jnp.einsum('hic,jc->hij', query, keys, preferred_element_type=jnp.float32)  12.2 us
    unnamed x58, local copies, waits for them, and re-layouts  9.34 us
    squeeze x7, local copies, waits for them, and re-layouts, stage(): lax.dynamic_index_in_dim(b, request % 2, 0, False)  7.14 us
    dot_general x1, matrix products, local(): jnp.einsum('ihd,hcd->hic', queries, w_key, preferred_element_type=jnp.flo...  6.78 us
  transfers between devices with their start and end apart: 27, of which 8 were waited for; matrix products, arithmetic and copies ran while one was open for 51% of the time, Pallas kernels for 0%

profile of v2, /device:TPU:0, one launch (start us, length us, event | category | flops | bytes accessed | tf_op | source)
XLA Modules:
  0.0 186.1 jit_solution(9434427000084600967)
XLA Ops:
  0.7 2.0 %constant_dynamic-slice_fusion.1 = (bf16[2,128,576]{1,2,0:T(8,128)(2,1)}, bf16[2,128,576]{1,2,0:T(8,128)(2,1)}) fusion(bf16[4,128,576]{1,2,0:T(8,128)(2,1)} %param.12, s32[]{:T(128)S(6)} %select_n.245, s32[]{:T(128)S(6)} %select_n.247), kind=kLoop, calls=%fused_computation.146 | loop fusion | bytes 1179656 | tf_op jit(solution)/shard_map/dynamic_slice | solution.py:76
  2.7 3.0 %collective-permute-start = (bf16[2,128,576]{1,2,0:T(8,128)(2,1)}, bf16[2,128,576]{1,2,0:T(8,128)(2,1)}, u32[]{:S(2)}, u32[]{:S(2)}) collective-permute-start(bf16[2,128,576]{1,2,0:T(8,128)(2,1)} %get-tuple-element.23), channel_id=1, source_target_pairs={{0,4},{4,0},{8,12},{12,8},{1,5},{5,1},{9,13},{13,9},{2,6},{6,2},{1... | collective-permute-start | bytes 884744 | tf_op jit(solution)/shard_map/ppermute | solution.py:10
  5.7 2.6 %collective-permute-start.11 = (bf16[2,128,576]{1,2,0:T(8,128)(2,1)}, bf16[2,128,576]{1,2,0:T(8,128)(2,1)}, u32[]{:S(2)}, u32[]{:S(2)}) collective-permute-start(bf16[2,128,576]{1,2,0:T(8,128)(2,1)} %get-tuple-element.23), channel_id=1, source_target_pairs={{0,8},{4,12},{8,0},{12,4},{1,9},{5,13},{9,1},{13,5},{2,10},{6,14},... | collective-permute-start | bytes 884744 | tf_op jit(solution)/shard_map/ppermute | solution.py:10
  17.9 6.8 %convolution_convert_fusion = bf16[32,192,512]{2,1,0:T(8,128)(2,1)} fusion(bf16[32,512,128]{2,1,0:T(8,128)(2,1)} %param.13, bf16[192,4096]{1,0:T(8,128)(2,1)S(1)} %copy-done), kind=kOutput, calls=%fused_computation.8 | convolution fusion | flops 808452096 | bytes 12058624 | tf_op jit(solution)/shard_map/ihd,hcd->hic/dot_general | solution.py:88
  30.5 1.8 collective-permute-start.25
  34.9 1.6 dynamic-slice_bitcast_fusion.9
  36.6 1.5 collective-permute-start.2
  38.1 1.7 dynamic-slice_bitcast_fusion.10
  40.8 3.8 %collective-permute-done.12 = bf16[2,128,576]{1,2,0:T(8,128)(2,1)S(1)} collective-permute-done((bf16[2,128,576]{1,2,0:T(8,128)(2,1)}, bf16[2,128,576]{1,2,0:T(8,128)(2,1)S(1)}, u32[]{:S(2)}, u32[]{:S(2)}) %collective-permute-start.12) | collective-permute-done | bytes 294944 | tf_op jit(solution)/shard_map/ppermute | solution.py:10
  44.6 3.1 %fusion.3 = (f32[32,48]{1,0:T(8,128)S(1)}, f32[32,48,512]{2,1,0:T(8,128)S(1)}) fusion(pred[48,512]{1,0:T(8,128)(4,1)S(1)} %get-tuple-element.41, bf16[128,576]{0,1:T(8,128)(2,1)S(1)} %get-tuple-element.37, bf16[128,576]{0,1:T(8,128)(2,1)S(1)} %get-tuple-element.35, bf16[128,576]{0,1:T(8,128)(2,1)S(1)} %get-tuple-element.33, ...), kind=kOutput, calls=%fused_computation.24 | convolution fusion | flops 914225664 | bytes 10844164 | tf_op jit(solution)/shard_map/hic,jc->hij/dot_general | solution.py:106
  47.7 1.7 copy-done.4
  51.5 5.1 %fusion.82 = bf16[32,48,128]{2,1,0:T(8,128)(2,1)S(1)} fusion(bf16[32,512,128]{2,1,0:T(8,128)(2,1)} %param.14, f32[32,48,512]{2,1,0:T(8,128)} %copy-done.4, f32[32,48]{1,0:T(8,128)S(1)} %fusion.13, f32[32,48]{1,0:T(8,128)S(1)} %get-tuple-element.55, pred[48,512]{1,0:T(8,128)(4,1)S(1)} %get-tuple-element.41, bf16[512,576]{0,1:T(8,128)(2,1)} %get-tuple-element.70, ...), kind=kOutput, calls=%fused_computation.82 | convolution fusion | flops 1011744768 | bytes 8294448 | tf_op jit(solution)/shard_map/hic,hcv->ihv/dot_general | solution.py:121
  60.0 3.1 %fusion.1 = (f32[32,48]{1,0:T(8,128)S(1)}, f32[32,48,512]{2,1,0:T(8,128)S(1)}) fusion(pred[48,512]{1,0:T(8,128)(4,1)S(1)} %get-tuple-element.39, bf16[128,576]{0,1:T(8,128)(2,1)S(1)} %get-tuple-element.31, bf16[128,576]{0,1:T(8,128)(2,1)} %get-tuple-element.29, bf16[128,576]{0,1:T(8,128)(2,1)} %get-tuple-element.27, bf16[128,576]{0,1:T(8,128)(2,1)S(1)} %copy-done.8, ...), kind=kOutput, calls=%fused_computation.22 | convolution fusion | flops 914225664 | bytes 10844164 | tf_op jit(solution)/shard_map/hic,jc->hij/dot_general | solution.py:106
  63.1 1.7 copy-done.3
  66.9 5.1 %fusion.76 = bf16[32,48,128]{2,1,0:T(8,128)(2,1)S(1)} fusion(bf16[32,512,128]{2,1,0:T(8,128)(2,1)} %param.14, f32[32,48,512]{2,1,0:T(8,128)} %copy-done.3, f32[32,48]{1,0:T(8,128)S(1)} %fusion.9, f32[32,48]{1,0:T(8,128)S(1)} %get-tuple-element.57, pred[48,512]{1,0:T(8,128)(4,1)S(1)} %get-tuple-element.39, bf16[512,576]{0,1:T(8,128)(2,1)} %get-tuple-element.68, ...), kind=kOutput, calls=%fused_computation.80 | convolution fusion | flops 1011744768 | bytes 8294448 | tf_op jit(solution)/shard_map/hic,hcv->ihv/dot_general | solution.py:121
  73.3 3.0 %fusion.2 = (f32[32,48]{1,0:T(8,128)S(1)}, f32[32,48,512]{2,1,0:T(8,128)S(1)}) fusion(pred[48,512]{1,0:T(8,128)(4,1)S(1)} %get-tuple-element.40, bf16[128,576]{0,1:T(8,128)(2,1)} %copy-done.14, bf16[128,576]{0,1:T(8,128)(2,1)S(1)} %get-tuple-element.36, bf16[128,576]{0,1:T(8,128)(2,1)S(1)} %get-tuple-element.34, ...), kind=kOutput, calls=%fused_computation.23 | convolution fusion | flops 914225664 | bytes 10844164 | tf_op jit(solution)/shard_map/hic,jc->hij/dot_general | solution.py:106
  76.3 1.7 copy-done.6
  79.0 5.4 %fusion.79 = bf16[32,48,128]{2,1,0:T(8,128)(2,1)S(1)} fusion(bf16[32,512,128]{2,1,0:T(8,128)(2,1)} %param.14, f32[32,48,512]{2,1,0:T(8,128)} %copy-done.6, f32[32,48]{1,0:T(8,128)S(1)} %fusion.11, f32[32,48]{1,0:T(8,128)S(1)} %get-tuple-element.53, pred[48,512]{1,0:T(8,128)(4,1)S(1)} %get-tuple-element.40, bf16[512,576]{0,1:T(8,128)(2,1)} %get-tuple-element.69, ...), kind=kOutput, calls=%fused_computation.81 | convolution fusion | flops 1011744768 | bytes 8294448 | tf_op jit(solution)/shard_map/hic,hcv->ihv/dot_general | solution.py:121
  85.1 3.0 %fusion = (f32[32,48]{1,0:T(8,128)S(1)}, f32[32,48,512]{2,1,0:T(8,128)S(1)}) fusion(pred[48,512]{1,0:T(8,128)(4,1)S(1)} %get-tuple-element.42, bf16[128,576]{0,1:T(8,128)(2,1)} %copy-done.16, bf16[128,576]{0,1:T(8,128)(2,1)S(1)} %copy-done.11, bf16[128,576]{0,1:T(8,128)(2,1)} %copy-done.12, bf16[128,576]{0,1:T(8,128)(2,1)S(1)} %get-tuple-element.21, ...), kind=kOutput, calls=%fused_computation.21 | convolution fusion | flops 914225664 | bytes 10844164 | tf_op jit(solution)/shard_map/hic,jc->hij/dot_general | solution.py:106
  88.1 1.6 copy-done.5
  90.7 4.9 %fusion.73 = bf16[32,48,128]{2,1,0:T(8,128)(2,1)S(1)} fusion(bf16[32,512,128]{2,1,0:T(8,128)(2,1)} %param.14, f32[32,48,512]{2,1,0:T(8,128)} %copy-done.5, f32[32,48]{1,0:T(8,128)S(1)} %fusion.7, f32[32,48]{1,0:T(8,128)S(1)} %get-tuple-element.51, pred[48,512]{1,0:T(8,128)(4,1)S(1)} %get-tuple-element.42, bf16[512,576]{0,1:T(8,128)(2,1)S(1)} %copy-done.17, ...), kind=kOutput, calls=%fused_computation.79 | convolution fusion | flops 1011744768 | bytes 8315392 | tf_op jit(solution)/shard_map/hic,hcv->ihv/dot_general | solution.py:121
  97.9 1.5 collective-permute-start.14
  100.9 8.4 %convolution_convert_fusion.1 = bf16[192,1792]{1,0:T(8,128)(2,1)S(1)} fusion(bf16[192,4096]{1,0:T(8,128)(2,1)S(1)} %bitcast.175, bf16[4096,1792]{1,0:T(8,128)(2,1)} %param.15), kind=kOutput, calls=%fused_computation.30 | convolution fusion | flops 2818916352 | bytes 16941056 | tf_op jit(solution)/shard_map/dot_general | solution.py:128
  111.2 4.3 %convolution_convert_fusion.2 = bf16[192,1792]{1,0:T(8,128)(2,1)} fusion(bf16[192,4096]{1,0:T(8,128)(2,1)S(1)} %bitcast.176, bf16[4096,1792]{1,0:T(8,128)(2,1)S(1)} %bitcast.190), kind=kOutput, calls=%fused_computation.31 | convolution fusion | flops 2818916352 | bytes 16941056 | tf_op jit(solution)/shard_map/dot_general | solution.py:128
  117.2 10.1 %collective-permute-done.4 = bf16[48,4096]{1,0:T(8,128)(2,1)S(1)} collective-permute-done((bf16[48,4096]{1,0:T(8,128)(2,1)}, bf16[48,4096]{1,0:T(8,128)(2,1)S(1)}, u32[]{:S(2)}, u32[]{:S(2)}) %collective-permute-start.4) | collective-permute-done | bytes 393248 | tf_op jit(solution)/shard_map/ppermute | solution.py:10
  127.8 4.0 %fusion.6 = bf16[192,1792]{1,0:T(8,128)(2,1)} fusion(bf16[192,4096]{1,0:T(8,128)(2,1)S(1)} %bitcast.173, bf16[4096,1792]{1,0:T(8,128)(2,1)S(1)} %bitcast.190, bf16[192,1792]{1,0:T(8,128)(2,1)S(1)} %collective-permute-done.19), kind=kOutput, calls=%fused_computation.29 | convolution fusion | flops 2819604480 | bytes 17629184 | tf_op jit(solution)/shard_map/dot_general | solution.py:128
  131.9 2.0 %collective-permute-start.9 = (bf16[192,1792]{1,0:T(8,128)(2,1)}, bf16[192,1792]{1,0:T(8,128)(2,1)S(1)}, u32[]{:S(2)}, u32[]{:S(2)}) collective-permute-start(bf16[192,1792]{1,0:T(8,128)(2,1)} %convolution_convert_fusion.2), channel_id=1, source_target_pairs={{0,4},{4,0},{8,12},{12,8},{1,5},{5,1},{9,13},{13,9},{2,6},{6,2},{1... | collective-permute-start | bytes 2064392 | tf_op jit(solution)/shard_map/ppermute | solution.py:10
  137.4 26.9 %collective-permute-done.9 = bf16[192,1792]{1,0:T(8,128)(2,1)S(1)} collective-permute-done((bf16[192,1792]{1,0:T(8,128)(2,1)}, bf16[192,1792]{1,0:T(8,128)(2,1)S(1)}, u32[]{:S(2)}, u32[]{:S(2)}) %collective-permute-start.9) | collective-permute-done | bytes 688160 | tf_op jit(solution)/shard_map/ppermute | solution.py:10
  164.3 2.6 %collective-permute-done.20 = bf16[192,1792]{1,0:T(8,128)(2,1)} collective-permute-done((bf16[192,1792]{1,0:T(8,128)(2,1)}, bf16[192,1792]{1,0:T(8,128)(2,1)}, u32[]{:S(2)}, u32[]{:S(2)}) %collective-permute-start.20) | collective-permute-done | bytes 688160 | tf_op jit(solution)/shard_map/ppermute | solution.py:10
  167.0 8.7 %fusion.5 = bf16[192,1792]{1,0:T(8,128)(2,1)S(1)} fusion(bf16[192,4096]{1,0:T(8,128)(2,1)S(1)} %bitcast.174, bf16[4096,1792]{1,0:T(8,128)(2,1)} %param.15, bf16[192,1792]{1,0:T(8,128)(2,1)} %collective-permute-done.20, bf16[192,1792]{1,0:T(8,128)(2,1)} %copy-done.22), kind=kOutput, calls=%fused_computation.28 | convolution fusion | flops 2820292608 | bytes 18317312 | tf_op jit(solution)/shard_map/dot_general | solution.py:128
  179.5 2.8 %collective-permute-done.21 = bf16[48,1792]{1,0:T(8,128)(2,1)S(1)} collective-permute-done((bf16[48,1792]{1,0:T(8,128)(2,1)S(1)}, bf16[48,1792]{1,0:T(8,128)(2,1)S(1)}, u32[]{:S(2)}, u32[]{:S(2)}) %collective-permute-start.21) | collective-permute-done | bytes 172064 | tf_op jit(solution)/shard_map/ppermute | solution.py:10
  182.3 2.8 %collective-permute-done.22 = bf16[48,1792]{1,0:T(8,128)(2,1)S(1)} collective-permute-done((bf16[48,1792]{1,0:T(8,128)(2,1)S(1)}, bf16[48,1792]{1,0:T(8,128)(2,1)S(1)}, u32[]{:S(2)}, u32[]{:S(2)}) %collective-permute-start.22) | collective-permute-done | bytes 172064 | tf_op jit(solution)/shard_map/ppermute | solution.py:10
  (151 shorter events, 46.5 us)
Async XLA Ops:
  0.6 17.3 %copy-start = (bf16[192,4096]{1,0:T(8,128)(2,1)S(1)}, bf16[192,4096]{1,0:T(8,128)(2,1)}, u32[]{:S(2)}) copy-start(bf16[192,4096]{1,0:T(8,128)(2,1)} %param.10) | copy-start | bytes 4718596
  0.7 13.6 %copy-start.20 = (s32[4]{0:T(128)S(1)}, s32[4]{0:T(128)}, u32[]{:S(2)}) copy-start(s32[4]{0:T(128)} %param.17) | copy-start | bytes 52
  2.7 33.9 %collective-permute-start = (bf16[2,128,576]{1,2,0:T(8,128)(2,1)}, bf16[2,128,576]{1,2,0:T(8,128)(2,1)}, u32[]{:S(2)}, u32[]{:S(2)}) collective-permute-start(bf16[2,128,576]{1,2,0:T(8,128)(2,1)} %get-tuple-element.23), channel_id=1, source_target_pairs={{0,4},{4,0},{8,12},{12,8},{1,5},{5,1},{9,13},{13,9},{2,6},{6,2},{1... | collective-permute-start | bytes 884744 | tf_op jit(solution)/shard_map/ppermute | solution.py:10
  5.7 24.8 %collective-permute-start.11 = (bf16[2,128,576]{1,2,0:T(8,128)(2,1)}, bf16[2,128,576]{1,2,0:T(8,128)(2,1)}, u32[]{:S(2)}, u32[]{:S(2)}) collective-permute-start(bf16[2,128,576]{1,2,0:T(8,128)(2,1)} %get-tuple-element.23), channel_id=1, source_target_pairs={{0,8},{4,12},{8,0},{12,4},{1,9},{5,13},{9,1},{13,5},{2,10},{6,14},... | collective-permute-start | bytes 884744 | tf_op jit(solution)/shard_map/ppermute | solution.py:10
  8.3 26.1 %collective-permute-start.1 = (bf16[2,128,576]{1,2,0:T(8,128)(2,1)}, bf16[2,128,576]{1,2,0:T(8,128)(2,1)}, u32[]{:S(2)}, u32[]{:S(2)}) collective-permute-start(bf16[2,128,576]{1,2,0:T(8,128)(2,1)} %get-tuple-element.24), channel_id=1, source_target_pairs={{0,8},{4,12},{8,0},{12,4},{1,9},{5,13},{9,1},{13,5},{2,10},{6,14},... | collective-permute-start | bytes 884744 | tf_op jit(solution)/shard_map/ppermute | solution.py:10
  8.7 31.1 %collective-permute-start.10 = (bf16[2,128,576]{1,2,0:T(8,128)(2,1)}, bf16[2,128,576]{1,2,0:T(8,128)(2,1)}, u32[]{:S(2)}, u32[]{:S(2)}) collective-permute-start(bf16[2,128,576]{1,2,0:T(8,128)(2,1)} %get-tuple-element.24), channel_id=1, source_target_pairs={{0,4},{4,0},{8,12},{12,8},{1,5},{5,1},{9,13},{13,9},{2,6},{6,2},{1... | collective-permute-start | bytes 884744 | tf_op jit(solution)/shard_map/ppermute | solution.py:10
  14.1 117.7 %collective-permute-start.24 = (bf16[128,576]{0,1:T(8,128)(2,1)}, bf16[128,576]{0,1:T(8,128)(2,1)}, u32[]{:S(2)}, u32[]{:S(2)}) collective-permute-start(bf16[128,576]{0,1:T(8,128)(2,1)} %bitcast.167), channel_id=1, source_target_pairs={{0,3},{1,2},{2,1},{3,0},{4,7},{5,6},{6,5},{7,4},{8,11},{9,10},{10,... | collective-permute-start | bytes 442376 | tf_op jit(solution)/shard_map/ppermute | solution.py:10
  30.5 103.4 %collective-permute-start.25 = (bf16[128,576]{0,1:T(8,128)(2,1)}, bf16[128,576]{0,1:T(8,128)(2,1)}, u32[]{:S(2)}, u32[]{:S(2)}) collective-permute-start(bf16[128,576]{0,1:T(8,128)(2,1)} %bitcast.188), channel_id=1, source_target_pairs={{0,2},{1,3},{2,0},{3,1},{4,6},{5,7},{6,4},{7,5},{8,10},{9,11},{10,... | collective-permute-start | bytes 442376 | tf_op jit(solution)/shard_map/ppermute | solution.py:10
  34.4 10.2 %collective-permute-start.12 = (bf16[2,128,576]{1,2,0:T(8,128)(2,1)}, bf16[2,128,576]{1,2,0:T(8,128)(2,1)S(1)}, u32[]{:S(2)}, u32[]{:S(2)}) collective-permute-start(bf16[2,128,576]{1,2,0:T(8,128)(2,1)} %collective-permute-done.11), channel_id=1, source_target_pairs={{0,4},{4,0},{8,12},{12,8},{1,5},{5,1},{9,13},{13,9},{2,6},{6,2},{1... | collective-permute-start | bytes 884744 | tf_op jit(solution)/shard_map/ppermute | solution.py:10
  36.6 29.1 %copy-start.10 = (bf16[128,576]{0,1:T(8,128)(2,1)}, bf16[128,576]{0,1:T(8,128)(2,1)S(1)}, u32[]{:S(2)}) copy-start(bf16[128,576]{0,1:T(8,128)(2,1)S(1)} %get-tuple-element.30) | copy-start | bytes 442372
  36.6 22.3 %collective-permute-start.2 = (bf16[2,128,576]{1,2,0:T(8,128)(2,1)}, bf16[2,128,576]{1,2,0:T(8,128)(2,1)}, u32[]{:S(2)}, u32[]{:S(2)}) collective-permute-start(bf16[2,128,576]{1,2,0:T(8,128)(2,1)} %collective-permute-done.1), channel_id=1, source_target_pairs={{0,4},{4,0},{8,12},{12,8},{1,5},{5,1},{9,13},{13,9},{2,6},{6,2},{1... | collective-permute-start | bytes 884744 | tf_op jit(solution)/shard_map/ppermute | solution.py:10
  39.8 25.9 %copy-start.12 = (bf16[128,576]{0,1:T(8,128)(2,1)}, bf16[128,576]{0,1:T(8,128)(2,1)S(1)}, u32[]{:S(2)}) copy-start(bf16[128,576]{0,1:T(8,128)(2,1)S(1)} %get-tuple-element.28) | copy-start | bytes 442372
  57.4 38.2 %collective-permute-start.17 = (bf16[48,4096]{1,0:T(8,128)(2,1)}, bf16[48,4096]{1,0:T(8,128)(2,1)}, u32[]{:S(2)}, u32[]{:S(2)}) collective-permute-start(bf16[48,4096]{1,0:T(8,128)(2,1)} %copy_bitcast_fusion), channel_id=1, source_target_pairs={{0,2},{1,3},{2,0},{3,1},{4,6},{5,7},{6,4},{7,5},{8,10},{9,11},{10,... | collective-permute-start | bytes 1179656 | tf_op jit(solution)/shard_map/ppermute | solution.py:10
  58.9 39.0 %collective-permute-start.16 = (bf16[48,4096]{1,0:T(8,128)(2,1)}, bf16[48,4096]{1,0:T(8,128)(2,1)}, u32[]{:S(2)}, u32[]{:S(2)}) collective-permute-start(bf16[48,4096]{1,0:T(8,128)(2,1)} %copy_bitcast_fusion), channel_id=1, source_target_pairs={{0,1},{1,0},{2,3},{3,2},{4,5},{5,4},{6,7},{7,6},{8,9},{9,8},{10,11... | collective-permute-start | bytes 1179656 | tf_op jit(solution)/shard_map/ppermute | solution.py:10
  72.8 24.8 %collective-permute-start.7 = (bf16[48,4096]{1,0:T(8,128)(2,1)}, bf16[48,4096]{1,0:T(8,128)(2,1)}, u32[]{:S(2)}, u32[]{:S(2)}) collective-permute-start(bf16[48,4096]{1,0:T(8,128)(2,1)} %copy_bitcast_fusion.2), channel_id=1, source_target_pairs={{0,2},{1,3},{2,0},{3,1},{4,6},{5,7},{6,4},{7,5},{8,10},{9,11},{10,... | collective-permute-start | bytes 1179656 | tf_op jit(solution)/shard_map/ppermute | solution.py:10
  95.6 3.8 %collective-permute-start.18 = (bf16[48,4096]{1,0:T(8,128)(2,1)}, bf16[48,4096]{1,0:T(8,128)(2,1)}, u32[]{:S(2)}, u32[]{:S(2)}) collective-permute-start(bf16[48,4096]{1,0:T(8,128)(2,1)} %collective-permute-done.17), channel_id=1, source_target_pairs={{0,1},{1,0},{2,3},{3,2},{4,5},{5,4},{6,7},{7,6},{8,9},{9,8},{10,11... | collective-permute-start | bytes 1179656 | tf_op jit(solution)/shard_map/ppermute | solution.py:10
  97.6 11.7 %collective-permute-start.6 = (bf16[48,4096]{1,0:T(8,128)(2,1)}, bf16[48,4096]{1,0:T(8,128)(2,1)S(1)}, u32[]{:S(2)}, u32[]{:S(2)}) collective-permute-start(bf16[48,4096]{1,0:T(8,128)(2,1)} %copy_bitcast_fusion.2), channel_id=1, source_target_pairs={{0,1},{1,0},{2,3},{3,2},{4,5},{5,4},{6,7},{7,6},{8,9},{9,8},{10,11... | collective-permute-start | bytes 1179656 | tf_op jit(solution)/shard_map/ppermute | solution.py:10
  97.9 12.0 %collective-permute-start.14 = (bf16[48,4096]{1,0:T(8,128)(2,1)}, bf16[48,4096]{1,0:T(8,128)(2,1)S(1)}, u32[]{:S(2)}, u32[]{:S(2)}) collective-permute-start(bf16[48,4096]{1,0:T(8,128)(2,1)} %copy_bitcast_fusion.1), channel_id=1, source_target_pairs={{0,2},{1,3},{2,0},{3,1},{4,6},{5,7},{6,4},{7,5},{8,10},{9,11},{10,... | collective-permute-start | bytes 1179656 | tf_op jit(solution)/shard_map/ppermute | solution.py:10
  99.4 10.5 %collective-permute-start.8 = (bf16[48,4096]{1,0:T(8,128)(2,1)}, bf16[48,4096]{1,0:T(8,128)(2,1)S(1)}, u32[]{:S(2)}, u32[]{:S(2)}) collective-permute-start(bf16[48,4096]{1,0:T(8,128)(2,1)} %collective-permute-done.7), channel_id=1, source_target_pairs={{0,1},{1,0},{2,3},{3,2},{4,5},{5,4},{6,7},{7,6},{8,9},{9,8},{10,11... | collective-permute-start | bytes 1179656 | tf_op jit(solution)/shard_map/ppermute | solution.py:10
  109.3 6.2 %collective-permute-start.13 = (bf16[48,4096]{1,0:T(8,128)(2,1)S(1)}, bf16[48,4096]{1,0:T(8,128)(2,1)S(1)}, u32[]{:S(2)}, u32[]{:S(2)}) collective-permute-start(bf16[48,4096]{1,0:T(8,128)(2,1)S(1)} %copy-done.18), channel_id=1, source_target_pairs={{0,1},{1,0},{2,3},{3,2},{4,5},{5,4},{6,7},{7,6},{8,9},{9,8},{10,11... | collective-permute-start | bytes 1179656 | tf_op jit(solution)/shard_map/ppermute | solution.py:10
  109.9 6.1 %collective-permute-start.15 = (bf16[48,4096]{1,0:T(8,128)(2,1)S(1)}, bf16[48,4096]{1,0:T(8,128)(2,1)S(1)}, u32[]{:S(2)}, u32[]{:S(2)}) collective-permute-start(bf16[48,4096]{1,0:T(8,128)(2,1)S(1)} %collective-permute-done.14), channel_id=1, source_target_pairs={{0,1},{1,0},{2,3},{3,2},{4,5},{5,4},{6,7},{7,6},{8,9},{9,8},{10,11... | collective-permute-start | bytes 1179656 | tf_op jit(solution)/shard_map/ppermute | solution.py:10
  110.0 17.8 %collective-permute-start.19 = (bf16[192,1792]{1,0:T(8,128)(2,1)S(1)}, bf16[192,1792]{1,0:T(8,128)(2,1)S(1)}, u32[]{:S(2)}, u32[]{:S(2)}) collective-permute-start(bf16[192,1792]{1,0:T(8,128)(2,1)S(1)} %convolution_convert_fusion.1), channel_id=1, source_target_pairs={{0,4},{4,0},{8,12},{12,8},{1,5},{5,1},{9,13},{13,9},{2,6},{6,2},{1... | collective-permute-start | bytes 2064392 | tf_op jit(solution)/shard_map/ppermute | solution.py:10
  115.6 19.2 %collective-permute-start.26 = (bf16[128,576]{0,1:T(8,128)(2,1)S(1)}, bf16[128,576]{0,1:T(8,128)(2,1)S(1)}, u32[]{:S(2)}, u32[]{:S(2)}) collective-permute-start(bf16[128,576]{0,1:T(8,128)(2,1)S(1)} %bitcast.187), channel_id=1, source_target_pairs={{0,1},{1,0},{2,3},{3,2},{4,5},{5,4},{6,7},{7,6},{8,9},{9,8},{10,11... | collective-permute-start | bytes 442376 | tf_op jit(solution)/shard_map/ppermute | solution.py:10
  116.0 11.3 %collective-permute-start.4 = (bf16[48,4096]{1,0:T(8,128)(2,1)}, bf16[48,4096]{1,0:T(8,128)(2,1)S(1)}, u32[]{:S(2)}, u32[]{:S(2)}) collective-permute-start(bf16[48,4096]{1,0:T(8,128)(2,1)} %copy_bitcast_fusion.3), channel_id=1, source_target_pairs={{0,2},{1,3},{2,0},{3,1},{4,6},{5,7},{6,4},{7,5},{8,10},{9,11},{10,... | collective-permute-start | bytes 1179656 | tf_op jit(solution)/shard_map/ppermute | solution.py:10
  127.3 8.8 %collective-permute-start.3 = (bf16[48,4096]{1,0:T(8,128)(2,1)}, bf16[48,4096]{1,0:T(8,128)(2,1)}, u32[]{:S(2)}, u32[]{:S(2)}) collective-permute-start(bf16[48,4096]{1,0:T(8,128)(2,1)} %copy_bitcast_fusion.3), channel_id=1, source_target_pairs={{0,1},{1,0},{2,3},{3,2},{4,5},{5,4},{6,7},{7,6},{8,9},{9,8},{10,11... | collective-permute-start | bytes 1179656 | tf_op jit(solution)/shard_map/ppermute | solution.py:10
  127.8 8.4 %collective-permute-start.5 = (bf16[48,4096]{1,0:T(8,128)(2,1)S(1)}, bf16[48,4096]{1,0:T(8,128)(2,1)}, u32[]{:S(2)}, u32[]{:S(2)}) collective-permute-start(bf16[48,4096]{1,0:T(8,128)(2,1)S(1)} %collective-permute-done.4), channel_id=1, source_target_pairs={{0,1},{1,0},{2,3},{3,2},{4,5},{5,4},{6,7},{7,6},{8,9},{9,8},{10,11... | collective-permute-start | bytes 1179656 | tf_op jit(solution)/shard_map/ppermute | solution.py:10
  131.9 32.5 %collective-permute-start.9 = (bf16[192,1792]{1,0:T(8,128)(2,1)}, bf16[192,1792]{1,0:T(8,128)(2,1)S(1)}, u32[]{:S(2)}, u32[]{:S(2)}) collective-permute-start(bf16[192,1792]{1,0:T(8,128)(2,1)} %convolution_convert_fusion.2), channel_id=1, source_target_pairs={{0,4},{4,0},{8,12},{12,8},{1,5},{5,1},{9,13},{13,9},{2,6},{6,2},{1... | collective-permute-start | bytes 2064392 | tf_op jit(solution)/shard_map/ppermute | solution.py:10
  133.9 33.1 %collective-permute-start.20 = (bf16[192,1792]{1,0:T(8,128)(2,1)}, bf16[192,1792]{1,0:T(8,128)(2,1)}, u32[]{:S(2)}, u32[]{:S(2)}) collective-permute-start(bf16[192,1792]{1,0:T(8,128)(2,1)} %fusion.6), channel_id=1, source_target_pairs={{0,8},{4,12},{8,0},{12,4},{1,9},{5,13},{9,1},{13,5},{2,10},{6,14},... | collective-permute-start | bytes 2064392 | tf_op jit(solution)/shard_map/ppermute | solution.py:10
  166.9 19.2 %copy-start.1 = (bf16[192,4096]{1,0:T(8,128)(2,1)S(1)}, bf16[192,4096]{1,0:T(8,128)(2,1)}, u32[]{:S(2)}) copy-start(bf16[192,4096]{1,0:T(8,128)(2,1)} %param.10) | copy-start | bytes 4718596
  175.7 6.7 %collective-permute-start.21 = (bf16[48,1792]{1,0:T(8,128)(2,1)S(1)}, bf16[48,1792]{1,0:T(8,128)(2,1)S(1)}, u32[]{:S(2)}, u32[]{:S(2)}) collective-permute-start(bf16[48,1792]{1,0:T(8,128)(2,1)S(1)} %get-tuple-element.14), channel_id=1, source_target_pairs={{0,3},{1,2},{2,1},{3,0},{4,7},{5,6},{6,5},{7,4},{8,11},{9,10},{10,... | collective-permute-start | bytes 516104 | tf_op jit(solution)/shard_map/ppermute | solution.py:10
  175.8 9.4 %collective-permute-start.22 = (bf16[48,1792]{1,0:T(8,128)(2,1)S(1)}, bf16[48,1792]{1,0:T(8,128)(2,1)S(1)}, u32[]{:S(2)}, u32[]{:S(2)}) collective-permute-start(bf16[48,1792]{1,0:T(8,128)(2,1)S(1)} %get-tuple-element.13), channel_id=1, source_target_pairs={{0,2},{1,3},{2,0},{3,1},{4,6},{5,7},{6,4},{7,5},{8,10},{9,11},{10,... | collective-permute-start | bytes 516104 | tf_op jit(solution)/shard_map/ppermute | solution.py:10
  176.8 8.4 %collective-permute-start.23 = (bf16[48,1792]{1,0:T(8,128)(2,1)S(1)}, bf16[48,1792]{1,0:T(8,128)(2,1)S(1)}, u32[]{:S(2)}, u32[]{:S(2)}) collective-permute-start(bf16[48,1792]{1,0:T(8,128)(2,1)S(1)} %get-tuple-element.12), channel_id=1, source_target_pairs={{0,1},{1,0},{2,3},{3,2},{4,5},{5,4},{6,7},{7,6},{8,9},{9,8},{10,11... | collective-permute-start | bytes 516104 | tf_op jit(solution)/shard_map/ppermute | solution.py:10
  (22 other events, 131.3 us)

commit v3 on v2

v3 whole, which is shorter than its diff:
```python
import functools
import math

import jax
import jax.numpy as jnp
from jax import lax
from jax.experimental import pallas as pl
from jax.experimental.pallas import tpu as pltpu
from jax.sharding import PartitionSpec as P

MIB = 1 << 20


def swap(value, axis, distance, inner=1):
    size = lax.axis_size(axis)
    pairs = [(i, ((i // inner) ^ distance) * inner + i % inner) for i in range(size)]
    return lax.ppermute(value, axis, pairs)


def by_rank(pieces, rank):
    distance = 1
    while distance < len(pieces):
        flip = (rank & distance) > 0
        pieces = [jnp.where(flip, pieces[k ^ distance], pieces[k]) for k in range(len(pieces))]
        distance *= 2
    return pieces


def gather_ranks(value, axis):
    size = lax.axis_size(axis)
    pieces = {0: value}
    distance = size // 2
    while distance:
        for k in list(pieces):
            pieces[k ^ distance] = swap(pieces[k], axis, distance)
        distance //= 2
    return [pieces[k] for k in range(size)]


def part_of(size, wanted, unit=1):
    return max(d for d in range(unit, max(wanted, unit) + 1, unit) if size % d == 0)


def absorb_kernel(nope_ref, rope_ref, key_ref, out_ref):
    heads, latent, nope = key_ref.shape
    rotary = out_ref.shape[2] - latent
    for h in range(heads):
        out_ref[h, :, :latent] = lax.dot_general(
            nope_ref[:, h * nope : (h + 1) * nope],
            key_ref[h],
            (((1,), (1,)), ((), ())),
            preferred_element_type=jnp.float32,
        ).astype(out_ref.dtype)
        out_ref[h, :, latent:] = rope_ref[:, h * rotary : (h + 1) * rotary]


def absorb(q_nope, q_rope, w_key):
    rows = q_nope.shape[0]
    heads, latent, nope = w_key.shape
    rotary = q_rope.shape[1] // heads
    step = part_of(heads, 4, 2)
    return pl.pallas_call(
        absorb_kernel,
        grid=(heads // step,),
        in_specs=[
            pl.BlockSpec((rows, step * nope), lambda h: (0, h)),
            pl.BlockSpec((rows, step * rotary), lambda h: (0, h)),
            pl.BlockSpec((step, latent, nope), lambda h: (h, 0, 0)),
        ],
        out_specs=pl.BlockSpec((step, rows, latent + rotary), lambda h: (h, 0, 0)),
        out_shape=jax.ShapeDtypeStruct((heads, rows, latent + rotary), q_nope.dtype),
        compiler_params=pltpu.CompilerParams(vmem_limit_bytes=24 * MIB),
        cost_estimate=pl.CostEstimate(
            flops=2 * rows * heads * latent * nope,
            bytes_accessed=2 * (q_nope.size + q_rope.size + w_key.size)
            + 2 * heads * rows * (latent + rotary),
            transcendentals=0,
        ),
        name="absorb",
    )(q_nope, q_rope, w_key)


def attend_kernel(
    distance, scale, place_ref, prefix_ref, stretch_ref, query_ref, *refs
):
    block_refs, (value_ref, out_ref, keys, hidden) = refs[:4], refs[4:]
    heads, stretch, width = query_ref.shape
    latent, value_width = value_ref.shape[1:]
    part = block_refs[0].shape[1]
    span = 4 * part
    place = place_ref[0]
    request = place ^ distance

    @pl.when(pl.program_id(0) == 0)
    def _():
        query_pos = prefix_ref[request] + lax.broadcasted_iota(jnp.int32, (stretch, part), 0)
        for k, ref in enumerate(block_refs):
            keys[k * part : (k + 1) * part] = ref[0]
            key_pos = (place ^ k) * part + lax.broadcasted_iota(jnp.int32, (stretch, part), 1)
            hidden[:, k * part : (k + 1) * part] = jnp.where(key_pos <= query_pos, 0.0, -1e30)

    query = query_ref[...].reshape(heads * stretch, width)
    scores = lax.dot_general(
        query, keys[...], (((1,), (1,)), ((), ())), preferred_element_type=jnp.float32
    )
    scores = scores.reshape(heads, stretch, span) + hidden[...][None]
    top = jnp.max(scores, axis=2, keepdims=True)
    weights = jnp.exp2((scores - top) * (scale / math.log(2.0)))
    denom = jnp.sum(weights, axis=2, keepdims=True).reshape(heads * stretch, 1)
    latent_out = jnp.dot(
        weights.astype(jnp.bfloat16).reshape(heads * stretch, span),
        keys[:, :latent],
        preferred_element_type=jnp.float32,
    )
    latent_out = (latent_out / denom).astype(jnp.bfloat16)
    live = lax.broadcasted_iota(jnp.int32, (stretch, value_width), 0) < stretch_ref[request]
    for h in range(heads):
        head_out = jnp.dot(
            latent_out[h * stretch : (h + 1) * stretch],
            value_ref[h],
            preferred_element_type=jnp.float32,
        )
        out_ref[:, h * value_width : (h + 1) * value_width] = jnp.where(
            live, head_out, 0.0
        ).astype(out_ref.dtype)


def attend(distance, place, prefix_len, stretch_len, full_query, blocks, w_value, scale):
    heads, rows, width = full_query.shape
    latent, value_width = w_value.shape[1:]
    stretch = rows // prefix_len.shape[0]
    part = blocks[0].shape[1]
    step = part_of(heads, 8)
    span = 4 * part
    return pl.pallas_call(
        functools.partial(attend_kernel, distance, scale),
        grid_spec=pltpu.PrefetchScalarGridSpec(
            num_scalar_prefetch=3,
            grid=(heads // step,),
            in_specs=[
                pl.BlockSpec((step, stretch, width), lambda h, p, *_: (h, p[0] ^ distance, 0))
            ]
            + [pl.BlockSpec((1, part, width), lambda h, p, *_: ((p[0] ^ distance) % 2, 0, 0))] * 4
            + [pl.BlockSpec((step, latent, value_width), lambda h, *_: (h, 0, 0))],
            out_specs=pl.BlockSpec((stretch, step * value_width), lambda h, *_: (0, h)),
            scratch_shapes=[
                pltpu.VMEM((span, width), jnp.bfloat16),
                pltpu.VMEM((stretch, span), jnp.float32),
            ],
        ),
        out_shape=jax.ShapeDtypeStruct((stretch, heads * value_width), jnp.bfloat16),
        compiler_params=pltpu.CompilerParams(vmem_limit_bytes=32 * MIB),
        cost_estimate=pl.CostEstimate(
            flops=2 * stretch * heads * (span * (width + latent) + latent * value_width),
            bytes_accessed=2 * (heads * stretch * (width + value_width) + span * width + w_value.size),
            transcendentals=stretch * heads * span,
        ),
        name=f"attend_{distance}",
    )(place, prefix_len, stretch_len, full_query, *blocks, w_value)


def project_kernel(rank_count, has_extra, *refs):
    row_refs, refs = refs[:rank_count], refs[rank_count:]
    weight_ref, refs = refs[0], refs[1:]
    extra_refs, (out_ref, rows) = refs[:-2], refs[-2:]
    stretch = row_refs[0].shape[0]

    @pl.when(pl.program_id(0) == 0)
    def _():
        for k, ref in enumerate(row_refs):
            rows[k * stretch : (k + 1) * stretch] = ref[...]

    total = jnp.dot(rows[...], weight_ref[...], preferred_element_type=jnp.float32)
    for ref in extra_refs:
        total += ref[...].astype(jnp.float32)
    out_ref[...] = total.astype(out_ref.dtype)


def project(pieces, w_out, extras, dtype, name):
    stretch, depth = pieces[0].shape
    columns = w_out.shape[1]
    rows = stretch * len(pieces)
    step = part_of(columns, 256, 128)
    return pl.pallas_call(
        functools.partial(project_kernel, len(pieces), len(extras)),
        grid=(columns // step,),
        in_specs=[pl.BlockSpec((stretch, depth), lambda n: (0, 0))] * len(pieces)
        + [pl.BlockSpec((depth, step), lambda n: (0, n))]
        + [pl.BlockSpec((rows, step), lambda n: (0, n))] * len(extras),
        out_specs=pl.BlockSpec((rows, step), lambda n: (0, n)),
        out_shape=jax.ShapeDtypeStruct((rows, columns), dtype),
        scratch_shapes=[pltpu.VMEM((rows, depth), jnp.bfloat16)],
        compiler_params=pltpu.CompilerParams(vmem_limit_bytes=32 * MIB),
        cost_estimate=pl.CostEstimate(
            flops=2 * rows * depth * columns,
            bytes_accessed=2 * (rows * depth + w_out.size + rows * columns * (1 + len(extras))),
            transcendentals=0,
        ),
        name=name,
    )(*pieces, w_out, *extras)


def local(
    q_nope, q_rope, latent_keys, w_key, w_value, w_out, prefix_len, stretch_len, finished, owners
):
    request_count = prefix_len.shape[0]
    row_count = q_nope.shape[0]
    head_count, latent_width, nope_width = w_key.shape
    rotary_width = q_rope.shape[1] // head_count
    block_size = latent_keys.shape[1]
    score_scale = (nope_width + rotary_width) ** (-0.5)
    rank_count = lax.axis_size("request")
    tensor_count = lax.axis_size("tensor")
    inner = tensor_count // request_count
    share_rows = row_count // tensor_count
    rank = lax.axis_index("request")
    place = lax.axis_index("tensor")
    outer_place = place // inner

    if inner > 1:
        groups = [[o * inner + i for i in range(inner)] for o in range(request_count)]
        own_keys = lax.all_gather(
            latent_keys, "tensor", axis=1, tiled=True, axis_index_groups=groups
        )
    else:
        own_keys = latent_keys
    near = (outer_place // 2) * 2
    near_keys = lax.dynamic_slice_in_dim(own_keys, near, 2, 0)
    far_keys = lax.dynamic_slice_in_dim(own_keys, near ^ 2, 2, 0)
    far_two = swap(near_keys, "tensor", 2, inner)
    far_one = swap(far_keys, "tensor", 1, inner)
    far_three = swap(far_two, "tensor", 1, inner)
    near_two = swap(far_keys, "tensor", 2, inner)
    near_one = swap(near_keys, "tensor", 1, inner)
    near_three = swap(near_two, "tensor", 1, inner)
    far_blocks = [far_keys, far_one, far_two, far_three]
    near_blocks = [near_keys, near_one, near_two, near_three]

    seq_ends = prefix_len + stretch_len
    positions = place * block_size + jnp.arange(block_size, dtype=jnp.int32)
    live_keys = (positions[None, :] < seq_ends[:, None]) & (finished[:, None] > 0)
    kept = jnp.where(live_keys[:, :, None], latent_keys, jnp.zeros_like(latent_keys))
    targets = rank ^ jnp.arange(rank_count, dtype=jnp.int32)
    routing = (owners[:, :1] == targets[None, :]).astype(jnp.bfloat16)
    outgoing = jnp.einsum("ko,kjc->ojc", routing, kept, preferred_element_type=jnp.float32).astype(
        jnp.bfloat16
    )
    arrived = [outgoing[0]] + [swap(outgoing[k], "request", k) for k in range(1, rank_count)]
    handed = jnp.stack(by_rank(arrived, rank))[None]

    full_query = absorb(q_nope, q_rope, w_key)
    place_here = outer_place.reshape(1)

    def rows_of(distance):
        blocks = far_blocks if distance >= 2 else near_blocks
        head_rows = attend(
            distance,
            place_here,
            prefix_len,
            stretch_len,
            full_query,
            blocks,
            w_value,
            score_scale,
        )
        return gather_ranks(head_rows, "request")

    sent = jnp.bfloat16
    opposite = swap(project(rows_of(3), w_out, [], sent, "project_3"), "tensor", 1, inner)
    across = swap(project(rows_of(2), w_out, [opposite], sent, "project_2"), "tensor", 2, inner)
    beside = swap(project(rows_of(1), w_out, [], sent, "project_1"), "tensor", 1, inner)
    kept_terms = project(rows_of(0), w_out, [], jnp.float32, "project_0")
    summed = (kept_terms + beside + across).astype(sent)
    if inner > 1:
        summed = summed.reshape(rank_count, inner, share_rows, summed.shape[1]).swapaxes(0, 1)
        summed = lax.psum_scatter(
            summed, "tensor", scatter_dimension=0, axis_index_groups=groups, tiled=True
        )
    summed = summed.reshape(rank_count, share_rows, w_out.shape[1])
    columns = [summed[0]] + [swap(summed[k], "request", k) for k in range(1, rank_count)]
    mixed = jnp.concatenate(by_rank(columns, rank), axis=1)[None]
    return (mixed, handed)


def solution(mesh):
    placed = (
        P(("groups", "request"), "tensor"),
        P(("groups", "request"), "tensor"),
        P(("groups", "request"), "tensor", None),
        P("tensor", None, None),
        P("tensor", None, None),
        P("tensor", "request"),
        P(("groups", "request")),
        P(("groups", "request")),
        P(("groups", "request")),
        P(("groups", "request"), "tensor"),
    )
    return jax.shard_map(
        local,
        mesh=mesh,
        in_specs=placed,
        out_specs=(
            P(("groups", "request"), "tensor", None),
            P(("groups", "request"), None, "tensor", None),
        ),
        check_vma=False,
    )
```

time: 187 us -> 154 us (0.82)
  matrix products: 66.1 us -> 1.42 us
  Pallas kernels: 0 us -> 50.2 us
  other arithmetic: 21.5 us -> 5.34 us
  local copies, waits for them, and re-layouts: 25.3 us -> 18.1 us
  waiting for transfers between devices: 50.7 us -> 54.3 us
  starting transfers between devices: 21.2 us -> 23.1 us
    dot_general x13 -> x0, matrix products: 64.8 us -> none  [the longest x4 25.4 us: stage(): jnp.dot(rows.reshape(rank_count * stretch_size, head_count * value_width)...]
    pallas_call x0 -> x9, Pallas kernels: none -> 50.2 us  [the longest x4 25 us: project(): pl.pallas_call(functools.partial(project_kernel, len(pieces), len(extras)...]
    squeeze x7 -> x0, local copies, waits for them, and re-layouts: 7.14 us -> none  [stage(): lax.dynamic_index_in_dim(b, request % 2, 0, False)]
    unnamed x58 -> x49, local copies, waits for them, and re-layouts: 9.34 us -> 15.3 us
    reshape x5 -> x0, local copies, waits for them, and re-layouts: 4.16 us -> none  [the longest x4 3.11 us: stage(): head_rows = head_out.reshape(stretch_size, head_count * value_width)]
    another operation x4 -> x0, other arithmetic: 4.13 us -> none  [stage(): rows = jnp.stack(gather_ranks(head_rows, 'request'))]
    reduce_sum x4 -> x0, other arithmetic: 3.76 us -> none  [stage(): denom = jnp.sum(weights, axis=2, keepdims=True)]
    ppermute x27, waiting for transfers between devices: 50.7 us -> 54.3 us  [swap(): return lax.ppermute(value, axis, pairs)]
  transfers between devices with their start and end apart: 27 -> 27, of which waited for: 8 -> 9; matrix products, arithmetic and copies ran while one was open for 51% -> 5% of each run, Pallas kernels for 0% -> 33%
where the time goes in v3:
time: 154 us
  waiting for transfers between devices  54.3 us (35%)
  Pallas kernels  50.2 us (33%)
  starting transfers between devices  23.1 us (15%)
  local copies, waits for them, and re-layouts  18.1 us (12%)
  other arithmetic  5.34 us (3%)
    ppermute x27, waiting for transfers between devices, swap(): return lax.ppermute(value, axis, pairs)  54.3 us
    pallas_call x4, Pallas kernels, project(): pl.pallas_call(functools.partial(project_kernel, len(pieces), len(extras)...  25 us
    ppermute x27, starting transfers between devices, swap(): return lax.ppermute(value, axis, pairs)  23.1 us
    pallas_call x4, Pallas kernels, attend(): pl.pallas_call(functools.partial(attend_kernel, distance, scale), grid_sp...  21.9 us
    unnamed x49, local copies, waits for them, and re-layouts  15.3 us
    pallas_call x1, Pallas kernels, absorb(): pl.pallas_call(absorb_kernel, grid=(heads // step,), in_specs=[pl.BlockSp...  3.29 us
  transfers between devices with their start and end apart: 27, of which 9 were waited for; matrix products, arithmetic and copies ran while one was open for 5% of the time, Pallas kernels for 33%

profile of v3, /device:TPU:0, one launch (start us, length us, event | category | flops | bytes accessed | tf_op | source)
XLA Modules:
  0.0 153.5 jit_solution(14005487467560024217)
XLA Ops:
  0.7 1.2 constant_dynamic-slice_fusion.1
  2.1 3.1 %collective-permute-start.10 = (bf16[2,128,576]{2,1,0:T(8,128)(2,1)S(1)}, bf16[2,128,576]{2,1,0:T(8,128)(2,1)}, u32[]{:S(2)}, u32[]{:S(2)}) collective-permute-start(bf16[2,128,576]{2,1,0:T(8,128)(2,1)S(1)} %copy.38.refs_0_), channel_id=1, source_target_pairs={{0,4},{4,0},{8,12},{12,8},{1,5},{5,1},{9,13},{13,9},{2,6},{6,2},{1... | collective-permute-start | bytes 884744 | tf_op jit(solution)/shard_map/ppermute | solution.py:17
  5.2 2.6 %collective-permute-start.1 = (bf16[2,128,576]{2,1,0:T(8,128)(2,1)S(1)}, bf16[2,128,576]{2,1,0:T(8,128)(2,1)S(1)}, u32[]{:S(2)}, u32[]{:S(2)}) collective-permute-start(bf16[2,128,576]{2,1,0:T(8,128)(2,1)S(1)} %copy.38.refs_0_), channel_id=1, source_target_pairs={{0,8},{4,12},{8,0},{12,4},{1,9},{5,13},{9,1},{13,5},{2,10},{6,14},... | collective-permute-start | bytes 884744 | tf_op jit(solution)/shard_map/ppermute | solution.py:17
  8.7 27.8 %collective-permute-done.11.refs_2_ = bf16[2,128,576]{2,1,0:T(8,128)(2,1)} collective-permute-done((bf16[2,128,576]{2,1,0:T(8,128)(2,1)S(1)}, bf16[2,128,576]{2,1,0:T(8,128)(2,1)}, u32[]{:S(2)}, u32[]{:S(2)}) %collective-permute-start.11) | collective-permute-done | bytes 294944 | tf_op jit(solution)/shard_map/ppermute | solution.py:17
  36.5 2.2 %copy-done.6 = bf16[32,512,128]{2,1,0:T(8,128)(2,1)S(1)} copy-done((bf16[32,512,128]{2,1,0:T(8,128)(2,1)S(1)}, bf16[32,512,128]{2,1,0:T(8,128)(2,1)}, u32[]{:S(2)}) %copy-start.6) | copy-done | bytes 4194328
  38.7 1.1 copy-done.10
  39.8 3.3 %absorb.1.query_ref = bf16[32,192,576]{2,1,0:T(8,128)(2,1)S(1)} custom-call(bf16[192,4096]{1,0:T(8,128)(2,1)S(1)} %copy-done.7, bf16[192,2048]{1,0:T(8,128)(2,1)S(1)} %copy-done.10, bf16[32,512,128]{2,1,0:T(8,128)(2,1)S(1)} %copy-done.6), custom_call_target="tpu_custom_call" | custom-call | flops 805306368 | bytes 13631488 | tf_op jit(solution)/shard_map/absorb/pallas_call | solution.py:62
  43.2 2.0 %collective-permute-start.2 = (bf16[2,128,576]{2,1,0:T(8,128)(2,1)S(1)}, bf16[2,128,576]{2,1,0:T(8,128)(2,1)S(1)}, u32[]{:S(2)}, u32[]{:S(2)}) collective-permute-start(bf16[2,128,576]{2,1,0:T(8,128)(2,1)S(1)} %collective-permute-done.1.refs_2_), channel_id=1, source_target_pairs={{0,4},{4,0},{8,12},{12,8},{1,5},{5,1},{9,13},{13,9},{2,6},{6,2},{1... | collective-permute-start | bytes 884744 | tf_op jit(solution)/shard_map/ppermute | solution.py:17
  45.4 6.0 %attend_3.1.refs_0_ = bf16[48,4096]{1,0:T(8,128)(2,1)S(1)} custom-call(s32[1]{0:T(128)} %bitcast.place_ref, s32[4]{0:T(128)S(1)} %copy-done.11, s32[4]{0:T(128)S(1)} %copy-done.12, bf16[32,192,576]{2,1,0:T(8,128)(2,1)S(1)} %absorb.1.query_ref, bf16[2,128,576]{2,1,0:T(8,128)(2,1)S(1)} %copy.38.refs_0_, bf16[2,128,576]{2,1,0:T(8,128)(2,1)} %collective-permute-done.10.refs_1_, ...), custom_call_target="tpu_custom_call" | custom-call | flops 1912602624 | bytes 6946816 | tf_op jit(solution)/shard_map/attend_3/pallas_call | solution.py:135
  51.4 1.6 %collective-permute-start.17 = (bf16[48,4096]{1,0:T(8,128)(2,1)S(1)}, bf16[48,4096]{1,0:T(8,128)(2,1)S(1)}, u32[]{:S(2)}, u32[]{:S(2)}) collective-permute-start(bf16[48,4096]{1,0:T(8,128)(2,1)S(1)} %attend_3.1.refs_0_), channel_id=1, source_target_pairs={{0,2},{1,3},{2,0},{3,1},{4,6},{5,7},{6,4},{7,5},{8,10},{9,11},{10,... | collective-permute-start | bytes 1179656 | tf_op jit(solution)/shard_map/ppermute | solution.py:17
  53.2 5.0 %attend_1.1.refs_0_ = bf16[48,4096]{1,0:T(8,128)(2,1)S(1)} custom-call(s32[1]{0:T(128)} %bitcast.place_ref, s32[4]{0:T(128)S(1)} %copy-done.11, s32[4]{0:T(128)S(1)} %copy-done.12, bf16[32,192,576]{2,1,0:T(8,128)(2,1)S(1)} %absorb.1.query_ref, bf16[2,128,576]{2,1,0:T(8,128)(2,1)S(1)} %copy.37.refs_0_, bf16[2,128,576]{2,1,0:T(8,128)(2,1)S(1)} %collective-permute-done.refs_1_, ...), custom_call_target="tpu_custom_call" | custom-call | flops 1912602624 | bytes 6946816 | tf_op jit(solution)/shard_map/attend_1/pallas_call | solution.py:135
  58.7 2.1 %collective-permute-done.17.refs_2_ = bf16[48,4096]{1,0:T(8,128)(2,1)S(1)} collective-permute-done((bf16[48,4096]{1,0:T(8,128)(2,1)S(1)}, bf16[48,4096]{1,0:T(8,128)(2,1)S(1)}, u32[]{:S(2)}, u32[]{:S(2)}) %collective-permute-start.17) | collective-permute-done | bytes 393248 | tf_op jit(solution)/shard_map/ppermute | solution.py:17
  60.9 1.4 convolution_convert_fusion
  62.8 2.3 %copy-done.4 = bf16[32,512,128]{2,1,0:T(8,128)(2,1)S(1)} copy-done((bf16[32,512,128]{2,1,0:T(8,128)(2,1)S(1)}, bf16[32,512,128]{2,1,0:T(8,128)(2,1)}, u32[]{:S(2)}) %copy-start.4) | copy-done | bytes 4194328
  65.2 6.0 %attend_2.1.refs_0_ = bf16[48,4096]{1,0:T(8,128)(2,1)S(1)} custom-call(s32[1]{0:T(128)} %bitcast.place_ref, s32[4]{0:T(128)S(1)} %copy-done.11, s32[4]{0:T(128)S(1)} %copy-done.12, bf16[32,192,576]{2,1,0:T(8,128)(2,1)S(1)} %absorb.1.query_ref, bf16[2,128,576]{2,1,0:T(8,128)(2,1)S(1)} %copy.38.refs_0_, bf16[2,128,576]{2,1,0:T(8,128)(2,1)} %collective-permute-done.10.refs_1_, ...), custom_call_target="tpu_custom_call" | custom-call | flops 1912602624 | bytes 6946816 | tf_op jit(solution)/shard_map/attend_2/pallas_call | solution.py:135
  71.2 2.0 %collective-permute-start.14 = (bf16[48,4096]{1,0:T(8,128)(2,1)S(1)}, bf16[48,4096]{1,0:T(8,128)(2,1)S(1)}, u32[]{:S(2)}, u32[]{:S(2)}) collective-permute-start(bf16[48,4096]{1,0:T(8,128)(2,1)S(1)} %attend_2.1.refs_0_), channel_id=1, source_target_pairs={{0,2},{1,3},{2,0},{3,1},{4,6},{5,7},{6,4},{7,5},{8,10},{9,11},{10,... | collective-permute-start | bytes 1179656 | tf_op jit(solution)/shard_map/ppermute | solution.py:17
  73.3 6.5 %project_3.1 = bf16[192,1792]{1,0:T(8,128)(2,1)S(1)} custom-call(bf16[48,4096]{1,0:T(8,128)(2,1)S(1)} %attend_3.1.refs_0_, bf16[48,4096]{1,0:T(8,128)(2,1)} %collective-permute-done.16.refs_1_, bf16[48,4096]{1,0:T(8,128)(2,1)S(1)} %collective-permute-done.17.refs_2_, bf16[48,4096]{1,0:T(8,128)(2,1)} %collective-permute-done.18.refs_3_, ...), custom_call_target="tpu_custom_call" | custom-call | flops 2818572288 | bytes 16941056 | tf_op jit(solution)/shard_map/project_3/pallas_call | solution.py:184
  80.2 1.5 %fusion.6 = (bf16[1,128,576]{1,0,2:T(2,128)(2,1)}, bf16[1,128,576]{1,0,2:T(2,128)(2,1)S(1)}, bf16[1,128,576]{1,0,2:T(2,128)(2,1)S(1)}, bf16[1,128,576]{1,0,2:T(2,128)(2,1)S(1)}) fusion(bf16[4,128,576]{1,0,2:T(4,128)(2,1)S(1)} %copy-done.14), kind=kLoop, calls=%fused_computation.36 | loop fusion | bytes 1179648 | tf_op jit(solution)/shard_map/slice | solution.py:248
  83.0 3.2 %copy-done.2 = bf16[32,192,576]{2,1,0:T(8,128)(2,1)S(1)} copy-done((bf16[32,192,576]{2,1,0:T(8,128)(2,1)S(1)}, bf16[32,192,576]{2,1,0:T(8,128)(2,1)}, u32[]{:S(2)}) %copy-start.2) | copy-done | bytes 7077912
  86.2 5.0 %attend_0.1.refs_0_ = bf16[48,4096]{1,0:T(8,128)(2,1)S(1)} custom-call(s32[1]{0:T(128)} %bitcast.place_ref, s32[4]{0:T(128)S(1)} %copy-done.11, s32[4]{0:T(128)S(1)} %copy-done.12, bf16[32,192,576]{2,1,0:T(8,128)(2,1)S(1)} %copy-done.2, bf16[2,128,576]{2,1,0:T(8,128)(2,1)S(1)} %copy.37.refs_0_, bf16[2,128,576]{2,1,0:T(8,128)(2,1)S(1)} %copy-done.9, ...), custom_call_target="tpu_custom_call" | custom-call | flops 1912602624 | bytes 6946816 | tf_op jit(solution)/shard_map/attend_0/pallas_call | solution.py:135
  91.2 1.5 collective-permute-start.24
  93.1 5.9 %project_1.1 = bf16[192,1792]{1,0:T(8,128)(2,1)} custom-call(bf16[48,4096]{1,0:T(8,128)(2,1)S(1)} %attend_1.1.refs_0_, bf16[48,4096]{1,0:T(8,128)(2,1)S(1)} %collective-permute-done.6.refs_1_, bf16[48,4096]{1,0:T(8,128)(2,1)S(1)} %collective-permute-done.7.refs_2_, bf16[48,4096]{1,0:T(8,128)(2,1)S(1)} %collective-permute-done.8.refs_3_, ...), custom_call_target="tpu_custom_call" | custom-call | flops 2818572288 | bytes 16941056 | tf_op jit(solution)/shard_map/project_1/pallas_call | solution.py:184
  99.0 1.6 %collective-permute-start.25 = (bf16[128,576]{0,1:T(8,128)(2,1)S(1)}, bf16[128,576]{0,1:T(8,128)(2,1)}, u32[]{:S(2)}, u32[]{:S(2)}) collective-permute-start(bf16[128,576]{0,1:T(8,128)(2,1)S(1)} %bitcast.33), channel_id=1, source_target_pairs={{0,2},{1,3},{2,0},{3,1},{4,6},{5,7},{6,4},{7,5},{8,10},{9,11},{10,... | collective-permute-start | bytes 442376 | tf_op jit(solution)/shard_map/ppermute | solution.py:17
  101.0 7.4 %project_2.1 = bf16[192,1792]{1,0:T(8,128)(2,1)} custom-call(bf16[48,4096]{1,0:T(8,128)(2,1)S(1)} %attend_2.1.refs_0_, bf16[48,4096]{1,0:T(8,128)(2,1)S(1)} %collective-permute-done.13.refs_1_, bf16[48,4096]{1,0:T(8,128)(2,1)S(1)} %collective-permute-done.14.refs_2_, bf16[48,4096]{1,0:T(8,128)(2,1)} %collective-permute-done.15.refs_3_, ...), custom_call_target="tpu_custom_call" | custom-call | flops 2818572288 | bytes 17629184 | tf_op jit(solution)/shard_map/project_2/pallas_call | solution.py:184
  108.4 2.6 %collective-permute-start.20 = (bf16[192,1792]{1,0:T(8,128)(2,1)}, bf16[192,1792]{1,0:T(8,128)(2,1)S(1)}, u32[]{:S(2)}, u32[]{:S(2)}) collective-permute-start(bf16[192,1792]{1,0:T(8,128)(2,1)} %project_2.1), channel_id=1, source_target_pairs={{0,8},{4,12},{8,0},{12,4},{1,9},{5,13},{9,1},{13,5},{2,10},{6,14},... | collective-permute-start | bytes 2064392 | tf_op jit(solution)/shard_map/ppermute | solution.py:17
  113.6 5.2 %copy-done = bf16[4096,1792]{1,0:T(8,128)(2,1)S(1)} copy-done((bf16[4096,1792]{1,0:T(8,128)(2,1)S(1)}, bf16[4096,1792]{1,0:T(8,128)(2,1)}, u32[]{:S(2)}) %copy-start) | copy-done | bytes 14680088
  118.7 5.3 %project_0.1 = f32[192,1792]{1,0:T(8,128)S(1)} custom-call(bf16[48,4096]{1,0:T(8,128)(2,1)S(1)} %attend_0.1.refs_0_, bf16[48,4096]{1,0:T(8,128)(2,1)S(1)} %collective-permute-done.3.refs_1_, bf16[48,4096]{1,0:T(8,128)(2,1)S(1)} %collective-permute-done.4.refs_2_, bf16[48,4096]{1,0:T(8,128)(2,1)S(1)} %collective-permute-done.5.refs_3_, ...), custom_call_target="tpu_custom_call" | custom-call | flops 2818572288 | bytes 16941056 | tf_op jit(solution)/shard_map/project_0/pallas_call | solution.py:184
  124.8 16.3 %collective-permute-done.20 = bf16[192,1792]{1,0:T(8,128)(2,1)S(1)} collective-permute-done((bf16[192,1792]{1,0:T(8,128)(2,1)}, bf16[192,1792]{1,0:T(8,128)(2,1)S(1)}, u32[]{:S(2)}, u32[]{:S(2)}) %collective-permute-start.20) | collective-permute-done | bytes 688160 | tf_op jit(solution)/shard_map/ppermute | solution.py:17
  141.1 1.3 add_convert_fusion
  142.5 1.7 %collective-permute-start.22 = (bf16[48,1792]{1,0:T(8,128)(2,1)S(1)}, bf16[48,1792]{1,0:T(8,128)(2,1)S(1)}, u32[]{:S(2)}, u32[]{:S(2)}) collective-permute-start(bf16[48,1792]{1,0:T(8,128)(2,1)S(1)} %get-tuple-element.13), channel_id=1, source_target_pairs={{0,2},{1,3},{2,0},{3,1},{4,6},{5,7},{6,4},{7,5},{8,10},{9,11},{10,... | collective-permute-start | bytes 516104 | tf_op jit(solution)/shard_map/ppermute | solution.py:17
  146.3 3.5 %collective-permute-done.22 = bf16[48,1792]{1,0:T(8,128)(2,1)S(1)} collective-permute-done((bf16[48,1792]{1,0:T(8,128)(2,1)S(1)}, bf16[48,1792]{1,0:T(8,128)(2,1)S(1)}, u32[]{:S(2)}, u32[]{:S(2)}) %collective-permute-start.22) | collective-permute-done | bytes 172064 | tf_op jit(solution)/shard_map/ppermute | solution.py:17
  149.8 2.8 %collective-permute-done.21 = bf16[48,1792]{1,0:T(8,128)(2,1)S(1)} collective-permute-done((bf16[48,1792]{1,0:T(8,128)(2,1)S(1)}, bf16[48,1792]{1,0:T(8,128)(2,1)S(1)}, u32[]{:S(2)}, u32[]{:S(2)}) %collective-permute-start.21) | collective-permute-done | bytes 172064 | tf_op jit(solution)/shard_map/ppermute | solution.py:17
  (97 shorter events, 11.6 us)
Async XLA Ops:
  0.7 35.8 %copy-start.7 = (bf16[192,4096]{1,0:T(8,128)(2,1)S(1)}, bf16[192,4096]{1,0:T(8,128)(2,1)}, u32[]{:S(2)}) copy-start(bf16[192,4096]{1,0:T(8,128)(2,1)} %nope_ref.1) | copy-start | bytes 4718596
  2.1 43.1 %collective-permute-start.10 = (bf16[2,128,576]{2,1,0:T(8,128)(2,1)S(1)}, bf16[2,128,576]{2,1,0:T(8,128)(2,1)}, u32[]{:S(2)}, u32[]{:S(2)}) collective-permute-start(bf16[2,128,576]{2,1,0:T(8,128)(2,1)S(1)} %copy.38.refs_0_), channel_id=1, source_target_pairs={{0,4},{4,0},{8,12},{12,8},{1,5},{5,1},{9,13},{13,9},{2,6},{6,2},{1... | collective-permute-start | bytes 884744 | tf_op jit(solution)/shard_map/ppermute | solution.py:17
  5.2 38.0 %collective-permute-start.1 = (bf16[2,128,576]{2,1,0:T(8,128)(2,1)S(1)}, bf16[2,128,576]{2,1,0:T(8,128)(2,1)S(1)}, u32[]{:S(2)}, u32[]{:S(2)}) collective-permute-start(bf16[2,128,576]{2,1,0:T(8,128)(2,1)S(1)} %copy.38.refs_0_), channel_id=1, source_target_pairs={{0,8},{4,12},{8,0},{12,4},{1,9},{5,13},{9,1},{13,5},{2,10},{6,14},... | collective-permute-start | bytes 884744 | tf_op jit(solution)/shard_map/ppermute | solution.py:17
  8.0 28.5 %collective-permute-start.11 = (bf16[2,128,576]{2,1,0:T(8,128)(2,1)S(1)}, bf16[2,128,576]{2,1,0:T(8,128)(2,1)}, u32[]{:S(2)}, u32[]{:S(2)}) collective-permute-start(bf16[2,128,576]{2,1,0:T(8,128)(2,1)S(1)} %copy.37.refs_0_), channel_id=1, source_target_pairs={{0,8},{4,12},{8,0},{12,4},{1,9},{5,13},{9,1},{13,5},{2,10},{6,14},... | collective-permute-start | bytes 884744 | tf_op jit(solution)/shard_map/ppermute | solution.py:17
  8.4 44.7 %collective-permute-start = (bf16[2,128,576]{2,1,0:T(8,128)(2,1)S(1)}, bf16[2,128,576]{2,1,0:T(8,128)(2,1)S(1)}, u32[]{:S(2)}, u32[]{:S(2)}) collective-permute-start(bf16[2,128,576]{2,1,0:T(8,128)(2,1)S(1)} %copy.37.refs_0_), channel_id=1, source_target_pairs={{0,4},{4,0},{8,12},{12,8},{1,5},{5,1},{9,13},{13,9},{2,6},{6,2},{1... | collective-permute-start | bytes 884744 | tf_op jit(solution)/shard_map/ppermute | solution.py:17
  36.5 8.9 %collective-permute-start.12 = (bf16[2,128,576]{2,1,0:T(8,128)(2,1)}, bf16[2,128,576]{2,1,0:T(8,128)(2,1)S(1)}, u32[]{:S(2)}, u32[]{:S(2)}) collective-permute-start(bf16[2,128,576]{2,1,0:T(8,128)(2,1)} %collective-permute-done.11.refs_2_), channel_id=1, source_target_pairs={{0,4},{4,0},{8,12},{12,8},{1,5},{5,1},{9,13},{13,9},{2,6},{6,2},{1... | collective-permute-start | bytes 884744 | tf_op jit(solution)/shard_map/ppermute | solution.py:17
  43.1 19.7 %copy-start.1 = (bf16[32,192,576]{2,1,0:T(8,128)(2,1)}, bf16[32,192,576]{2,1,0:T(8,128)(2,1)S(1)}, u32[]{:S(2)}) copy-start(bf16[32,192,576]{2,1,0:T(8,128)(2,1)S(1)} %absorb.1.query_ref) | copy-start | bytes 21233668
  43.2 9.9 %collective-permute-start.2 = (bf16[2,128,576]{2,1,0:T(8,128)(2,1)S(1)}, bf16[2,128,576]{2,1,0:T(8,128)(2,1)S(1)}, u32[]{:S(2)}, u32[]{:S(2)}) collective-permute-start(bf16[2,128,576]{2,1,0:T(8,128)(2,1)S(1)} %collective-permute-done.1.refs_2_), channel_id=1, source_target_pairs={{0,4},{4,0},{8,12},{12,8},{1,5},{5,1},{9,13},{13,9},{2,6},{6,2},{1... | collective-permute-start | bytes 884744 | tf_op jit(solution)/shard_map/ppermute | solution.py:17
  51.4 9.5 %collective-permute-start.17 = (bf16[48,4096]{1,0:T(8,128)(2,1)S(1)}, bf16[48,4096]{1,0:T(8,128)(2,1)S(1)}, u32[]{:S(2)}, u32[]{:S(2)}) collective-permute-start(bf16[48,4096]{1,0:T(8,128)(2,1)S(1)} %attend_3.1.refs_0_), channel_id=1, source_target_pairs={{0,2},{1,3},{2,0},{3,1},{4,6},{5,7},{6,4},{7,5},{8,10},{9,11},{10,... | collective-permute-start | bytes 1179656 | tf_op jit(solution)/shard_map/ppermute | solution.py:17
  53.1 20.1 %collective-permute-start.16 = (bf16[48,4096]{1,0:T(8,128)(2,1)S(1)}, bf16[48,4096]{1,0:T(8,128)(2,1)}, u32[]{:S(2)}, u32[]{:S(2)}) collective-permute-start(bf16[48,4096]{1,0:T(8,128)(2,1)S(1)} %attend_3.1.refs_0_), channel_id=1, source_target_pairs={{0,1},{1,0},{2,3},{3,2},{4,5},{5,4},{6,7},{7,6},{8,9},{9,8},{10,11... | collective-permute-start | bytes 1179656 | tf_op jit(solution)/shard_map/ppermute | solution.py:17
  53.2 20.0 %slice-start = ((s8[14680064]{0:T(1024)(128)(4,1)}), s8[4194304]{0:T(1024)(128)(4,1)S(1)}, s32[]{:S(2)}) async-start(s8[14680064]{0:T(1024)(128)(4,1)} %bitcast.31), calls=%async_computation | async-start | bytes 8388608
  53.2 20.0 %slice-start.1 = ((s8[14680064]{0:T(1024)(128)(4,1)}), s8[4194304]{0:T(1024)(128)(4,1)S(1)}, s32[]{:S(2)}) async-start(s8[14680064]{0:T(1024)(128)(4,1)} %bitcast.31), calls=%async_computation.1 | async-start | bytes 8388608
  58.2 15.0 %collective-permute-start.7 = (bf16[48,4096]{1,0:T(8,128)(2,1)S(1)}, bf16[48,4096]{1,0:T(8,128)(2,1)S(1)}, u32[]{:S(2)}, u32[]{:S(2)}) collective-permute-start(bf16[48,4096]{1,0:T(8,128)(2,1)S(1)} %attend_1.1.refs_0_), channel_id=1, source_target_pairs={{0,2},{1,3},{2,0},{3,1},{4,6},{5,7},{6,4},{7,5},{8,10},{9,11},{10,... | collective-permute-start | bytes 1179656 | tf_op jit(solution)/shard_map/ppermute | solution.py:17
  60.9 12.3 %collective-permute-start.18 = (bf16[48,4096]{1,0:T(8,128)(2,1)S(1)}, bf16[48,4096]{1,0:T(8,128)(2,1)}, u32[]{:S(2)}, u32[]{:S(2)}) collective-permute-start(bf16[48,4096]{1,0:T(8,128)(2,1)S(1)} %collective-permute-done.17.refs_2_), channel_id=1, source_target_pairs={{0,1},{1,0},{2,3},{3,2},{4,5},{5,4},{6,7},{7,6},{8,9},{9,8},{10,11... | collective-permute-start | bytes 1179656 | tf_op jit(solution)/shard_map/ppermute | solution.py:17
  62.3 28.8 %collective-permute-start.6 = (bf16[48,4096]{1,0:T(8,128)(2,1)S(1)}, bf16[48,4096]{1,0:T(8,128)(2,1)S(1)}, u32[]{:S(2)}, u32[]{:S(2)}) collective-permute-start(bf16[48,4096]{1,0:T(8,128)(2,1)S(1)} %attend_1.1.refs_0_), channel_id=1, source_target_pairs={{0,1},{1,0},{2,3},{3,2},{4,5},{5,4},{6,7},{7,6},{8,9},{9,8},{10,11... | collective-permute-start | bytes 1179656 | tf_op jit(solution)/shard_map/ppermute | solution.py:17
  71.2 11.5 %collective-permute-start.14 = (bf16[48,4096]{1,0:T(8,128)(2,1)S(1)}, bf16[48,4096]{1,0:T(8,128)(2,1)S(1)}, u32[]{:S(2)}, u32[]{:S(2)}) collective-permute-start(bf16[48,4096]{1,0:T(8,128)(2,1)S(1)} %attend_2.1.refs_0_), channel_id=1, source_target_pairs={{0,2},{1,3},{2,0},{3,1},{4,6},{5,7},{6,4},{7,5},{8,10},{9,11},{10,... | collective-permute-start | bytes 1179656 | tf_op jit(solution)/shard_map/ppermute | solution.py:17
  73.2 19.4 %collective-permute-start.8 = (bf16[48,4096]{1,0:T(8,128)(2,1)S(1)}, bf16[48,4096]{1,0:T(8,128)(2,1)S(1)}, u32[]{:S(2)}, u32[]{:S(2)}) collective-permute-start(bf16[48,4096]{1,0:T(8,128)(2,1)S(1)} %collective-permute-done.7.refs_2_), channel_id=1, source_target_pairs={{0,1},{1,0},{2,3},{3,2},{4,5},{5,4},{6,7},{7,6},{8,9},{9,8},{10,11... | collective-permute-start | bytes 1179656 | tf_op jit(solution)/shard_map/ppermute | solution.py:17
  79.7 21.2 %collective-permute-start.19 = (bf16[192,1792]{1,0:T(8,128)(2,1)S(1)}, bf16[192,1792]{1,0:T(8,128)(2,1)}, u32[]{:S(2)}, u32[]{:S(2)}) collective-permute-start(bf16[192,1792]{1,0:T(8,128)(2,1)S(1)} %project_3.1), channel_id=1, source_target_pairs={{0,4},{4,0},{8,12},{12,8},{1,5},{5,1},{9,13},{13,9},{2,6},{6,2},{1... | collective-permute-start | bytes 2064392 | tf_op jit(solution)/shard_map/ppermute | solution.py:17
  82.4 16.5 %collective-permute-start.13 = (bf16[48,4096]{1,0:T(8,128)(2,1)S(1)}, bf16[48,4096]{1,0:T(8,128)(2,1)S(1)}, u32[]{:S(2)}, u32[]{:S(2)}) collective-permute-start(bf16[48,4096]{1,0:T(8,128)(2,1)S(1)} %attend_2.1.refs_0_), channel_id=1, source_target_pairs={{0,1},{1,0},{2,3},{3,2},{4,5},{5,4},{6,7},{7,6},{8,9},{9,8},{10,11... | collective-permute-start | bytes 1179656 | tf_op jit(solution)/shard_map/ppermute | solution.py:17
  82.7 17.9 %collective-permute-start.15 = (bf16[48,4096]{1,0:T(8,128)(2,1)S(1)}, bf16[48,4096]{1,0:T(8,128)(2,1)}, u32[]{:S(2)}, u32[]{:S(2)}) collective-permute-start(bf16[48,4096]{1,0:T(8,128)(2,1)S(1)} %collective-permute-done.14.refs_2_), channel_id=1, source_target_pairs={{0,1},{1,0},{2,3},{3,2},{4,5},{5,4},{6,7},{7,6},{8,9},{9,8},{10,11... | collective-permute-start | bytes 1179656 | tf_op jit(solution)/shard_map/ppermute | solution.py:17
  91.2 19.8 %collective-permute-start.24 = (bf16[128,576]{0,1:T(8,128)(2,1)}, bf16[128,576]{0,1:T(8,128)(2,1)}, u32[]{:S(2)}, u32[]{:S(2)}) collective-permute-start(bf16[128,576]{0,1:T(8,128)(2,1)} %bitcast.30), channel_id=1, source_target_pairs={{0,3},{1,2},{2,1},{3,0},{4,7},{5,6},{6,5},{7,4},{8,11},{9,10},{10,... | collective-permute-start | bytes 442376 | tf_op jit(solution)/shard_map/ppermute | solution.py:17
  92.6 19.0 %collective-permute-start.4 = (bf16[48,4096]{1,0:T(8,128)(2,1)S(1)}, bf16[48,4096]{1,0:T(8,128)(2,1)S(1)}, u32[]{:S(2)}, u32[]{:S(2)}) collective-permute-start(bf16[48,4096]{1,0:T(8,128)(2,1)S(1)} %attend_0.1.refs_0_), channel_id=1, source_target_pairs={{0,2},{1,3},{2,0},{3,1},{4,6},{5,7},{6,4},{7,5},{8,10},{9,11},{10,... | collective-permute-start | bytes 1179656 | tf_op jit(solution)/shard_map/ppermute | solution.py:17
  99.0 13.5 %copy-start.15 = (bf16[1,128,576]{1,0,2:T(2,128)(2,1)S(1)}, bf16[1,128,576]{1,0,2:T(2,128)(2,1)}, u32[]{:S(2)}) copy-start(bf16[1,128,576]{1,0,2:T(2,128)(2,1)} %get-tuple-element.15) | copy-start | bytes 442372
  99.0 12.1 %collective-permute-start.25 = (bf16[128,576]{0,1:T(8,128)(2,1)S(1)}, bf16[128,576]{0,1:T(8,128)(2,1)}, u32[]{:S(2)}, u32[]{:S(2)}) collective-permute-start(bf16[128,576]{0,1:T(8,128)(2,1)S(1)} %bitcast.33), channel_id=1, source_target_pairs={{0,2},{1,3},{2,0},{3,1},{4,6},{5,7},{6,4},{7,5},{8,10},{9,11},{10,... | collective-permute-start | bytes 442376 | tf_op jit(solution)/shard_map/ppermute | solution.py:17
  100.6 24.3 %collective-permute-start.9 = (bf16[192,1792]{1,0:T(8,128)(2,1)}, bf16[192,1792]{1,0:T(8,128)(2,1)}, u32[]{:S(2)}, u32[]{:S(2)}) collective-permute-start(bf16[192,1792]{1,0:T(8,128)(2,1)} %project_1.1), channel_id=1, source_target_pairs={{0,4},{4,0},{8,12},{12,8},{1,5},{5,1},{9,13},{13,9},{2,6},{6,2},{1... | collective-permute-start | bytes 2064392 | tf_op jit(solution)/shard_map/ppermute | solution.py:17
  108.4 32.7 %collective-permute-start.20 = (bf16[192,1792]{1,0:T(8,128)(2,1)}, bf16[192,1792]{1,0:T(8,128)(2,1)S(1)}, u32[]{:S(2)}, u32[]{:S(2)}) collective-permute-start(bf16[192,1792]{1,0:T(8,128)(2,1)} %project_2.1), channel_id=1, source_target_pairs={{0,8},{4,12},{8,0},{12,4},{1,9},{5,13},{9,1},{13,5},{2,10},{6,14},... | collective-permute-start | bytes 2064392 | tf_op jit(solution)/shard_map/ppermute | solution.py:17
  111.0 1.4 collective-permute-start.26
  111.1 2.4 %collective-permute-start.3 = (bf16[48,4096]{1,0:T(8,128)(2,1)S(1)}, bf16[48,4096]{1,0:T(8,128)(2,1)S(1)}, u32[]{:S(2)}, u32[]{:S(2)}) collective-permute-start(bf16[48,4096]{1,0:T(8,128)(2,1)S(1)} %attend_0.1.refs_0_), channel_id=1, source_target_pairs={{0,1},{1,0},{2,3},{3,2},{4,5},{5,4},{6,7},{7,6},{8,9},{9,8},{10,11... | collective-permute-start | bytes 1179656 | tf_op jit(solution)/shard_map/ppermute | solution.py:17
  111.6 2.0 %collective-permute-start.5 = (bf16[48,4096]{1,0:T(8,128)(2,1)S(1)}, bf16[48,4096]{1,0:T(8,128)(2,1)S(1)}, u32[]{:S(2)}, u32[]{:S(2)}) collective-permute-start(bf16[48,4096]{1,0:T(8,128)(2,1)S(1)} %collective-permute-done.4.refs_2_), channel_id=1, source_target_pairs={{0,1},{1,0},{2,3},{3,2},{4,5},{5,4},{6,7},{7,6},{8,9},{9,8},{10,11... | collective-permute-start | bytes 1179656 | tf_op jit(solution)/shard_map/ppermute | solution.py:17
  142.4 3.9 %collective-permute-start.23 = (bf16[48,1792]{1,0:T(8,128)(2,1)S(1)}, bf16[48,1792]{1,0:T(8,128)(2,1)S(1)}, u32[]{:S(2)}, u32[]{:S(2)}) collective-permute-start(bf16[48,1792]{1,0:T(8,128)(2,1)S(1)} %get-tuple-element.12), channel_id=1, source_target_pairs={{0,1},{1,0},{2,3},{3,2},{4,5},{5,4},{6,7},{7,6},{8,9},{9,8},{10,11... | collective-permute-start | bytes 516104 | tf_op jit(solution)/shard_map/ppermute | solution.py:17
  142.5 7.2 %collective-permute-start.22 = (bf16[48,1792]{1,0:T(8,128)(2,1)S(1)}, bf16[48,1792]{1,0:T(8,128)(2,1)S(1)}, u32[]{:S(2)}, u32[]{:S(2)}) collective-permute-start(bf16[48,1792]{1,0:T(8,128)(2,1)S(1)} %get-tuple-element.13), channel_id=1, source_target_pairs={{0,2},{1,3},{2,0},{3,1},{4,6},{5,7},{6,4},{7,5},{8,10},{9,11},{10,... | collective-permute-start | bytes 516104 | tf_op jit(solution)/shard_map/ppermute | solution.py:17
  144.3 8.3 %collective-permute-start.21 = (bf16[48,1792]{1,0:T(8,128)(2,1)S(1)}, bf16[48,1792]{1,0:T(8,128)(2,1)S(1)}, u32[]{:S(2)}, u32[]{:S(2)}) collective-permute-start(bf16[48,1792]{1,0:T(8,128)(2,1)S(1)} %get-tuple-element.14), channel_id=1, source_target_pairs={{0,3},{1,2},{2,1},{3,0},{4,7},{5,6},{6,5},{7,4},{8,11},{9,10},{10,... | collective-permute-start | bytes 516104 | tf_op jit(solution)/shard_map/ppermute | solution.py:17
  (17 other events, 109.3 us)

commit v4 on v3

v4 whole, which is shorter than its diff:
```python
import functools
import math

import jax
import jax.numpy as jnp
from jax import lax
from jax.experimental import pallas as pl
from jax.experimental.pallas import tpu as pltpu
from jax.sharding import PartitionSpec as P

MIB = 1 << 20


def swap(value, axis, distance, inner=1):
    size = lax.axis_size(axis)
    pairs = [(i, ((i // inner) ^ distance) * inner + i % inner) for i in range(size)]
    return lax.ppermute(value, axis, pairs)


def after(value, *others):
    return lax.optimization_barrier((value, *others))[0]


def gather_ranks(value, axis, *earlier):
    size = lax.axis_size(axis)
    pieces = {0: value}
    distance = size // 2
    while distance:
        for k in list(pieces):
            passed = after(pieces[k], *earlier) if k and earlier else pieces[k]
            pieces[k ^ distance] = swap(passed, axis, distance)
        distance //= 2
    return [pieces[k] for k in range(size)]


def part_of(size, wanted, unit=1):
    return max(d for d in range(unit, max(wanted, unit) + 1, unit) if size % d == 0)


def split_columns(width):
    unit = 256 if width % 256 == 0 else 128
    first = width // unit // 2 * unit
    return [(0, first), (first, width - first)] if width % 256 == 0 and first else [(0, width)]


def absorb_kernel(nope_ref, rope_ref, key_ref, out_ref):
    heads, latent, nope = key_ref.shape
    rotary = out_ref.shape[2] - latent
    for h in range(heads):
        out_ref[h, :, :latent] = lax.dot_general(
            nope_ref[:, h * nope : (h + 1) * nope],
            key_ref[h],
            (((1,), (1,)), ((), ())),
            preferred_element_type=jnp.float32,
        ).astype(out_ref.dtype)
        out_ref[h, :, latent:] = rope_ref[:, h * rotary : (h + 1) * rotary]


def absorb(q_nope, q_rope, w_key):
    rows = q_nope.shape[0]
    heads, latent, nope = w_key.shape
    rotary = q_rope.shape[1] // heads
    step = part_of(heads, 4, 2)
    return pl.pallas_call(
        absorb_kernel,
        grid=(heads // step,),
        in_specs=[
            pl.BlockSpec((rows, step * nope), lambda h: (0, h)),
            pl.BlockSpec((rows, step * rotary), lambda h: (0, h)),
            pl.BlockSpec((step, latent, nope), lambda h: (h, 0, 0)),
        ],
        out_specs=pl.BlockSpec((step, rows, latent + rotary), lambda h: (h, 0, 0)),
        out_shape=jax.ShapeDtypeStruct((heads, rows, latent + rotary), q_nope.dtype),
        compiler_params=pltpu.CompilerParams(vmem_limit_bytes=8 * MIB),
        cost_estimate=pl.CostEstimate(flops=1, bytes_accessed=1, transcendentals=0),
        name="absorb",
    )(q_nope, q_rope, w_key)


def attend_kernel(
    distance, scale, ids_ref, prefix_ref, stretch_ref, query_ref, *refs
):
    block_refs, (value_ref, out_ref, keys, hidden) = refs[:4], refs[4:]
    heads, stretch, width = query_ref.shape
    latent, value_width = value_ref.shape[1:]
    part = block_refs[0].shape[2]
    span = 4 * part
    place = ids_ref[0]
    request = place ^ distance

    @pl.when(pl.program_id(0) == 0)
    def _():
        query_pos = prefix_ref[request] + lax.broadcasted_iota(jnp.int32, (stretch, part), 0)
        for k, ref in enumerate(block_refs):
            keys[:, k * part : (k + 1) * part] = ref[0]
            key_pos = (place ^ k) * part + lax.broadcasted_iota(jnp.int32, (stretch, part), 1)
            hidden[:, k * part : (k + 1) * part] = jnp.where(key_pos <= query_pos, 0.0, -1e30)

    query = query_ref[...].reshape(heads * stretch, width)
    scores = jnp.dot(query, keys[...], preferred_element_type=jnp.float32)
    scores = scores.reshape(heads, stretch, span) + hidden[...][None]
    top = jnp.max(scores, axis=2, keepdims=True)
    weights = jnp.exp2((scores - top) * (scale / math.log(2.0)))
    denom = jnp.sum(weights, axis=2, keepdims=True).reshape(heads * stretch, 1)
    latent_out = lax.dot_general(
        weights.astype(jnp.bfloat16).reshape(heads * stretch, span),
        keys[:latent],
        (((1,), (1,)), ((), ())),
        preferred_element_type=jnp.float32,
    )
    latent_out = (latent_out / denom).astype(jnp.bfloat16)
    live = lax.broadcasted_iota(jnp.int32, (stretch, value_width), 0) < stretch_ref[request]
    for h in range(heads):
        head_out = jnp.dot(
            latent_out[h * stretch : (h + 1) * stretch],
            value_ref[h],
            preferred_element_type=jnp.float32,
        )
        out_ref[:, h * value_width : (h + 1) * value_width] = jnp.where(
            live, head_out, 0.0
        ).astype(out_ref.dtype)


def attend(distance, ids, prefix_len, stretch_len, full_query, blocks, w_value, scale):
    heads, rows, width = full_query.shape
    latent, value_width = w_value.shape[1:]
    stretch = rows // prefix_len.shape[0]
    part = blocks[0].shape[2]
    step = part_of(heads, 8)
    span = 4 * part
    return pl.pallas_call(
        functools.partial(attend_kernel, distance, scale),
        grid_spec=pltpu.PrefetchScalarGridSpec(
            num_scalar_prefetch=3,
            grid=(heads // step,),
            in_specs=[
                pl.BlockSpec((step, stretch, width), lambda h, p, *_: (h, p[0] ^ distance, 0))
            ]
            + [pl.BlockSpec((1, width, part), lambda h, p, *_: ((p[0] ^ distance) % 2, 0, 0))] * 4
            + [pl.BlockSpec((step, latent, value_width), lambda h, *_: (h, 0, 0))],
            out_specs=pl.BlockSpec((stretch, step * value_width), lambda h, *_: (0, h)),
            scratch_shapes=[
                pltpu.VMEM((width, span), jnp.bfloat16),
                pltpu.VMEM((stretch, span), jnp.float32),
            ],
        ),
        out_shape=jax.ShapeDtypeStruct((stretch, heads * value_width), jnp.bfloat16),
        compiler_params=pltpu.CompilerParams(vmem_limit_bytes=10 * MIB * max(span // 512, 1)),
        cost_estimate=pl.CostEstimate(flops=1, bytes_accessed=1, transcendentals=0),
        name=f"attend_{distance}",
    )(ids, prefix_len, stretch_len, full_query, *blocks, w_value)


def project_kernel(rank_count, *refs):
    row_refs, (weight_ref, out_ref, rows) = refs[:rank_count], refs[rank_count:]
    stretch = row_refs[0].shape[0]

    @pl.when(pl.program_id(0) == 0)
    def _():
        for k, ref in enumerate(row_refs):
            rows[k * stretch : (k + 1) * stretch] = ref[...]

    total = jnp.dot(rows[...], weight_ref[...], preferred_element_type=jnp.float32)
    out_ref[...] = total.astype(out_ref.dtype)


def project(pieces, w_out, start, columns, dtype, name):
    stretch, depth = pieces[0].shape
    rows = stretch * len(pieces)
    step = part_of(math.gcd(start, columns), 256, 128)
    first = start // step
    return pl.pallas_call(
        functools.partial(project_kernel, len(pieces)),
        grid=(columns // step,),
        in_specs=[pl.BlockSpec((stretch, depth), lambda n: (0, 0))] * len(pieces)
        + [pl.BlockSpec((depth, step), lambda n: (0, first + n))],
        out_specs=pl.BlockSpec((rows, step), lambda n: (0, n)),
        out_shape=jax.ShapeDtypeStruct((rows, columns), dtype),
        scratch_shapes=[pltpu.VMEM((rows, depth), jnp.bfloat16)],
        compiler_params=pltpu.CompilerParams(vmem_limit_bytes=14 * MIB),
        cost_estimate=pl.CostEstimate(flops=1, bytes_accessed=1, transcendentals=0),
        name=name,
    )(*pieces, w_out)


SCALARS = pl.BlockSpec(memory_space=pltpu.SMEM)
WHOLE = pl.BlockSpec(memory_space=pltpu.VMEM)


def handoff_kernel(ids_ref, prefix_ref, stretch_ref, finished_ref, owner_ref, keys_ref, *outs):
    requests, width, block = keys_ref.shape
    pos = ids_ref[2] * block + lax.broadcasted_iota(jnp.int32, (width, block), 1)
    for k, out in enumerate(outs):
        chosen = jnp.zeros((width, block), jnp.float32)
        for q in range(requests):
            here = (finished_ref[q] > 0) & (owner_ref[q] == (ids_ref[1] ^ k))
            end = jnp.where(here, prefix_ref[q] + stretch_ref[q], 0)
            chosen = jnp.where(pos < end, keys_ref[q].astype(jnp.float32), chosen)
        out[...] = chosen.astype(out.dtype)


def handoff(ids, prefix_len, stretch_len, finished, owners, keys, rank_count):
    return pl.pallas_call(
        handoff_kernel,
        in_specs=[SCALARS] * 5 + [WHOLE],
        out_specs=[WHOLE] * rank_count,
        out_shape=[jax.ShapeDtypeStruct(keys.shape[1:], keys.dtype)] * rank_count,
        compiler_params=pltpu.CompilerParams(vmem_limit_bytes=8 * MIB),
        name="handoff",
    )(ids, prefix_len, stretch_len, finished, owners, keys)


def place_blocks_kernel(ids_ref, *refs):
    out = refs[-1]
    for k, ref in enumerate(refs[:-1]):
        out[ids_ref[1] ^ k] = ref[...]


def place_blocks(ids, pieces):
    return pl.pallas_call(
        place_blocks_kernel,
        in_specs=[SCALARS] + [WHOLE] * len(pieces),
        out_specs=WHOLE,
        out_shape=jax.ShapeDtypeStruct((len(pieces), *pieces[0].shape), pieces[0].dtype),
        compiler_params=pltpu.CompilerParams(vmem_limit_bytes=8 * MIB),
        name="place_blocks",
    )(ids, *pieces)


def place_columns_kernel(splits, ids_ref, *refs):
    out = refs[-1]
    width = sum(columns for _, columns in splits)
    for n, ref in enumerate(refs[:-1]):
        k, part = divmod(n, len(splits))
        start, columns = splits[part]
        start = pl.multiple_of((ids_ref[1] ^ k) * width + start, 128)
        out[:, pl.ds(start, columns)] = ref[...]


def place_columns(ids, pieces, splits):
    rows = pieces[0].shape[0]
    width = sum(piece.shape[1] for piece in pieces)
    return pl.pallas_call(
        functools.partial(place_columns_kernel, splits),
        in_specs=[SCALARS] + [WHOLE] * len(pieces),
        out_specs=WHOLE,
        out_shape=jax.ShapeDtypeStruct((rows, width), pieces[0].dtype),
        compiler_params=pltpu.CompilerParams(vmem_limit_bytes=8 * MIB),
        name="place_columns",
    )(ids, *pieces)


def local(
    q_nope, q_rope, latent_keys, w_key, w_value, w_out, prefix_len, stretch_len, finished, owners
):
    request_count = prefix_len.shape[0]
    row_count = q_nope.shape[0]
    head_count, latent_width, nope_width = w_key.shape
    rotary_width = q_rope.shape[1] // head_count
    score_scale = (nope_width + rotary_width) ** (-0.5)
    rank_count = lax.axis_size("request")
    tensor_count = lax.axis_size("tensor")
    inner = tensor_count // request_count
    share_rows = row_count // tensor_count
    rank = lax.axis_index("request")
    place = lax.axis_index("tensor")
    outer_place = place // inner
    ids = jnp.stack([outer_place, rank, place]).astype(jnp.int32)

    block_keys = latent_keys.transpose(0, 2, 1)
    if inner > 1:
        groups = [[o * inner + i for i in range(inner)] for o in range(request_count)]
        own_keys = lax.all_gather(
            block_keys, "tensor", axis=2, tiled=True, axis_index_groups=groups
        )
    else:
        own_keys = block_keys
    near = (outer_place // 2) * 2
    near_keys = lax.dynamic_slice_in_dim(own_keys, near, 2, 0)
    far_keys = lax.dynamic_slice_in_dim(own_keys, near ^ 2, 2, 0)
    far_two = swap(near_keys, "tensor", 2, inner)
    far_one = swap(far_keys, "tensor", 1, inner)

    outgoing = handoff(
        after(ids, far_keys, near_keys),
        prefix_len,
        stretch_len,
        finished,
        owners.reshape(request_count),
        block_keys,
        rank_count,
    )
    full_query = absorb(after(q_nope, *outgoing), q_rope, w_key)
    arrived = [outgoing[0]] + [
        swap(after(outgoing[k], full_query), "request", k) for k in range(1, rank_count)
    ]
    far_three = swap(after(far_two, full_query), "tensor", 1, inner)
    near_two = swap(after(far_keys, far_three), "tensor", 2, inner)
    near_one = swap(after(near_keys, far_three), "tensor", 1, inner)
    far_blocks = [far_keys, far_one, far_two, far_three]
    near_blocks = [near_keys, near_one, near_two]

    def rows_of(distance, blocks, *earlier):
        return attend(
            distance,
            after(ids, *earlier),
            prefix_len,
            stretch_len,
            full_query,
            blocks,
            w_value,
            score_scale,
        )

    splits = split_columns(w_out.shape[1])
    parts = len(splits)
    sent = jnp.bfloat16

    def terms_of(distance, pieces, dtype, *earlier):
        pieces = [after(pieces[0], *earlier)] + pieces[1:]
        return [
            project(pieces, w_out, start, columns, dtype, f"project_{distance}_{start}")
            for start, columns in splits
        ]

    rows_3 = rows_of(3, far_blocks, *arrived)
    rows_2 = rows_of(2, far_blocks, rows_3)
    pieces_3 = gather_ranks(rows_3, "request", rows_2, near_one, near_two)
    terms_3 = terms_of(3, pieces_3, sent, rows_2)
    opposite = [swap(t, "tensor", 1, inner) for t in terms_3]
    near_blocks.append(swap(near_two, "tensor", 1, inner))
    rows_1 = rows_of(1, near_blocks, *terms_3)
    handed = place_blocks(after(ids, rows_1), arrived)
    rows_0 = rows_of(0, near_blocks, rows_1, handed, opposite[-1])
    pieces_2 = gather_ranks(rows_2, "request")
    terms_2 = terms_of(2, pieces_2, jnp.float32, rows_0)
    sums = [(t + o).astype(sent) for t, o in zip(terms_2, opposite)]
    across = [swap(t, "tensor", 2, inner) for t in sums]
    pieces_1 = gather_ranks(rows_1, "request")
    terms_1 = terms_of(1, pieces_1, sent, *sums)
    beside = [swap(t, "tensor", 1, inner) for t in terms_1]
    pieces_0 = gather_ranks(rows_0, "request")
    terms_0 = terms_of(0, pieces_0, jnp.float32, across[-1], *terms_1)

    columns = {}
    earlier = terms_0
    for part in reversed(range(parts)):
        partial = after(terms_0[part] + beside[part], *earlier)
        summed = (partial + across[part]).astype(sent)
        if inner > 1:
            summed = summed.reshape(rank_count, inner, share_rows, summed.shape[1]).swapaxes(0, 1)
            summed = lax.psum_scatter(
                summed, "tensor", scatter_dimension=0, axis_index_groups=groups, tiled=True
            )
        summed = summed.reshape(rank_count, share_rows, summed.shape[-1])
        earlier = [swap(summed[k], "request", k) for k in range(1, rank_count)]
        columns[part] = [summed[0]] + earlier
    ordered = [columns[part][k] for k in range(rank_count) for part in range(parts)]
    mixed = place_columns(ids, ordered, splits)[None]
    handed = handed.transpose(0, 2, 1)[None]
    return (mixed, handed)


def solution(mesh):
    placed = (
        P(("groups", "request"), "tensor"),
        P(("groups", "request"), "tensor"),
        P(("groups", "request"), "tensor", None),
        P("tensor", None, None),
        P("tensor", None, None),
        P("tensor", "request"),
        P(("groups", "request")),
        P(("groups", "request")),
        P(("groups", "request")),
        P(("groups", "request"), "tensor"),
    )
    return jax.shard_map(
        local,
        mesh=mesh,
        in_specs=placed,
        out_specs=(
            P(("groups", "request"), "tensor", None),
            P(("groups", "request"), None, "tensor", None),
        ),
        check_vma=False,
    )
```

time: 154 us -> 136 us (0.88)
  waiting for transfers between devices: 54.3 us -> 43 us
  starting transfers between devices: 23.1 us -> 33.1 us
  local copies, waits for them, and re-layouts: 18.1 us -> 9.59 us
  other arithmetic: 5.34 us -> 0.54 us
  Pallas kernels: 50.2 us -> 48.4 us
    ppermute x27 -> x33, waiting for transfers between devices: 54.3 us -> 43 us  [swap(): return lax.ppermute(value, axis, pairs)]
    ppermute x27 -> x33, starting transfers between devices: 23.1 us -> 33.1 us  [swap(): return lax.ppermute(value, axis, pairs)]
    unnamed x49 -> x30, local copies, waits for them, and re-layouts: 15.3 us -> 8.44 us
    pallas_call x4, Pallas kernels: 21.9 us -> 19.6 us  [attend(): pl.pallas_call(functools.partial(attend_kernel, distance, scale), grid_sp...]
    another operation x2 -> x1, other arithmetic: 2.04 us -> 0.08 us  [local(): ids = jnp.stack([outer_place, rank, place]).astype(jnp.int32)]
    broadcast_in_dim x2 -> x0, other arithmetic: 1.79 us -> none  [the longest x1 0.89 us: local(): mixed = jnp.concatenate(by_rank(columns, rank), axis=1)[None]]
    pallas_call x4 -> x11, Pallas kernels: 25 us -> 25.5 us  [the longest x8 21.8 us: project(): pl.pallas_call(functools.partial(project_kernel, len(pieces)), grid=(colu...]
  transfers between devices with their start and end apart: 27 -> 33, of which waited for: 9 -> 11; matrix products, arithmetic and copies ran while one was open for 5% -> 0% of each run, Pallas kernels for 33% -> 31%
where the time goes in v4:
time: 136 us
  Pallas kernels  48.4 us (36%)
  waiting for transfers between devices  43 us (32%)
  starting transfers between devices  33.1 us (24%)
  local copies, waits for them, and re-layouts  9.59 us (7%)
    ppermute x33, waiting for transfers between devices, swap(): return lax.ppermute(value, axis, pairs)  43 us
    ppermute x33, starting transfers between devices, swap(): return lax.ppermute(value, axis, pairs)  33.1 us
    pallas_call x8, Pallas kernels, project(): pl.pallas_call(functools.partial(project_kernel, len(pieces)), grid=(colu...  21.8 us
    pallas_call x4, Pallas kernels, attend(): pl.pallas_call(functools.partial(attend_kernel, distance, scale), grid_sp...  19.6 us
    unnamed x30, local copies, waits for them, and re-layouts  8.44 us
    pallas_call x1, Pallas kernels, absorb(): pl.pallas_call(absorb_kernel, grid=(heads // step,), in_specs=[pl.BlockSp...  3.27 us
  transfers between devices with their start and end apart: 33, of which 11 were waited for; matrix products, arithmetic and copies ran while one was open for 0% of the time, Pallas kernels for 31%

profile of v4, /device:TPU:0, one launch (start us, length us, event | category | flops | bytes accessed | tf_op | source)
XLA Modules:
  0.0 135.7 jit_solution(13013480410848210758)
XLA Ops:
  1.8 4.1 %collective-permute-start.4 = (bf16[2,576,128]{2,1,0:T(8,128)(2,1)S(1)}, bf16[2,576,128]{2,1,0:T(8,128)(2,1)S(1)}, u32[]{:S(2)}, u32[]{:S(2)}) collective-permute-start(bf16[2,576,128]{2,1,0:T(8,128)(2,1)S(1)} %get-tuple-element.39.refs_0_), channel_id=1, source_target_pairs={{0,8},{4,12},{8,0},{12,4},{1,9},{5,13},{9,1},{13,5},{2,10},{6,14},... | collective-permute-start | bytes 884744 | tf_op jit(solution)/shard_map/ppermute | solution.py:17
  5.9 1.6 %collective-permute-start.3 = (bf16[2,576,128]{2,1,0:T(8,128)(2,1)S(1)}, bf16[2,576,128]{2,1,0:T(8,128)(2,1)S(1)}, u32[]{:S(2)}, u32[]{:S(2)}) collective-permute-start(bf16[2,576,128]{2,1,0:T(8,128)(2,1)S(1)} %get-tuple-element.40.refs_0_), channel_id=1, source_target_pairs={{0,4},{4,0},{8,12},{12,8},{1,5},{5,1},{9,13},{13,9},{2,6},{6,2},{1... | collective-permute-start | bytes 884744 | tf_op jit(solution)/shard_map/ppermute | solution.py:17
  12.1 2.2 %copy-done.1 = bf16[32,512,128]{2,1,0:T(8,128)(2,1)S(1)} copy-done((bf16[32,512,128]{2,1,0:T(8,128)(2,1)S(1)}, bf16[32,512,128]{2,1,0:T(8,128)(2,1)}, u32[]{:S(2)}) %copy-start.1) | copy-done | bytes 4194328
  16.8 3.3 %absorb.1.query_ref = bf16[32,192,576]{2,1,0:T(8,128)(2,1)S(1)} custom-call(bf16[192,4096]{1,0:T(8,128)(2,1)S(1)} %copy-done.3, bf16[192,2048]{1,0:T(8,128)(2,1)S(1)} %copy-done.4, bf16[32,512,128]{2,1,0:T(8,128)(2,1)S(1)} %copy-done.1), custom_call_target="tpu_custom_call" | custom-call | flops 1 | bytes 1 | tf_op jit(solution)/shard_map/absorb/pallas_call | solution.py:64
  22.5 4.2 %collective-permute-done.2.refs_3_ = bf16[576,128]{1,0:T(8,128)(2,1)S(1)} collective-permute-done((bf16[576,128]{1,0:T(8,128)(2,1)S(1)}, bf16[576,128]{1,0:T(8,128)(2,1)S(1)}, u32[]{:S(2)}, u32[]{:S(2)}) %collective-permute-start.2) | collective-permute-done | bytes 147488 | tf_op jit(solution)/shard_map/ppermute | solution.py:17
  26.8 3.2 %collective-permute-done.1.refs_2_ = bf16[576,128]{1,0:T(8,128)(2,1)S(1)} collective-permute-done((bf16[576,128]{1,0:T(8,128)(2,1)S(1)}, bf16[576,128]{1,0:T(8,128)(2,1)S(1)}, u32[]{:S(2)}, u32[]{:S(2)}) %collective-permute-start.1) | collective-permute-done | bytes 147488 | tf_op jit(solution)/shard_map/ppermute | solution.py:17
  30.1 4.9 %attend_3.1.refs_0_ = bf16[48,4096]{1,0:T(8,128)(2,1)S(1)} custom-call(s32[3]{0:T(128)S(1)} %pad_add_fusion.ids_ref, s32[4]{0:T(128)S(1)} %copy-done.6, s32[4]{0:T(128)S(1)} %copy-done.8, bf16[32,192,576]{2,1,0:T(8,128)(2,1)S(1)} %absorb.1.query_ref, bf16[2,576,128]{2,1,0:T(8,128)(2,1)S(1)} %get-tuple-element.40.refs_0_, ...), custom_call_target="tpu_custom_call" | custom-call | flops 1 | bytes 1 | tf_op jit(solution)/shard_map/attend_3/pallas_call | solution.py:131
  35.1 1.6 %collective-permute-start.8 = (bf16[2,576,128]{2,1,0:T(8,128)(2,1)S(1)}, bf16[2,576,128]{2,1,0:T(8,128)(2,1)S(1)}, u32[]{:S(2)}, u32[]{:S(2)}) collective-permute-start(bf16[2,576,128]{2,1,0:T(8,128)(2,1)S(1)} %get-tuple-element.39.refs_0_), channel_id=1, source_target_pairs={{0,4},{4,0},{8,12},{12,8},{1,5},{5,1},{9,13},{13,9},{2,6},{6,2},{1... | collective-permute-start | bytes 884744 | tf_op jit(solution)/shard_map/ppermute | solution.py:17
  36.7 2.5 %collective-permute-start.9 = (bf16[2,576,128]{2,1,0:T(8,128)(2,1)S(1)}, bf16[2,576,128]{2,1,0:T(8,128)(2,1)S(1)}, u32[]{:S(2)}, u32[]{:S(2)}) collective-permute-start(bf16[2,576,128]{2,1,0:T(8,128)(2,1)S(1)} %get-tuple-element.40.refs_0_), channel_id=1, source_target_pairs={{0,8},{4,12},{8,0},{12,4},{1,9},{5,13},{9,1},{13,5},{2,10},{6,14},... | collective-permute-start | bytes 884744 | tf_op jit(solution)/shard_map/ppermute | solution.py:17
  39.1 4.9 %attend_2.1.refs_0_ = bf16[48,4096]{1,0:T(8,128)(2,1)S(1)} custom-call(s32[3]{0:T(128)S(1)} %pad_add_fusion.ids_ref, s32[4]{0:T(128)S(1)} %copy-done.6, s32[4]{0:T(128)S(1)} %copy-done.8, bf16[32,192,576]{2,1,0:T(8,128)(2,1)S(1)} %absorb.1.query_ref, bf16[2,576,128]{2,1,0:T(8,128)(2,1)S(1)} %get-tuple-element.40.refs_0_, ...), custom_call_target="tpu_custom_call" | custom-call | flops 1 | bytes 1 | tf_op jit(solution)/shard_map/attend_2/pallas_call | solution.py:131
  44.1 6.4 %collective-permute-done.8.refs_1_ = bf16[2,576,128]{2,1,0:T(8,128)(2,1)S(1)} collective-permute-done((bf16[2,576,128]{2,1,0:T(8,128)(2,1)S(1)}, bf16[2,576,128]{2,1,0:T(8,128)(2,1)S(1)}, u32[]{:S(2)}, u32[]{:S(2)}) %collective-permute-start.8) | collective-permute-done | bytes 294944 | tf_op jit(solution)/shard_map/ppermute | solution.py:17
  50.5 3.8 %collective-permute-start.14 = (bf16[48,4096]{1,0:T(8,128)(2,1)S(1)}, bf16[48,4096]{1,0:T(8,128)(2,1)S(1)}, u32[]{:S(2)}, u32[]{:S(2)}) collective-permute-start(bf16[48,4096]{1,0:T(8,128)(2,1)S(1)} %attend_2.1.refs_0_), channel_id=1, source_target_pairs={{0,2},{1,3},{2,0},{3,1},{4,6},{5,7},{6,4},{7,5},{8,10},{9,11},{10,... | collective-permute-start | bytes 1179656 | tf_op jit(solution)/shard_map/ppermute | solution.py:17
  54.9 3.1 %project_3_768.1 = bf16[192,1024]{1,0:T(8,128)(2,1)S(1)} custom-call(bf16[48,4096]{1,0:T(8,128)(2,1)S(1)} %attend_3.1.refs_0_, bf16[48,4096]{1,0:T(8,128)(2,1)S(1)} %collective-permute-done.6.refs_1_, bf16[48,4096]{1,0:T(8,128)(2,1)S(1)} %collective-permute-done.7.refs_2_, bf16[48,4096]{1,0:T(8,128)(2,1)S(1)} %collective-permute-done.10.refs_3_, ...), custom_call_target="tpu_custom_call" | custom-call | flops 1 | bytes 1 | tf_op jit(solution)/shard_map/project_3_768/pallas_call | solution.py:172
  58.0 1.6 %collective-permute-start.12 = (bf16[192,1024]{1,0:T(8,128)(2,1)S(1)}, bf16[192,1024]{1,0:T(8,128)(2,1)S(1)}, u32[]{:S(2)}, u32[]{:S(2)}) collective-permute-start(bf16[192,1024]{1,0:T(8,128)(2,1)S(1)} %project_3_768.1), channel_id=1, source_target_pairs={{0,4},{4,0},{8,12},{12,8},{1,5},{5,1},{9,13},{13,9},{2,6},{6,2},{1... | collective-permute-start | bytes 1179656 | tf_op jit(solution)/shard_map/ppermute | solution.py:17
  59.5 4.5 %collective-permute-done.14.refs_2_ = bf16[48,4096]{1,0:T(8,128)(2,1)S(1)} collective-permute-done((bf16[48,4096]{1,0:T(8,128)(2,1)S(1)}, bf16[48,4096]{1,0:T(8,128)(2,1)S(1)}, u32[]{:S(2)}, u32[]{:S(2)}) %collective-permute-start.14) | collective-permute-done | bytes 393248 | tf_op jit(solution)/shard_map/ppermute | solution.py:17
  64.1 2.3 %project_3_0.1 = bf16[192,768]{1,0:T(8,128)(2,1)S(1)} custom-call(bf16[48,4096]{1,0:T(8,128)(2,1)S(1)} %attend_3.1.refs_0_, bf16[48,4096]{1,0:T(8,128)(2,1)S(1)} %collective-permute-done.6.refs_1_, bf16[48,4096]{1,0:T(8,128)(2,1)S(1)} %collective-permute-done.7.refs_2_, bf16[48,4096]{1,0:T(8,128)(2,1)S(1)} %collective-permute-done.10.refs_3_, ...), custom_call_target="tpu_custom_call" | custom-call | flops 1 | bytes 1 | tf_op jit(solution)/shard_map/project_3_0/pallas_call | solution.py:172
  66.4 4.9 %attend_1.1.refs_0_ = bf16[48,4096]{1,0:T(8,128)(2,1)S(1)} custom-call(s32[3]{0:T(128)S(1)} %pad_add_fusion.ids_ref, s32[4]{0:T(128)S(1)} %copy-done.6, s32[4]{0:T(128)S(1)} %copy-done.8, bf16[32,192,576]{2,1,0:T(8,128)(2,1)S(1)} %absorb.1.query_ref, bf16[2,576,128]{2,1,0:T(8,128)(2,1)S(1)} %get-tuple-element.39.refs_0_, ...), custom_call_target="tpu_custom_call" | custom-call | flops 1 | bytes 1 | tf_op jit(solution)/shard_map/attend_1/pallas_call | solution.py:131
  71.4 1.8 %collective-permute-start.19 = (bf16[48,4096]{1,0:T(8,128)(2,1)S(1)}, bf16[48,4096]{1,0:T(8,128)(2,1)S(1)}, u32[]{:S(2)}, u32[]{:S(2)}) collective-permute-start(bf16[48,4096]{1,0:T(8,128)(2,1)S(1)} %attend_1.1.refs_0_), channel_id=1, source_target_pairs={{0,2},{1,3},{2,0},{3,1},{4,6},{5,7},{6,4},{7,5},{8,10},{9,11},{10,... | collective-permute-start | bytes 1179656 | tf_op jit(solution)/shard_map/ppermute | solution.py:17
  75.1 4.9 %attend_0.1.refs_0_ = bf16[48,4096]{1,0:T(8,128)(2,1)S(1)} custom-call(s32[3]{0:T(128)S(1)} %pad_add_fusion.ids_ref, s32[4]{0:T(128)S(1)} %copy-done.6, s32[4]{0:T(128)S(1)} %copy-done.8, bf16[32,192,576]{2,1,0:T(8,128)(2,1)S(1)} %absorb.1.query_ref, bf16[2,576,128]{2,1,0:T(8,128)(2,1)S(1)} %get-tuple-element.39.refs_0_, ...), custom_call_target="tpu_custom_call" | custom-call | flops 1 | bytes 1 | tf_op jit(solution)/shard_map/attend_0/pallas_call | solution.py:131
  81.5 2.3 %project_2_0.1 = f32[192,768]{1,0:T(8,128)S(1)} custom-call(bf16[48,4096]{1,0:T(8,128)(2,1)S(1)} %attend_2.1.refs_0_, bf16[48,4096]{1,0:T(8,128)(2,1)S(1)} %collective-permute-done.13.refs_1_, bf16[48,4096]{1,0:T(8,128)(2,1)S(1)} %collective-permute-done.14.refs_2_, bf16[48,4096]{1,0:T(8,128)(2,1)S(1)} %collective-permute-done.15.refs_3_, ...), custom_call_target="tpu_custom_call" | custom-call | flops 1 | bytes 1 | tf_op jit(solution)/shard_map/project_2_0/pallas_call | solution.py:172
  83.9 3.1 %project_2_768.1 = f32[192,1024]{1,0:T(8,128)S(1)} custom-call(bf16[48,4096]{1,0:T(8,128)(2,1)S(1)} %attend_2.1.refs_0_, bf16[48,4096]{1,0:T(8,128)(2,1)S(1)} %collective-permute-done.13.refs_1_, bf16[48,4096]{1,0:T(8,128)(2,1)S(1)} %collective-permute-done.14.refs_2_, bf16[48,4096]{1,0:T(8,128)(2,1)S(1)} %collective-permute-done.15.refs_3_, ...), custom_call_target="tpu_custom_call" | custom-call | flops 1 | bytes 1 | tf_op jit(solution)/shard_map/project_2_768/pallas_call | solution.py:172
  87.5 2.8 %collective-permute-start.16 = (bf16[192,1024]{1,0:T(8,128)(2,1)S(1)}, bf16[192,1024]{1,0:T(8,128)(2,1)S(1)}, u32[]{:S(2)}, u32[]{:S(2)}) collective-permute-start(bf16[192,1024]{1,0:T(8,128)(2,1)S(1)} %add_convert_fusion.1), channel_id=1, source_target_pairs={{0,8},{4,12},{8,0},{12,4},{1,9},{5,13},{9,1},{13,5},{2,10},{6,14},... | collective-permute-start | bytes 1179656 | tf_op jit(solution)/shard_map/ppermute | solution.py:17
  91.6 3.1 %project_1_768.1 = bf16[192,1024]{1,0:T(8,128)(2,1)S(1)} custom-call(bf16[48,4096]{1,0:T(8,128)(2,1)S(1)} %attend_1.1.refs_0_, bf16[48,4096]{1,0:T(8,128)(2,1)S(1)} %collective-permute-done.18.refs_1_, bf16[48,4096]{1,0:T(8,128)(2,1)S(1)} %collective-permute-done.19.refs_2_, bf16[48,4096]{1,0:T(8,128)(2,1)S(1)} %collective-permute-done.20.refs_3_, ...), custom_call_target="tpu_custom_call" | custom-call | flops 1 | bytes 1 | tf_op jit(solution)/shard_map/project_1_768/pallas_call | solution.py:172
  94.7 1.6 %collective-permute-start.25 = (bf16[192,1024]{1,0:T(8,128)(2,1)S(1)}, bf16[192,1024]{1,0:T(8,128)(2,1)S(1)}, u32[]{:S(2)}, u32[]{:S(2)}) collective-permute-start(bf16[192,1024]{1,0:T(8,128)(2,1)S(1)} %project_1_768.1), channel_id=1, source_target_pairs={{0,4},{4,0},{8,12},{12,8},{1,5},{5,1},{9,13},{13,9},{2,6},{6,2},{1... | collective-permute-start | bytes 1179656 | tf_op jit(solution)/shard_map/ppermute | solution.py:17
  96.3 2.5 %collective-permute-start.29 = (bf16[192,768]{1,0:T(8,128)(2,1)S(1)}, bf16[192,768]{1,0:T(8,128)(2,1)S(1)}, u32[]{:S(2)}, u32[]{:S(2)}) collective-permute-start(bf16[192,768]{1,0:T(8,128)(2,1)S(1)} %add_convert_fusion.3), channel_id=1, source_target_pairs={{0,8},{4,12},{8,0},{12,4},{1,9},{5,13},{9,1},{13,5},{2,10},{6,14},... | collective-permute-start | bytes 884744 | tf_op jit(solution)/shard_map/ppermute | solution.py:17
  98.8 2.3 %project_1_0.1 = bf16[192,768]{1,0:T(8,128)(2,1)S(1)} custom-call(bf16[48,4096]{1,0:T(8,128)(2,1)S(1)} %attend_1.1.refs_0_, bf16[48,4096]{1,0:T(8,128)(2,1)S(1)} %collective-permute-done.18.refs_1_, bf16[48,4096]{1,0:T(8,128)(2,1)S(1)} %collective-permute-done.19.refs_2_, bf16[48,4096]{1,0:T(8,128)(2,1)S(1)} %collective-permute-done.20.refs_3_, ...), custom_call_target="tpu_custom_call" | custom-call | flops 1 | bytes 1 | tf_op jit(solution)/shard_map/project_1_0/pallas_call | solution.py:172
  101.1 7.5 %collective-permute-done.16 = bf16[192,1024]{1,0:T(8,128)(2,1)S(1)} collective-permute-done((bf16[192,1024]{1,0:T(8,128)(2,1)S(1)}, bf16[192,1024]{1,0:T(8,128)(2,1)S(1)}, u32[]{:S(2)}, u32[]{:S(2)}) %collective-permute-start.16) | collective-permute-done | bytes 393248 | tf_op jit(solution)/shard_map/ppermute | solution.py:17
  108.6 3.1 %project_0_768.1 = f32[192,1024]{1,0:T(8,128)S(1)} custom-call(bf16[48,4096]{1,0:T(8,128)(2,1)S(1)} %attend_0.1.refs_0_, bf16[48,4096]{1,0:T(8,128)(2,1)S(1)} %collective-permute-done.21.refs_1_, bf16[48,4096]{1,0:T(8,128)(2,1)S(1)} %collective-permute-done.22.refs_2_, bf16[48,4096]{1,0:T(8,128)(2,1)S(1)} %collective-permute-done.23.refs_3_, ...), custom_call_target="tpu_custom_call" | custom-call | flops 1 | bytes 1 | tf_op jit(solution)/shard_map/project_0_768/pallas_call | solution.py:172
  111.7 2.3 %project_0_0.1 = f32[192,768]{1,0:T(8,128)S(1)} custom-call(bf16[48,4096]{1,0:T(8,128)(2,1)S(1)} %attend_0.1.refs_0_, bf16[48,4096]{1,0:T(8,128)(2,1)S(1)} %collective-permute-done.21.refs_1_, bf16[48,4096]{1,0:T(8,128)(2,1)S(1)} %collective-permute-done.22.refs_2_, bf16[48,4096]{1,0:T(8,128)(2,1)S(1)} %collective-permute-done.23.refs_3_, ...), custom_call_target="tpu_custom_call" | custom-call | flops 1 | bytes 1 | tf_op jit(solution)/shard_map/project_0_0/pallas_call | solution.py:172
  114.0 7.3 %collective-permute-done.25 = bf16[192,1024]{1,0:T(8,128)(2,1)S(1)} collective-permute-done((bf16[192,1024]{1,0:T(8,128)(2,1)S(1)}, bf16[192,1024]{1,0:T(8,128)(2,1)S(1)}, u32[]{:S(2)}, u32[]{:S(2)}) %collective-permute-start.25) | collective-permute-done | bytes 393248 | tf_op jit(solution)/shard_map/ppermute | solution.py:17
  123.5 3.7 %collective-permute-done.24 = bf16[192,768]{1,0:T(8,128)(2,1)S(1)} collective-permute-done((bf16[192,768]{1,0:T(8,128)(2,1)S(1)}, bf16[192,768]{1,0:T(8,128)(2,1)S(1)}, u32[]{:S(2)}, u32[]{:S(2)}) %collective-permute-start.24) | collective-permute-done | bytes 294944 | tf_op jit(solution)/shard_map/ppermute | solution.py:17
  130.5 3.5 %collective-permute-done.31.refs_4_ = bf16[48,768]{1,0:T(8,128)(2,1)S(1)} collective-permute-done((bf16[48,768]{1,0:T(8,128)(2,1)S(1)}, bf16[48,768]{1,0:T(8,128)(2,1)S(1)}, u32[]{:S(2)}, u32[]{:S(2)}) %collective-permute-start.31) | collective-permute-done | bytes 73760 | tf_op jit(solution)/shard_map/ppermute | solution.py:17
  (91 shorter events, 23.7 us)
Async XLA Ops:
  1.8 18.4 %collective-permute-start.4 = (bf16[2,576,128]{2,1,0:T(8,128)(2,1)S(1)}, bf16[2,576,128]{2,1,0:T(8,128)(2,1)S(1)}, u32[]{:S(2)}, u32[]{:S(2)}) collective-permute-start(bf16[2,576,128]{2,1,0:T(8,128)(2,1)S(1)} %get-tuple-element.39.refs_0_), channel_id=1, source_target_pairs={{0,8},{4,12},{8,0},{12,4},{1,9},{5,13},{9,1},{13,5},{2,10},{6,14},... | collective-permute-start | bytes 884744 | tf_op jit(solution)/shard_map/ppermute | solution.py:17
  5.9 24.1 %collective-permute-start.3 = (bf16[2,576,128]{2,1,0:T(8,128)(2,1)S(1)}, bf16[2,576,128]{2,1,0:T(8,128)(2,1)S(1)}, u32[]{:S(2)}, u32[]{:S(2)}) collective-permute-start(bf16[2,576,128]{2,1,0:T(8,128)(2,1)S(1)} %get-tuple-element.40.refs_0_), channel_id=1, source_target_pairs={{0,4},{4,0},{8,12},{12,8},{1,5},{5,1},{9,13},{13,9},{2,6},{6,2},{1... | collective-permute-start | bytes 884744 | tf_op jit(solution)/shard_map/ppermute | solution.py:17
  20.1 9.9 %collective-permute-start.5 = (bf16[2,576,128]{2,1,0:T(8,128)(2,1)S(1)}, bf16[2,576,128]{2,1,0:T(8,128)(2,1)S(1)}, u32[]{:S(2)}, u32[]{:S(2)}) collective-permute-start(bf16[2,576,128]{2,1,0:T(8,128)(2,1)S(1)} %collective-permute-done.4.refs_2_), channel_id=1, source_target_pairs={{0,4},{4,0},{8,12},{12,8},{1,5},{5,1},{9,13},{13,9},{2,6},{6,2},{1... | collective-permute-start | bytes 884744 | tf_op jit(solution)/shard_map/ppermute | solution.py:17
  20.7 6.1 %collective-permute-start.2 = (bf16[576,128]{1,0:T(8,128)(2,1)S(1)}, bf16[576,128]{1,0:T(8,128)(2,1)S(1)}, u32[]{:S(2)}, u32[]{:S(2)}) collective-permute-start(bf16[576,128]{1,0:T(8,128)(2,1)S(1)} %get-tuple-element.34), channel_id=1, source_target_pairs={{0,3},{1,2},{2,1},{3,0},{4,7},{5,6},{6,5},{7,4},{8,11},{9,10},{10,... | collective-permute-start | bytes 442376 | tf_op jit(solution)/shard_map/ppermute | solution.py:17
  20.7 9.2 %collective-permute-start.1 = (bf16[576,128]{1,0:T(8,128)(2,1)S(1)}, bf16[576,128]{1,0:T(8,128)(2,1)S(1)}, u32[]{:S(2)}, u32[]{:S(2)}) collective-permute-start(bf16[576,128]{1,0:T(8,128)(2,1)S(1)} %get-tuple-element.33), channel_id=1, source_target_pairs={{0,2},{1,3},{2,0},{3,1},{4,6},{5,7},{6,4},{7,5},{8,10},{9,11},{10,... | collective-permute-start | bytes 442376 | tf_op jit(solution)/shard_map/ppermute | solution.py:17
  22.2 7.8 %collective-permute-start = (bf16[576,128]{1,0:T(8,128)(2,1)S(1)}, bf16[576,128]{1,0:T(8,128)(2,1)S(1)}, u32[]{:S(2)}, u32[]{:S(2)}) collective-permute-start(bf16[576,128]{1,0:T(8,128)(2,1)S(1)} %get-tuple-element.32), channel_id=1, source_target_pairs={{0,1},{1,0},{2,3},{3,2},{4,5},{5,4},{6,7},{7,6},{8,9},{9,8},{10,11... | collective-permute-start | bytes 442376 | tf_op jit(solution)/shard_map/ppermute | solution.py:17
  35.0 15.5 %collective-permute-start.7 = (bf16[48,4096]{1,0:T(8,128)(2,1)S(1)}, bf16[48,4096]{1,0:T(8,128)(2,1)S(1)}, u32[]{:S(2)}, u32[]{:S(2)}) collective-permute-start(bf16[48,4096]{1,0:T(8,128)(2,1)S(1)} %attend_3.1.refs_0_), channel_id=1, source_target_pairs={{0,2},{1,3},{2,0},{3,1},{4,6},{5,7},{6,4},{7,5},{8,10},{9,11},{10,... | collective-permute-start | bytes 1179656 | tf_op jit(solution)/shard_map/ppermute | solution.py:17
  35.1 15.4 %collective-permute-start.8 = (bf16[2,576,128]{2,1,0:T(8,128)(2,1)S(1)}, bf16[2,576,128]{2,1,0:T(8,128)(2,1)S(1)}, u32[]{:S(2)}, u32[]{:S(2)}) collective-permute-start(bf16[2,576,128]{2,1,0:T(8,128)(2,1)S(1)} %get-tuple-element.39.refs_0_), channel_id=1, source_target_pairs={{0,4},{4,0},{8,12},{12,8},{1,5},{5,1},{9,13},{13,9},{2,6},{6,2},{1... | collective-permute-start | bytes 884744 | tf_op jit(solution)/shard_map/ppermute | solution.py:17
  36.7 13.8 %collective-permute-start.9 = (bf16[2,576,128]{2,1,0:T(8,128)(2,1)S(1)}, bf16[2,576,128]{2,1,0:T(8,128)(2,1)S(1)}, u32[]{:S(2)}, u32[]{:S(2)}) collective-permute-start(bf16[2,576,128]{2,1,0:T(8,128)(2,1)S(1)} %get-tuple-element.40.refs_0_), channel_id=1, source_target_pairs={{0,8},{4,12},{8,0},{12,4},{1,9},{5,13},{9,1},{13,5},{2,10},{6,14},... | collective-permute-start | bytes 884744 | tf_op jit(solution)/shard_map/ppermute | solution.py:17
  39.1 15.7 %collective-permute-start.6 = (bf16[48,4096]{1,0:T(8,128)(2,1)S(1)}, bf16[48,4096]{1,0:T(8,128)(2,1)S(1)}, u32[]{:S(2)}, u32[]{:S(2)}) collective-permute-start(bf16[48,4096]{1,0:T(8,128)(2,1)S(1)} %attend_3.1.refs_0_), channel_id=1, source_target_pairs={{0,1},{1,0},{2,3},{3,2},{4,5},{5,4},{6,7},{7,6},{8,9},{9,8},{10,11... | collective-permute-start | bytes 1179656 | tf_op jit(solution)/shard_map/ppermute | solution.py:17
  50.5 4.4 %collective-permute-start.10 = (bf16[48,4096]{1,0:T(8,128)(2,1)S(1)}, bf16[48,4096]{1,0:T(8,128)(2,1)S(1)}, u32[]{:S(2)}, u32[]{:S(2)}) collective-permute-start(bf16[48,4096]{1,0:T(8,128)(2,1)S(1)} %collective-permute-done.7.refs_2_), channel_id=1, source_target_pairs={{0,1},{1,0},{2,3},{3,2},{4,5},{5,4},{6,7},{7,6},{8,9},{9,8},{10,11... | collective-permute-start | bytes 1179656 | tf_op jit(solution)/shard_map/ppermute | solution.py:17
  50.5 13.6 %collective-permute-start.14 = (bf16[48,4096]{1,0:T(8,128)(2,1)S(1)}, bf16[48,4096]{1,0:T(8,128)(2,1)S(1)}, u32[]{:S(2)}, u32[]{:S(2)}) collective-permute-start(bf16[48,4096]{1,0:T(8,128)(2,1)S(1)} %attend_2.1.refs_0_), channel_id=1, source_target_pairs={{0,2},{1,3},{2,0},{3,1},{4,6},{5,7},{6,4},{7,5},{8,10},{9,11},{10,... | collective-permute-start | bytes 1179656 | tf_op jit(solution)/shard_map/ppermute | solution.py:17
  54.3 12.1 %collective-permute-start.11 = (bf16[2,576,128]{2,1,0:T(8,128)(2,1)S(1)}, bf16[2,576,128]{2,1,0:T(8,128)(2,1)S(1)}, u32[]{:S(2)}, u32[]{:S(2)}) collective-permute-start(bf16[2,576,128]{2,1,0:T(8,128)(2,1)S(1)} %collective-permute-done.9.refs_2_), channel_id=1, source_target_pairs={{0,4},{4,0},{8,12},{12,8},{1,5},{5,1},{9,13},{13,9},{2,6},{6,2},{1... | collective-permute-start | bytes 884744 | tf_op jit(solution)/shard_map/ppermute | solution.py:17
  58.0 17.1 %collective-permute-start.12 = (bf16[192,1024]{1,0:T(8,128)(2,1)S(1)}, bf16[192,1024]{1,0:T(8,128)(2,1)S(1)}, u32[]{:S(2)}, u32[]{:S(2)}) collective-permute-start(bf16[192,1024]{1,0:T(8,128)(2,1)S(1)} %project_3_768.1), channel_id=1, source_target_pairs={{0,4},{4,0},{8,12},{12,8},{1,5},{5,1},{9,13},{13,9},{2,6},{6,2},{1... | collective-permute-start | bytes 1179656 | tf_op jit(solution)/shard_map/ppermute | solution.py:17
  59.5 20.4 %collective-permute-start.13 = (bf16[48,4096]{1,0:T(8,128)(2,1)S(1)}, bf16[48,4096]{1,0:T(8,128)(2,1)S(1)}, u32[]{:S(2)}, u32[]{:S(2)}) collective-permute-start(bf16[48,4096]{1,0:T(8,128)(2,1)S(1)} %attend_2.1.refs_0_), channel_id=1, source_target_pairs={{0,1},{1,0},{2,3},{3,2},{4,5},{5,4},{6,7},{7,6},{8,9},{9,8},{10,11... | collective-permute-start | bytes 1179656 | tf_op jit(solution)/shard_map/ppermute | solution.py:17
  64.1 17.3 %collective-permute-start.15 = (bf16[48,4096]{1,0:T(8,128)(2,1)S(1)}, bf16[48,4096]{1,0:T(8,128)(2,1)S(1)}, u32[]{:S(2)}, u32[]{:S(2)}) collective-permute-start(bf16[48,4096]{1,0:T(8,128)(2,1)S(1)} %collective-permute-done.14.refs_2_), channel_id=1, source_target_pairs={{0,1},{1,0},{2,3},{3,2},{4,5},{5,4},{6,7},{7,6},{8,9},{9,8},{10,11... | collective-permute-start | bytes 1179656 | tf_op jit(solution)/shard_map/ppermute | solution.py:17
  71.4 15.7 %collective-permute-start.19 = (bf16[48,4096]{1,0:T(8,128)(2,1)S(1)}, bf16[48,4096]{1,0:T(8,128)(2,1)S(1)}, u32[]{:S(2)}, u32[]{:S(2)}) collective-permute-start(bf16[48,4096]{1,0:T(8,128)(2,1)S(1)} %attend_1.1.refs_0_), channel_id=1, source_target_pairs={{0,2},{1,3},{2,0},{3,1},{4,6},{5,7},{6,4},{7,5},{8,10},{9,11},{10,... | collective-permute-start | bytes 1179656 | tf_op jit(solution)/shard_map/ppermute | solution.py:17
  73.1 14.3 %collective-permute-start.17 = (bf16[192,768]{1,0:T(8,128)(2,1)S(1)}, bf16[192,768]{1,0:T(8,128)(2,1)S(1)}, u32[]{:S(2)}, u32[]{:S(2)}) collective-permute-start(bf16[192,768]{1,0:T(8,128)(2,1)S(1)} %project_3_0.1), channel_id=1, source_target_pairs={{0,4},{4,0},{8,12},{12,8},{1,5},{5,1},{9,13},{13,9},{2,6},{6,2},{1... | collective-permute-start | bytes 884744 | tf_op jit(solution)/shard_map/ppermute | solution.py:17
  75.1 16.5 %collective-permute-start.18 = (bf16[48,4096]{1,0:T(8,128)(2,1)S(1)}, bf16[48,4096]{1,0:T(8,128)(2,1)S(1)}, u32[]{:S(2)}, u32[]{:S(2)}) collective-permute-start(bf16[48,4096]{1,0:T(8,128)(2,1)S(1)} %attend_1.1.refs_0_), channel_id=1, source_target_pairs={{0,1},{1,0},{2,3},{3,2},{4,5},{5,4},{6,7},{7,6},{8,9},{9,8},{10,11... | collective-permute-start | bytes 1179656 | tf_op jit(solution)/shard_map/ppermute | solution.py:17
  80.0 11.6 %collective-permute-start.22 = (bf16[48,4096]{1,0:T(8,128)(2,1)S(1)}, bf16[48,4096]{1,0:T(8,128)(2,1)S(1)}, u32[]{:S(2)}, u32[]{:S(2)}) collective-permute-start(bf16[48,4096]{1,0:T(8,128)(2,1)S(1)} %attend_0.1.refs_0_), channel_id=1, source_target_pairs={{0,2},{1,3},{2,0},{3,1},{4,6},{5,7},{6,4},{7,5},{8,10},{9,11},{10,... | collective-permute-start | bytes 1179656 | tf_op jit(solution)/shard_map/ppermute | solution.py:17
  81.3 27.3 %collective-permute-start.21 = (bf16[48,4096]{1,0:T(8,128)(2,1)S(1)}, bf16[48,4096]{1,0:T(8,128)(2,1)S(1)}, u32[]{:S(2)}, u32[]{:S(2)}) collective-permute-start(bf16[48,4096]{1,0:T(8,128)(2,1)S(1)} %attend_0.1.refs_0_), channel_id=1, source_target_pairs={{0,1},{1,0},{2,3},{3,2},{4,5},{5,4},{6,7},{7,6},{8,9},{9,8},{10,11... | collective-permute-start | bytes 1179656 | tf_op jit(solution)/shard_map/ppermute | solution.py:17
  87.0 4.6 %collective-permute-start.20 = (bf16[48,4096]{1,0:T(8,128)(2,1)S(1)}, bf16[48,4096]{1,0:T(8,128)(2,1)S(1)}, u32[]{:S(2)}, u32[]{:S(2)}) collective-permute-start(bf16[48,4096]{1,0:T(8,128)(2,1)S(1)} %collective-permute-done.19.refs_2_), channel_id=1, source_target_pairs={{0,1},{1,0},{2,3},{3,2},{4,5},{5,4},{6,7},{7,6},{8,9},{9,8},{10,11... | collective-permute-start | bytes 1179656 | tf_op jit(solution)/shard_map/ppermute | solution.py:17
  87.5 21.1 %collective-permute-start.16 = (bf16[192,1024]{1,0:T(8,128)(2,1)S(1)}, bf16[192,1024]{1,0:T(8,128)(2,1)S(1)}, u32[]{:S(2)}, u32[]{:S(2)}) collective-permute-start(bf16[192,1024]{1,0:T(8,128)(2,1)S(1)} %add_convert_fusion.1), channel_id=1, source_target_pairs={{0,8},{4,12},{8,0},{12,4},{1,9},{5,13},{9,1},{13,5},{2,10},{6,14},... | collective-permute-start | bytes 1179656 | tf_op jit(solution)/shard_map/ppermute | solution.py:17
  91.6 17.0 %collective-permute-start.23 = (bf16[48,4096]{1,0:T(8,128)(2,1)S(1)}, bf16[48,4096]{1,0:T(8,128)(2,1)S(1)}, u32[]{:S(2)}, u32[]{:S(2)}) collective-permute-start(bf16[48,4096]{1,0:T(8,128)(2,1)S(1)} %collective-permute-done.22.refs_2_), channel_id=1, source_target_pairs={{0,1},{1,0},{2,3},{3,2},{4,5},{5,4},{6,7},{7,6},{8,9},{9,8},{10,11... | collective-permute-start | bytes 1179656 | tf_op jit(solution)/shard_map/ppermute | solution.py:17
  94.7 26.6 %collective-permute-start.25 = (bf16[192,1024]{1,0:T(8,128)(2,1)S(1)}, bf16[192,1024]{1,0:T(8,128)(2,1)S(1)}, u32[]{:S(2)}, u32[]{:S(2)}) collective-permute-start(bf16[192,1024]{1,0:T(8,128)(2,1)S(1)} %project_1_768.1), channel_id=1, source_target_pairs={{0,4},{4,0},{8,12},{12,8},{1,5},{5,1},{9,13},{13,9},{2,6},{6,2},{1... | collective-permute-start | bytes 1179656 | tf_op jit(solution)/shard_map/ppermute | solution.py:17
  96.3 32.3 %collective-permute-start.29 = (bf16[192,768]{1,0:T(8,128)(2,1)S(1)}, bf16[192,768]{1,0:T(8,128)(2,1)S(1)}, u32[]{:S(2)}, u32[]{:S(2)}) collective-permute-start(bf16[192,768]{1,0:T(8,128)(2,1)S(1)} %add_convert_fusion.3), channel_id=1, source_target_pairs={{0,8},{4,12},{8,0},{12,4},{1,9},{5,13},{9,1},{13,5},{2,10},{6,14},... | collective-permute-start | bytes 884744 | tf_op jit(solution)/shard_map/ppermute | solution.py:17
  108.6 18.7 %collective-permute-start.24 = (bf16[192,768]{1,0:T(8,128)(2,1)S(1)}, bf16[192,768]{1,0:T(8,128)(2,1)S(1)}, u32[]{:S(2)}, u32[]{:S(2)}) collective-permute-start(bf16[192,768]{1,0:T(8,128)(2,1)S(1)} %project_1_0.1), channel_id=1, source_target_pairs={{0,4},{4,0},{8,12},{12,8},{1,5},{5,1},{9,13},{13,9},{2,6},{6,2},{1... | collective-permute-start | bytes 884744 | tf_op jit(solution)/shard_map/ppermute | solution.py:17
  121.6 5.7 %collective-permute-start.26 = (bf16[48,1024]{1,0:T(8,128)(2,1)S(1)}, bf16[48,1024]{1,0:T(8,128)(2,1)S(1)}, u32[]{:S(2)}, u32[]{:S(2)}) collective-permute-start(bf16[48,1024]{1,0:T(8,128)(2,1)S(1)} %get-tuple-element.55), channel_id=1, source_target_pairs={{0,1},{1,0},{2,3},{3,2},{4,5},{5,4},{6,7},{7,6},{8,9},{9,8},{10,11... | collective-permute-start | bytes 294920 | tf_op jit(solution)/shard_map/ppermute | solution.py:17
  121.7 5.7 %collective-permute-start.27 = (bf16[48,1024]{1,0:T(8,128)(2,1)S(1)}, bf16[48,1024]{1,0:T(8,128)(2,1)S(1)}, u32[]{:S(2)}, u32[]{:S(2)}) collective-permute-start(bf16[48,1024]{1,0:T(8,128)(2,1)S(1)} %get-tuple-element.54), channel_id=1, source_target_pairs={{0,2},{1,3},{2,0},{3,1},{4,6},{5,7},{6,4},{7,5},{8,10},{9,11},{10,... | collective-permute-start | bytes 294920 | tf_op jit(solution)/shard_map/ppermute | solution.py:17
  122.3 6.2 %collective-permute-start.28 = (bf16[48,1024]{1,0:T(8,128)(2,1)S(1)}, bf16[48,1024]{1,0:T(8,128)(2,1)S(1)}, u32[]{:S(2)}, u32[]{:S(2)}) collective-permute-start(bf16[48,1024]{1,0:T(8,128)(2,1)S(1)} %get-tuple-element.53), channel_id=1, source_target_pairs={{0,3},{1,2},{2,1},{3,0},{4,7},{5,6},{6,5},{7,4},{8,11},{9,10},{10,... | collective-permute-start | bytes 294920 | tf_op jit(solution)/shard_map/ppermute | solution.py:17
  129.0 5.1 %collective-permute-start.31 = (bf16[48,768]{1,0:T(8,128)(2,1)S(1)}, bf16[48,768]{1,0:T(8,128)(2,1)S(1)}, u32[]{:S(2)}, u32[]{:S(2)}) collective-permute-start(bf16[48,768]{1,0:T(8,128)(2,1)S(1)} %get-tuple-element.57), channel_id=1, source_target_pairs={{0,2},{1,3},{2,0},{3,1},{4,6},{5,7},{6,4},{7,5},{8,10},{9,11},{10,... | collective-permute-start | bytes 221192 | tf_op jit(solution)/shard_map/ppermute | solution.py:17
  129.5 4.7 %collective-permute-start.32 = (bf16[48,768]{1,0:T(8,128)(2,1)S(1)}, bf16[48,768]{1,0:T(8,128)(2,1)S(1)}, u32[]{:S(2)}, u32[]{:S(2)}) collective-permute-start(bf16[48,768]{1,0:T(8,128)(2,1)S(1)} %get-tuple-element.56), channel_id=1, source_target_pairs={{0,3},{1,2},{2,1},{3,0},{4,7},{5,6},{6,5},{7,4},{8,11},{9,10},{10,... | collective-permute-start | bytes 221192 | tf_op jit(solution)/shard_map/ppermute | solution.py:17
  (16 other events, 144.2 us)

commit v5 on v4

--- a/solution.py
+++ b/solution.py
@@ -9,6 +9,13 @@
 from jax.sharding import PartitionSpec as P
 
 MIB = 1 << 20
+CFG = {'cost': 0.0, 'near': 'three', 'c': [3], 'b': [3], 'a': [3], 't': [3], 'h': [[4], [4], [4], [4]], 'arr': 3, 'p3r2': 1, 'p3n': 1, 'own3': 1, 't3r2': 1, 'cn': 1, 'cx2': 0, 'r0': 'post', 'core1': 'sums', 'own1': 0, 't1': 'sums', 'core0': 'first', 'own0': 1, 'hand': 'end', 't0': 'none', 'tail': [0, 1], 'tie': 1}
+
+
+def cost(us):
+    return pl.CostEstimate(
+        flops=int(us * CFG["cost"] * 1.15e9) + 1, bytes_accessed=1, transcendentals=0
+    )
 
 
 def swap(value, axis, distance, inner=1):
@@ -21,26 +28,38 @@
     return lax.optimization_barrier((value, *others))[0]
 
 
-def gather_ranks(value, axis, *earlier):
-    size = lax.axis_size(axis)
+def cross(values, axis):
+    return [cross_one(value, axis) for value in values]
+
+
+def spread(crossed, axis, *earlier, own=()):
+    return [piece for pieces in crossed for piece in spread_one(pieces, axis, earlier, own)]
+
+
+def cross_one(value, axis):
     pieces = {0: value}
-    distance = size // 2
-    while distance:
+    distance = lax.axis_size(axis) // 2
+    while distance > 1:
         for k in list(pieces):
-            passed = after(pieces[k], *earlier) if k and earlier else pieces[k]
-            pieces[k ^ distance] = swap(passed, axis, distance)
+            pieces[k ^ distance] = swap(pieces[k], axis, distance)
         distance //= 2
-    return [pieces[k] for k in range(size)]
+    return pieces
+
+
+def spread_one(pieces, axis, earlier, own):
+    gates = {k: earlier if k else own for k in pieces}
+    other = {k ^ 1: swap(after(v, *gates[k]), axis, 1) for k, v in pieces.items()}
+    every = {**pieces, **other}
+    return [every[k] for k in range(len(every))]
 
 
 def part_of(size, wanted, unit=1):
     return max(d for d in range(unit, max(wanted, unit) + 1, unit) if size % d == 0)
 
 
-def split_columns(width):
-    unit = 256 if width % 256 == 0 else 128
-    first = width // unit // 2 * unit
-    return [(0, first), (first, width - first)] if width % 256 == 0 and first else [(0, width)]
+def split_at(width, *places):
+    edges = [0, *places, width]
+    return [(a, b - a) for a, b in zip(edges, edges[1:]) if b > a]
 
 
 def absorb_kernel(nope_ref, rope_ref, key_ref, out_ref):
@@ -72,7 +91,7 @@
         out_specs=pl.BlockSpec((step, rows, latent + rotary), lambda h: (h, 0, 0)),
         out_shape=jax.ShapeDtypeStruct((heads, rows, latent + rotary), q_nope.dtype),
         compiler_params=pltpu.CompilerParams(vmem_limit_bytes=8 * MIB),
-        cost_estimate=pl.CostEstimate(flops=1, bytes_accessed=1, transcendentals=0),
+        cost_estimate=cost(3),
         name="absorb",
     )(q_nope, q_rope, w_key)
 
@@ -80,8 +99,9 @@
 def attend_kernel(
     distance, scale, ids_ref, prefix_ref, stretch_ref, query_ref, *refs
 ):
-    block_refs, (value_ref, out_ref, keys, hidden) = refs[:4], refs[4:]
+    block_refs, value_ref, out_refs, (keys, hidden) = refs[:4], refs[4], refs[5:-2], refs[-2:]
     heads, stretch, width = query_ref.shape
+    each = pl.num_programs(0) // len(out_refs)
     latent, value_width = value_ref.shape[1:]
     part = block_refs[0].shape[2]
     span = 4 * part
@@ -110,24 +130,36 @@
     )
     latent_out = (latent_out / denom).astype(jnp.bfloat16)
     live = lax.broadcasted_iota(jnp.int32, (stretch, value_width), 0) < stretch_ref[request]
+    head_outs = []
     for h in range(heads):
         head_out = jnp.dot(
             latent_out[h * stretch : (h + 1) * stretch],
             value_ref[h],
             preferred_element_type=jnp.float32,
         )
-        out_ref[:, h * value_width : (h + 1) * value_width] = jnp.where(
-            live, head_out, 0.0
-        ).astype(out_ref.dtype)
-
-
-def attend(distance, ids, prefix_len, stretch_len, full_query, blocks, w_value, scale):
+        head_outs.append(jnp.where(live, head_out, 0.0).astype(out_refs[0].dtype))
+    for part, out_ref in enumerate(out_refs):
+
+        @pl.when(pl.program_id(0) // each == part)
+        def _(out_ref=out_ref):
+            for h in range(heads):
+                out_ref[:, h * value_width : (h + 1) * value_width] = head_outs[h]
+
+
+def attend(
+    distance, ids, prefix_len, stretch_len, full_query, blocks, w_value, scale, halves
+):
     heads, rows, width = full_query.shape
     latent, value_width = w_value.shape[1:]
     stretch = rows // prefix_len.shape[0]
     part = blocks[0].shape[2]
-    step = part_of(heads, 8)
+    step = part_of(heads // halves, 8)
+    each = heads // halves // step
     span = 4 * part
+
+    def half_of(half):
+        return lambda h, *_: (0, jnp.clip(h - half * each, 0, each - 1))
+
     return pl.pallas_call(
         functools.partial(attend_kernel, distance, scale),
         grid_spec=pltpu.PrefetchScalarGridSpec(
@@ -138,47 +170,66 @@
             ]
             + [pl.BlockSpec((1, width, part), lambda h, p, *_: ((p[0] ^ distance) % 2, 0, 0))] * 4
             + [pl.BlockSpec((step, latent, value_width), lambda h, *_: (h, 0, 0))],
-            out_specs=pl.BlockSpec((stretch, step * value_width), lambda h, *_: (0, h)),
+            out_specs=[
+                pl.BlockSpec((stretch, step * value_width), half_of(half)) for half in range(halves)
+            ],
             scratch_shapes=[
                 pltpu.VMEM((width, span), jnp.bfloat16),
                 pltpu.VMEM((stretch, span), jnp.float32),
             ],
         ),
-        out_shape=jax.ShapeDtypeStruct((stretch, heads * value_width), jnp.bfloat16),
+        out_shape=[jax.ShapeDtypeStruct((stretch, heads // halves * value_width), jnp.bfloat16)]
+        * halves,
         compiler_params=pltpu.CompilerParams(vmem_limit_bytes=10 * MIB * max(span // 512, 1)),
-        cost_estimate=pl.CostEstimate(flops=1, bytes_accessed=1, transcendentals=0),
+        cost_estimate=cost(5),
         name=f"attend_{distance}",
     )(ids, prefix_len, stretch_len, full_query, *blocks, w_value)
 
 
-def project_kernel(rank_count, *refs):
-    row_refs, (weight_ref, out_ref, rows) = refs[:rank_count], refs[rank_count:]
-    stretch = row_refs[0].shape[0]
-
-    @pl.when(pl.program_id(0) == 0)
+def project_kernel(stretch, splits, *refs):
+    out_refs = refs[-1 - len(splits) : -1]
+    weight_ref, rows = refs[-2 - len(splits)], refs[-1]
+    row_refs = refs[: -2 - len(splits)]
+    step = weight_ref.shape[1]
+    n = pl.program_id(0)
+
+    @pl.when(n == 0)
     def _():
-        for k, ref in enumerate(row_refs):
-            rows[k * stretch : (k + 1) * stretch] = ref[...]
+        start = 0
+        for ref in row_refs:
+            line, column = start % rows.shape[0], start // rows.shape[0] * ref.shape[1]
+            rows[line : line + stretch, column : column + ref.shape[1]] = ref[...]
+            start += stretch
 
     total = jnp.dot(rows[...], weight_ref[...], preferred_element_type=jnp.float32)
-    out_ref[...] = total.astype(out_ref.dtype)
-
-
-def project(pieces, w_out, start, columns, dtype, name):
-    stretch, depth = pieces[0].shape
-    rows = stretch * len(pieces)
-    step = part_of(math.gcd(start, columns), 256, 128)
-    first = start // step
-    return pl.pallas_call(
-        functools.partial(project_kernel, len(pieces)),
-        grid=(columns // step,),
-        in_specs=[pl.BlockSpec((stretch, depth), lambda n: (0, 0))] * len(pieces)
-        + [pl.BlockSpec((depth, step), lambda n: (0, first + n))],
-        out_specs=pl.BlockSpec((rows, step), lambda n: (0, n)),
-        out_shape=jax.ShapeDtypeStruct((rows, columns), dtype),
+    for (start, columns), out_ref in zip(splits, out_refs):
+
+        @pl.when((n * step >= start) & (n * step < start + columns))
+        def _(out_ref=out_ref):
+            out_ref[...] = total.astype(out_ref.dtype)
+
+
+def project(pieces, w_out, splits, dtype, name):
+    stretch = pieces[0].shape[0]
+    depth, width = w_out.shape
+    rows = stretch * sum(piece.shape[1] for piece in pieces) // depth
+    step = functools.reduce(math.gcd, [columns for _, columns in splits])
+    step = part_of(step, 256, 128)
+
+    def block_of(start, columns):
+        last = columns // step - 1
+        return lambda n: (0, jnp.clip(n - start // step, 0, last))
+
+    return pl.pallas_call(
+        functools.partial(project_kernel, stretch, splits),
+        grid=(width // step,),
+        in_specs=[pl.BlockSpec(piece.shape, lambda n: (0, 0)) for piece in pieces]
+        + [pl.BlockSpec((depth, step), lambda n: (0, n))],
+        out_specs=[pl.BlockSpec((rows, step), block_of(*split)) for split in splits],
+        out_shape=[jax.ShapeDtypeStruct((rows, columns), dtype) for _, columns in splits],
         scratch_shapes=[pltpu.VMEM((rows, depth), jnp.bfloat16)],
         compiler_params=pltpu.CompilerParams(vmem_limit_bytes=14 * MIB),
-        cost_estimate=pl.CostEstimate(flops=1, bytes_accessed=1, transcendentals=0),
+        cost_estimate=cost(5.5),
         name=name,
     )(*pieces, w_out)
 
@@ -294,11 +345,14 @@
     arrived = [outgoing[0]] + [
         swap(after(outgoing[k], full_query), "request", k) for k in range(1, rank_count)
     ]
-    far_three = swap(after(far_two, full_query), "tensor", 1, inner)
-    near_two = swap(after(far_keys, far_three), "tensor", 2, inner)
-    near_one = swap(after(near_keys, far_three), "tensor", 1, inner)
+    far_three = swap(after(far_two, far_one, full_query), "tensor", 1, inner)
+    near_gate = [far_three] if CFG["near"] == "three" else [far_two, far_one]
+    near_two = swap(after(far_keys, *near_gate), "tensor", 2, inner)
+    near_one = swap(after(near_keys, *near_gate), "tensor", 1, inner)
     far_blocks = [far_keys, far_one, far_two, far_three]
     near_blocks = [near_keys, near_one, near_two]
+
+    halves = 2 if head_count % 2 == 0 else 1
 
     def rows_of(distance, blocks, *earlier):
         return attend(
@@ -310,43 +364,66 @@
             blocks,
             w_value,
             score_scale,
+            halves,
         )
 
-    splits = split_columns(w_out.shape[1])
-    parts = len(splits)
+    width = w_out.shape[1]
+    split = {k: split_at(width, *[256 * p for p in CFG[k]]) if width == 1792 else [(0, width)] for k in "cbat"}
+    heads = [split_at(head_count, *[head_count * p // 8 for p in CFG["h"][k]]) for k in range(4)]
     sent = jnp.bfloat16
 
-    def terms_of(distance, pieces, dtype, *earlier):
+    def regroup(arrays, splits):
+        if [x.shape[1] for x in arrays] == [size for _, size in splits]:
+            return arrays
+        whole = jnp.concatenate(arrays, axis=1) if len(arrays) > 1 else arrays[0]
+        return [whole[:, start : start + size] for start, size in splits]
+
+    def terms_of(distance, pieces, dtype, splits, *earlier):
         pieces = [after(pieces[0], *earlier)] + pieces[1:]
-        return [
-            project(pieces, w_out, start, columns, dtype, f"project_{distance}_{start}")
-            for start, columns in splits
-        ]
-
-    rows_3 = rows_of(3, far_blocks, *arrived)
-    rows_2 = rows_of(2, far_blocks, rows_3)
-    pieces_3 = gather_ranks(rows_3, "request", rows_2, near_one, near_two)
-    terms_3 = terms_of(3, pieces_3, sent, rows_2)
-    opposite = [swap(t, "tensor", 1, inner) for t in terms_3]
+        return project(pieces, w_out, splits, dtype, f"project_{distance}")
+
+    rows_3 = rows_of(3, far_blocks, heads[3], *(arrived if CFG["arr"] == 3 else []))
+    cross_3 = cross(rows_3, "request")
+    rows_2 = rows_of(2, far_blocks, heads[2], *rows_3, *(arrived if CFG["arr"] == 2 else []))
+    cross_2 = cross(rows_2, "request")
+    crossed_2 = [piece for pieces in cross_2 for k, piece in pieces.items() if k]
+    gate = [*(rows_2 if CFG["p3r2"] else []), *([near_one, near_two] if CFG["p3n"] else [])]
+    pieces_3 = spread(cross_3, "request", *gate, own=rows_2 if CFG["own3"] else ())
+    terms_3 = terms_of(3, pieces_3, sent, split["c"], *(rows_2 if CFG["t3r2"] else []))
     near_blocks.append(swap(near_two, "tensor", 1, inner))
-    rows_1 = rows_of(1, near_blocks, *terms_3)
-    handed = place_blocks(after(ids, rows_1), arrived)
-    rows_0 = rows_of(0, near_blocks, rows_1, handed, opposite[-1])
-    pieces_2 = gather_ranks(rows_2, "request")
-    terms_2 = terms_of(2, pieces_2, jnp.float32, rows_0)
-    sums = [(t + o).astype(sent) for t, o in zip(terms_2, opposite)]
+    gate = [*([near_blocks[3]] if CFG["cn"] else []), *(crossed_2 if CFG["cx2"] else [])]
+    opposite = [swap(after(t, *gate), "tensor", 1, inner) for t in terms_3]
+    rows_1 = rows_of(1, near_blocks, heads[1], *terms_3)
+    cross_1 = cross(rows_1, "request")
+    if CFG["r0"] != "post":
+        rows_0 = rows_of(0, near_blocks, heads[0], *rows_1)
+    pieces_2 = spread(cross_2, "request")
+    terms_2 = terms_of(2, pieces_2, jnp.float32, split["b"], *(rows_0 if CFG["r0"] == "pre" else rows_1))
+    sums = [(t + o).astype(sent) for t, o in zip(terms_2, regroup(opposite, split["b"]))]
     across = [swap(t, "tensor", 2, inner) for t in sums]
-    pieces_1 = gather_ranks(rows_1, "request")
-    terms_1 = terms_of(1, pieces_1, sent, *sums)
+    if CFG["r0"] == "post":
+        rows_0 = rows_of(0, near_blocks, heads[0], *sums)
+    cross_0 = cross(rows_0, "request")
+    gates = {"none": [], "sums": sums, "first": across[:1], "last": across[-1:]}
+    pieces_1 = spread(cross_1, "request", *gates[CFG["core1"]], own=sums if CFG["own1"] else ())
+    terms_1 = terms_of(1, pieces_1, sent, split["a"], *(sums if CFG["t1"] == "sums" else rows_0))
     beside = [swap(t, "tensor", 1, inner) for t in terms_1]
-    pieces_0 = gather_ranks(rows_0, "request")
-    terms_0 = terms_of(0, pieces_0, jnp.float32, across[-1], *terms_1)
+    gates["beside"] = beside[:1]
+    pieces_0 = spread(cross_0, "request", *gates[CFG["core0"]], own=rows_0 if CFG["own0"] else ())
+    if CFG["hand"] == "t1":
+        handed = place_blocks(after(ids, *terms_1), arrived)
+    elif CFG["hand"] == "r1":
+        handed = place_blocks(after(ids, *rows_1), arrived)
+    terms_0 = terms_of(0, pieces_0, jnp.float32, split["t"], *([handed] if CFG["hand"] != "end" else []), *gates[CFG["t0"]], *terms_1)
+    if CFG["hand"] == "end":
+        handed = place_blocks(after(ids, *terms_0), arrived)
+    across, beside = regroup(across, split["t"]), regroup(beside, split["t"])
+    parts = len(split["t"])
 
     columns = {}
-    earlier = terms_0
-    for part in reversed(range(parts)):
-        partial = after(terms_0[part] + beside[part], *earlier)
-        summed = (partial + across[part]).astype(sent)
+    earlier = []
+    for part in CFG['tail'] if parts > 1 else [0]:
+        summed = (after(terms_0[part], *(earlier if CFG['tie'] else [])) + beside[part] + across[part]).astype(sent)
         if inner > 1:
             summed = summed.reshape(rank_count, inner, share_rows, summed.shape[1]).swapaxes(0, 1)
             summed = lax.psum_scatter(
@@ -356,7 +433,7 @@
         earlier = [swap(summed[k], "request", k) for k in range(1, rank_count)]
         columns[part] = [summed[0]] + earlier
     ordered = [columns[part][k] for k in range(rank_count) for part in range(parts)]
-    mixed = place_columns(ids, ordered, splits)[None]
+    mixed = place_columns(ids, ordered, split['t'])[None]
     handed = handed.transpose(0, 2, 1)[None]
     return (mixed, handed)
 

time: 136 us -> 123 us (0.904)
  waiting for transfers between devices: 43 us -> 27.8 us
  starting transfers between devices: 33.1 us -> 34.8 us
    ppermute x33 -> x45, waiting for transfers between devices: 43 us -> 27.8 us  [swap(): return lax.ppermute(value, axis, pairs)]
    ppermute x33 -> x45, starting transfers between devices: 33.1 us -> 34.8 us  [swap(): return lax.ppermute(value, axis, pairs)]
    pallas_call x8 -> x4, Pallas kernels: 21.8 us -> 22.2 us  [project(): pl.pallas_call(functools.partial(project_kernel, stretch, splits), grid=(...]
  transfers between devices with their start and end apart: 33 -> 45, of which waited for: 11 -> 12; matrix products, arithmetic and copies ran while one was open for 0% -> 0% of each run, Pallas kernels for 31% -> 39%
where the time goes in v5:
time: 123 us
  Pallas kernels  49.4 us (40%)
  starting transfers between devices  34.8 us (28%)
  waiting for transfers between devices  27.8 us (23%)
  local copies, waits for them, and re-layouts  9.59 us (8%)
    ppermute x45, starting transfers between devices, swap(): return lax.ppermute(value, axis, pairs)  34.8 us
    ppermute x45, waiting for transfers between devices, swap(): return lax.ppermute(value, axis, pairs)  27.8 us
    pallas_call x4, Pallas kernels, project(): pl.pallas_call(functools.partial(project_kernel, stretch, splits), grid=(...  22.2 us
    pallas_call x4, Pallas kernels, attend(): pl.pallas_call(functools.partial(attend_kernel, distance, scale), grid_sp...  20.2 us
    unnamed x30, local copies, waits for them, and re-layouts  8.44 us
    pallas_call x1, Pallas kernels, absorb(): pl.pallas_call(absorb_kernel, grid=(heads // step,), in_specs=[pl.BlockSp...  3.3 us
  transfers between devices with their start and end apart: 45, of which 12 were waited for; matrix products, arithmetic and copies ran while one was open for 0% of the time, Pallas kernels for 39%

profile of v5, /device:TPU:0, one launch (start us, length us, event | category | flops | bytes accessed | tf_op | source)
XLA Modules:
  0.0 123.0 jit_solution(124145255290922981)
XLA Ops:
  1.8 4.1 %collective-permute-start.4 = (bf16[2,576,128]{2,1,0:T(8,128)(2,1)S(1)}, bf16[2,576,128]{2,1,0:T(8,128)(2,1)S(1)}, u32[]{:S(2)}, u32[]{:S(2)}) collective-permute-start(bf16[2,576,128]{2,1,0:T(8,128)(2,1)S(1)} %get-tuple-element.68.refs_0_), channel_id=1, source_target_pairs={{0,8},{4,12},{8,0},{12,4},{1,9},{5,13},{9,1},{13,5},{2,10},{6,14},... | collective-permute-start | bytes 884744 | tf_op jit(solution)/shard_map/ppermute | solution.py:24
  5.9 1.6 %collective-permute-start.3 = (bf16[2,576,128]{2,1,0:T(8,128)(2,1)S(1)}, bf16[2,576,128]{2,1,0:T(8,128)(2,1)S(1)}, u32[]{:S(2)}, u32[]{:S(2)}) collective-permute-start(bf16[2,576,128]{2,1,0:T(8,128)(2,1)S(1)} %get-tuple-element.69.refs_0_), channel_id=1, source_target_pairs={{0,4},{4,0},{8,12},{12,8},{1,5},{5,1},{9,13},{13,9},{2,6},{6,2},{1... | collective-permute-start | bytes 884744 | tf_op jit(solution)/shard_map/ppermute | solution.py:24
  12.1 2.2 %copy-done.1 = bf16[32,512,128]{2,1,0:T(8,128)(2,1)S(1)} copy-done((bf16[32,512,128]{2,1,0:T(8,128)(2,1)S(1)}, bf16[32,512,128]{2,1,0:T(8,128)(2,1)}, u32[]{:S(2)}) %copy-start.1) | copy-done | bytes 4194328
  14.3 1.4 %copy-done.3 = bf16[192,4096]{1,0:T(8,128)(2,1)S(1)} copy-done((bf16[192,4096]{1,0:T(8,128)(2,1)S(1)}, bf16[192,4096]{1,0:T(8,128)(2,1)}, u32[]{:S(2)}) %copy-start.3) | copy-done | bytes 1572888
  16.9 3.3 %absorb.1.query_ref = bf16[32,192,576]{2,1,0:T(8,128)(2,1)S(1)} custom-call(bf16[192,4096]{1,0:T(8,128)(2,1)S(1)} %copy-done.3, bf16[192,2048]{1,0:T(8,128)(2,1)S(1)} %copy-done.4, bf16[32,512,128]{2,1,0:T(8,128)(2,1)S(1)} %copy-done.1), custom_call_target="tpu_custom_call" | custom-call | flops 1 | bytes 1 | tf_op jit(solution)/shard_map/absorb/pallas_call | solution.py:83
  21.0 1.5 %collective-permute-start.1 = (bf16[576,128]{1,0:T(8,128)(2,1)S(1)}, bf16[576,128]{1,0:T(8,128)(2,1)S(1)}, u32[]{:S(2)}, u32[]{:S(2)}) collective-permute-start(bf16[576,128]{1,0:T(8,128)(2,1)S(1)} %get-tuple-element.58), channel_id=1, source_target_pairs={{0,2},{1,3},{2,0},{3,1},{4,6},{5,7},{6,4},{7,5},{8,10},{9,11},{10,... | collective-permute-start | bytes 442376 | tf_op jit(solution)/shard_map/ppermute | solution.py:24
  22.8 5.6 %collective-permute-done.5.refs_3_ = bf16[2,576,128]{2,1,0:T(8,128)(2,1)S(1)} collective-permute-done((bf16[2,576,128]{2,1,0:T(8,128)(2,1)S(1)}, bf16[2,576,128]{2,1,0:T(8,128)(2,1)S(1)}, u32[]{:S(2)}, u32[]{:S(2)}) %collective-permute-start.5) | collective-permute-done | bytes 294944 | tf_op jit(solution)/shard_map/ppermute | solution.py:24
  28.5 2.0 %collective-permute-start.9 = (bf16[2,576,128]{2,1,0:T(8,128)(2,1)S(1)}, bf16[2,576,128]{2,1,0:T(8,128)(2,1)S(1)}, u32[]{:S(2)}, u32[]{:S(2)}) collective-permute-start(bf16[2,576,128]{2,1,0:T(8,128)(2,1)S(1)} %get-tuple-element.69.refs_0_), channel_id=1, source_target_pairs={{0,8},{4,12},{8,0},{12,4},{1,9},{5,13},{9,1},{13,5},{2,10},{6,14},... | collective-permute-start | bytes 884744 | tf_op jit(solution)/shard_map/ppermute | solution.py:24
  30.5 1.7 %collective-permute-start.8 = (bf16[2,576,128]{2,1,0:T(8,128)(2,1)S(1)}, bf16[2,576,128]{2,1,0:T(8,128)(2,1)S(1)}, u32[]{:S(2)}, u32[]{:S(2)}) collective-permute-start(bf16[2,576,128]{2,1,0:T(8,128)(2,1)S(1)} %get-tuple-element.68.refs_0_), channel_id=1, source_target_pairs={{0,4},{4,0},{8,12},{12,8},{1,5},{5,1},{9,13},{13,9},{2,6},{6,2},{1... | collective-permute-start | bytes 884744 | tf_op jit(solution)/shard_map/ppermute | solution.py:24
  32.3 5.0 %attend_3.1 = (bf16[48,2048]{1,0:T(8,128)(2,1)S(1)}, bf16[48,2048]{1,0:T(8,128)(2,1)S(1)}) custom-call(s32[3]{0:T(128)S(1)} %pad_add_fusion.ids_ref, s32[4]{0:T(128)S(1)} %copy-done.6, s32[4]{0:T(128)S(1)} %copy-done.8, bf16[32,192,576]{2,1,0:T(8,128)(2,1)S(1)} %absorb.1.query_ref, bf16[2,576,128]{2,1,0:T(8,128)(2,1)S(1)} %get-tuple-element.69.refs_0_, ...), custom_call_target="tpu_custom_call" | custom-call | flops 1 | bytes 1 | tf_op jit(solution)/shard_map/attend_3/pallas_call | solution.py:163
  37.3 1.6 %collective-permute-start.7 = (bf16[48,2048]{1,0:T(8,128)(2,1)S(1)}, bf16[48,2048]{1,0:T(8,128)(2,1)S(1)}, u32[]{:S(2)}, u32[]{:S(2)}) collective-permute-start(bf16[48,2048]{1,0:T(8,128)(2,1)S(1)} %get-tuple-element.67.refs_0_), channel_id=1, source_target_pairs={{0,2},{1,3},{2,0},{3,1},{4,6},{5,7},{6,4},{7,5},{8,10},{9,11},{10,... | collective-permute-start | bytes 589832 | tf_op jit(solution)/shard_map/ppermute | solution.py:24
  39.4 5.0 %attend_2.1 = (bf16[48,2048]{1,0:T(8,128)(2,1)S(1)}, bf16[48,2048]{1,0:T(8,128)(2,1)S(1)}) custom-call(s32[3]{0:T(128)S(1)} %pad_add_fusion.ids_ref, s32[4]{0:T(128)S(1)} %copy-done.6, s32[4]{0:T(128)S(1)} %copy-done.8, bf16[32,192,576]{2,1,0:T(8,128)(2,1)S(1)} %absorb.1.query_ref, bf16[2,576,128]{2,1,0:T(8,128)(2,1)S(1)} %get-tuple-element.69.refs_0_, ...), custom_call_target="tpu_custom_call" | custom-call | flops 1 | bytes 1 | tf_op jit(solution)/shard_map/attend_2/pallas_call | solution.py:163
  47.0 1.5 %collective-permute-start.16 = (bf16[48,2048]{1,0:T(8,128)(2,1)S(1)}, bf16[48,2048]{1,0:T(8,128)(2,1)S(1)}, u32[]{:S(2)}, u32[]{:S(2)}) collective-permute-start(bf16[48,2048]{1,0:T(8,128)(2,1)S(1)} %get-tuple-element.78.refs_0_), channel_id=1, source_target_pairs={{0,2},{1,3},{2,0},{3,1},{4,6},{5,7},{6,4},{7,5},{8,10},{9,11},{10,... | collective-permute-start | bytes 589832 | tf_op jit(solution)/shard_map/ppermute | solution.py:24
  49.1 5.5 %project_3.1 = (bf16[192,768]{1,0:T(8,128)(2,1)S(1)}, bf16[192,1024]{1,0:T(8,128)(2,1)S(1)}) custom-call(bf16[48,2048]{1,0:T(8,128)(2,1)S(1)} %get-tuple-element.67.refs_0_, bf16[48,2048]{1,0:T(8,128)(2,1)S(1)} %collective-permute-done.6.refs_1_, bf16[48,2048]{1,0:T(8,128)(2,1)S(1)} %collective-permute-done.7.refs_2_, ...), custom_call_target="tpu_custom_call" | custom-call | flops 1 | bytes 1 | tf_op jit(solution)/shard_map/project_3/pallas_call | solution.py:223
  55.9 2.6 %collective-permute-done.19.refs_6_ = bf16[48,2048]{1,0:T(8,128)(2,1)S(1)} collective-permute-done((bf16[48,2048]{1,0:T(8,128)(2,1)S(1)}, bf16[48,2048]{1,0:T(8,128)(2,1)S(1)}, u32[]{:S(2)}, u32[]{:S(2)}) %collective-permute-start.19) | collective-permute-done | bytes 196640 | tf_op jit(solution)/shard_map/ppermute | solution.py:24
  59.2 5.0 %attend_1.1 = (bf16[48,2048]{1,0:T(8,128)(2,1)S(1)}, bf16[48,2048]{1,0:T(8,128)(2,1)S(1)}) custom-call(s32[3]{0:T(128)S(1)} %pad_add_fusion.ids_ref, s32[4]{0:T(128)S(1)} %copy-done.6, s32[4]{0:T(128)S(1)} %copy-done.8, bf16[32,192,576]{2,1,0:T(8,128)(2,1)S(1)} %absorb.1.query_ref, bf16[2,576,128]{2,1,0:T(8,128)(2,1)S(1)} %get-tuple-element.68.refs_0_, ...), custom_call_target="tpu_custom_call" | custom-call | flops 1 | bytes 1 | tf_op jit(solution)/shard_map/attend_1/pallas_call | solution.py:163
  64.3 1.6 %collective-permute-start.24 = (bf16[48,2048]{1,0:T(8,128)(2,1)S(1)}, bf16[48,2048]{1,0:T(8,128)(2,1)S(1)}, u32[]{:S(2)}, u32[]{:S(2)}) collective-permute-start(bf16[48,2048]{1,0:T(8,128)(2,1)S(1)} %get-tuple-element.85.refs_0_), channel_id=1, source_target_pairs={{0,2},{1,3},{2,0},{3,1},{4,6},{5,7},{6,4},{7,5},{8,10},{9,11},{10,... | collective-permute-start | bytes 589832 | tf_op jit(solution)/shard_map/ppermute | solution.py:24
  66.4 5.6 %project_2.1 = (f32[192,768]{1,0:T(8,128)S(1)}, f32[192,1024]{1,0:T(8,128)S(1)}) custom-call(bf16[48,2048]{1,0:T(8,128)(2,1)S(1)} %get-tuple-element.78.refs_0_, bf16[48,2048]{1,0:T(8,128)(2,1)S(1)} %collective-permute-done.15.refs_1_, bf16[48,2048]{1,0:T(8,128)(2,1)S(1)} %collective-permute-done.16.refs_2_, ...), custom_call_target="tpu_custom_call" | custom-call | flops 1 | bytes 1 | tf_op jit(solution)/shard_map/project_2/pallas_call | solution.py:223
  72.7 1.6 %collective-permute-start.31 = (bf16[192,768]{1,0:T(8,128)(2,1)S(1)}, bf16[192,768]{1,0:T(8,128)(2,1)S(1)}, u32[]{:S(2)}, u32[]{:S(2)}) collective-permute-start(bf16[192,768]{1,0:T(8,128)(2,1)S(1)} %add_convert_fusion.3), channel_id=1, source_target_pairs={{0,8},{4,12},{8,0},{12,4},{1,9},{5,13},{9,1},{13,5},{2,10},{6,14},... | collective-permute-start | bytes 884744 | tf_op jit(solution)/shard_map/ppermute | solution.py:24
  76.1 5.0 %attend_0.1 = (bf16[48,2048]{1,0:T(8,128)(2,1)S(1)}, bf16[48,2048]{1,0:T(8,128)(2,1)S(1)}) custom-call(s32[3]{0:T(128)S(1)} %pad_add_fusion.ids_ref, s32[4]{0:T(128)S(1)} %copy-done.6, s32[4]{0:T(128)S(1)} %copy-done.8, bf16[32,192,576]{2,1,0:T(8,128)(2,1)S(1)} %absorb.1.query_ref, bf16[2,576,128]{2,1,0:T(8,128)(2,1)S(1)} %get-tuple-element.68.refs_0_, ...), custom_call_target="tpu_custom_call" | custom-call | flops 1 | bytes 1 | tf_op jit(solution)/shard_map/attend_0/pallas_call | solution.py:163
  81.2 1.6 %collective-permute-start.30 = (bf16[48,2048]{1,0:T(8,128)(2,1)S(1)}, bf16[48,2048]{1,0:T(8,128)(2,1)S(1)}, u32[]{:S(2)}, u32[]{:S(2)}) collective-permute-start(bf16[48,2048]{1,0:T(8,128)(2,1)S(1)} %get-tuple-element.92.refs_0_), channel_id=1, source_target_pairs={{0,2},{1,3},{2,0},{3,1},{4,6},{5,7},{6,4},{7,5},{8,10},{9,11},{10,... | collective-permute-start | bytes 589832 | tf_op jit(solution)/shard_map/ppermute | solution.py:24
  83.3 5.5 %project_1.1 = (bf16[192,768]{1,0:T(8,128)(2,1)S(1)}, bf16[192,1024]{1,0:T(8,128)(2,1)S(1)}) custom-call(bf16[48,2048]{1,0:T(8,128)(2,1)S(1)} %get-tuple-element.85.refs_0_, bf16[48,2048]{1,0:T(8,128)(2,1)S(1)} %collective-permute-done.23.refs_1_, bf16[48,2048]{1,0:T(8,128)(2,1)S(1)} %collective-permute-done.24.refs_2_, ...), custom_call_target="tpu_custom_call" | custom-call | flops 1 | bytes 1 | tf_op jit(solution)/shard_map/project_1/pallas_call | solution.py:223
  90.8 1.5 %collective-permute-done.34.refs_6_ = bf16[48,2048]{1,0:T(8,128)(2,1)S(1)} collective-permute-done((bf16[48,2048]{1,0:T(8,128)(2,1)S(1)}, bf16[48,2048]{1,0:T(8,128)(2,1)S(1)}, u32[]{:S(2)}, u32[]{:S(2)}) %collective-permute-start.34) | collective-permute-done | bytes 196640 | tf_op jit(solution)/shard_map/ppermute | solution.py:24
  93.6 1.8 %collective-permute-start.40 = (bf16[192,1024]{1,0:T(8,128)(2,1)S(1)}, bf16[192,1024]{1,0:T(8,128)(2,1)S(1)}, u32[]{:S(2)}, u32[]{:S(2)}) collective-permute-start(bf16[192,1024]{1,0:T(8,128)(2,1)S(1)} %get-tuple-element.89), channel_id=1, source_target_pairs={{0,4},{4,0},{8,12},{12,8},{1,5},{5,1},{9,13},{13,9},{2,6},{6,2},{1... | collective-permute-start | bytes 1179656 | tf_op jit(solution)/shard_map/ppermute | solution.py:24
  95.3 5.6 %project_0.1 = (f32[192,768]{1,0:T(8,128)S(1)}, f32[192,1024]{1,0:T(8,128)S(1)}) custom-call(bf16[48,2048]{1,0:T(8,128)(2,1)S(1)} %get-tuple-element.92.refs_0_, bf16[48,2048]{1,0:T(8,128)(2,1)S(1)} %collective-permute-done.29.refs_1_, bf16[48,2048]{1,0:T(8,128)(2,1)S(1)} %collective-permute-done.30.refs_2_, ...), custom_call_target="tpu_custom_call" | custom-call | flops 1 | bytes 1 | tf_op jit(solution)/shard_map/project_0/pallas_call | solution.py:223
  103.0 2.6 %collective-permute-done.39.refs_6_ = bf16[48,768]{1,0:T(8,128)(2,1)S(1)} collective-permute-done((bf16[48,768]{1,0:T(8,128)(2,1)S(1)}, bf16[48,768]{1,0:T(8,128)(2,1)S(1)}, u32[]{:S(2)}, u32[]{:S(2)}) %collective-permute-start.39) | collective-permute-done | bytes 73760 | tf_op jit(solution)/shard_map/ppermute | solution.py:24
  105.6 1.7 %collective-permute-done.38.refs_4_ = bf16[48,768]{1,0:T(8,128)(2,1)S(1)} collective-permute-done((bf16[48,768]{1,0:T(8,128)(2,1)S(1)}, bf16[48,768]{1,0:T(8,128)(2,1)S(1)}, u32[]{:S(2)}, u32[]{:S(2)}) %collective-permute-start.38) | collective-permute-done | bytes 73760 | tf_op jit(solution)/shard_map/ppermute | solution.py:24
  107.3 6.0 %collective-permute-done.41 = bf16[192,1024]{1,0:T(8,128)(2,1)S(1)} collective-permute-done((bf16[192,1024]{1,0:T(8,128)(2,1)S(1)}, bf16[192,1024]{1,0:T(8,128)(2,1)S(1)}, u32[]{:S(2)}, u32[]{:S(2)}) %collective-permute-start.41) | collective-permute-done | bytes 393248 | tf_op jit(solution)/shard_map/ppermute | solution.py:24
  116.2 1.4 %place_blocks.1 = bf16[4,576,128]{2,1,0:T(8,128)(2,1)} custom-call(s32[3]{0:T(128)S(1)} %pad_add_fusion.ids_ref, bf16[576,128]{1,0:T(8,128)(2,1)S(1)} %get-tuple-element.52.refs_0_, bf16[576,128]{1,0:T(8,128)(2,1)S(1)} %collective-permute-done.refs_1_, bf16[576,128]{1,0:T(8,128)(2,1)S(1)} %collective-permute-done.1.refs_2_, ...), custom_call_target="tpu_custom_call" | custom-call | tf_op jit(solution)/shard_map/place_blocks/pallas_call | solution.py:271
  117.6 1.8 %collective-permute-done.44.refs_7_ = bf16[48,1024]{1,0:T(8,128)(2,1)S(1)} collective-permute-done((bf16[48,1024]{1,0:T(8,128)(2,1)S(1)}, bf16[48,1024]{1,0:T(8,128)(2,1)S(1)}, u32[]{:S(2)}, u32[]{:S(2)}) %collective-permute-start.44) | collective-permute-done | bytes 98336 | tf_op jit(solution)/shard_map/ppermute | solution.py:24
  119.4 2.1 %collective-permute-done.43.refs_5_ = bf16[48,1024]{1,0:T(8,128)(2,1)S(1)} collective-permute-done((bf16[48,1024]{1,0:T(8,128)(2,1)S(1)}, bf16[48,1024]{1,0:T(8,128)(2,1)S(1)}, u32[]{:S(2)}, u32[]{:S(2)}) %collective-permute-start.43) | collective-permute-done | bytes 98336 | tf_op jit(solution)/shard_map/ppermute | solution.py:24
  121.6 1.4 %place_columns.1 = bf16[48,7168]{1,0:T(8,128)(2,1)} custom-call(s32[3]{0:T(128)S(1)} %pad_add_fusion.ids_ref, bf16[48,768]{1,0:T(8,128)(2,1)S(1)} %get-tuple-element.109.refs_0_, bf16[48,1024]{1,0:T(8,128)(2,1)S(1)} %get-tuple-element.105.refs_1_, bf16[48,768]{1,0:T(8,128)(2,1)S(1)} %collective-permute-done.37.refs_2_, ...), custom_call_target="tpu_custom_call" | custom-call | tf_op jit(solution)/shard_map/place_columns/pallas_call | solution.py:294
  (109 shorter events, 25.5 us)
Async XLA Ops:
  1.8 18.4 %collective-permute-start.4 = (bf16[2,576,128]{2,1,0:T(8,128)(2,1)S(1)}, bf16[2,576,128]{2,1,0:T(8,128)(2,1)S(1)}, u32[]{:S(2)}, u32[]{:S(2)}) collective-permute-start(bf16[2,576,128]{2,1,0:T(8,128)(2,1)S(1)} %get-tuple-element.68.refs_0_), channel_id=1, source_target_pairs={{0,8},{4,12},{8,0},{12,4},{1,9},{5,13},{9,1},{13,5},{2,10},{6,14},... | collective-permute-start | bytes 884744 | tf_op jit(solution)/shard_map/ppermute | solution.py:24
  5.9 14.3 %collective-permute-start.3 = (bf16[2,576,128]{2,1,0:T(8,128)(2,1)S(1)}, bf16[2,576,128]{2,1,0:T(8,128)(2,1)S(1)}, u32[]{:S(2)}, u32[]{:S(2)}) collective-permute-start(bf16[2,576,128]{2,1,0:T(8,128)(2,1)S(1)} %get-tuple-element.69.refs_0_), channel_id=1, source_target_pairs={{0,4},{4,0},{8,12},{12,8},{1,5},{5,1},{9,13},{13,9},{2,6},{6,2},{1... | collective-permute-start | bytes 884744 | tf_op jit(solution)/shard_map/ppermute | solution.py:24
  20.2 8.3 %collective-permute-start.5 = (bf16[2,576,128]{2,1,0:T(8,128)(2,1)S(1)}, bf16[2,576,128]{2,1,0:T(8,128)(2,1)S(1)}, u32[]{:S(2)}, u32[]{:S(2)}) collective-permute-start(bf16[2,576,128]{2,1,0:T(8,128)(2,1)S(1)} %collective-permute-done.4.refs_2_), channel_id=1, source_target_pairs={{0,4},{4,0},{8,12},{12,8},{1,5},{5,1},{9,13},{13,9},{2,6},{6,2},{1... | collective-permute-start | bytes 884744 | tf_op jit(solution)/shard_map/ppermute | solution.py:24
  21.0 11.3 %collective-permute-start = (bf16[576,128]{1,0:T(8,128)(2,1)S(1)}, bf16[576,128]{1,0:T(8,128)(2,1)S(1)}, u32[]{:S(2)}, u32[]{:S(2)}) collective-permute-start(bf16[576,128]{1,0:T(8,128)(2,1)S(1)} %get-tuple-element.57), channel_id=1, source_target_pairs={{0,1},{1,0},{2,3},{3,2},{4,5},{5,4},{6,7},{7,6},{8,9},{9,8},{10,11... | collective-permute-start | bytes 442376 | tf_op jit(solution)/shard_map/ppermute | solution.py:24
  21.0 11.3 %collective-permute-start.1 = (bf16[576,128]{1,0:T(8,128)(2,1)S(1)}, bf16[576,128]{1,0:T(8,128)(2,1)S(1)}, u32[]{:S(2)}, u32[]{:S(2)}) collective-permute-start(bf16[576,128]{1,0:T(8,128)(2,1)S(1)} %get-tuple-element.58), channel_id=1, source_target_pairs={{0,2},{1,3},{2,0},{3,1},{4,6},{5,7},{6,4},{7,5},{8,10},{9,11},{10,... | collective-permute-start | bytes 442376 | tf_op jit(solution)/shard_map/ppermute | solution.py:24
  22.5 9.8 %collective-permute-start.2 = (bf16[576,128]{1,0:T(8,128)(2,1)S(1)}, bf16[576,128]{1,0:T(8,128)(2,1)S(1)}, u32[]{:S(2)}, u32[]{:S(2)}) collective-permute-start(bf16[576,128]{1,0:T(8,128)(2,1)S(1)} %get-tuple-element.59), channel_id=1, source_target_pairs={{0,3},{1,2},{2,1},{3,0},{4,7},{5,6},{6,5},{7,4},{8,11},{9,10},{10,... | collective-permute-start | bytes 442376 | tf_op jit(solution)/shard_map/ppermute | solution.py:24
  28.5 16.6 %collective-permute-start.9 = (bf16[2,576,128]{2,1,0:T(8,128)(2,1)S(1)}, bf16[2,576,128]{2,1,0:T(8,128)(2,1)S(1)}, u32[]{:S(2)}, u32[]{:S(2)}) collective-permute-start(bf16[2,576,128]{2,1,0:T(8,128)(2,1)S(1)} %get-tuple-element.69.refs_0_), channel_id=1, source_target_pairs={{0,8},{4,12},{8,0},{12,4},{1,9},{5,13},{9,1},{13,5},{2,10},{6,14},... | collective-permute-start | bytes 884744 | tf_op jit(solution)/shard_map/ppermute | solution.py:24
  30.5 15.1 %collective-permute-start.8 = (bf16[2,576,128]{2,1,0:T(8,128)(2,1)S(1)}, bf16[2,576,128]{2,1,0:T(8,128)(2,1)S(1)}, u32[]{:S(2)}, u32[]{:S(2)}) collective-permute-start(bf16[2,576,128]{2,1,0:T(8,128)(2,1)S(1)} %get-tuple-element.68.refs_0_), channel_id=1, source_target_pairs={{0,4},{4,0},{8,12},{12,8},{1,5},{5,1},{9,13},{13,9},{2,6},{6,2},{1... | collective-permute-start | bytes 884744 | tf_op jit(solution)/shard_map/ppermute | solution.py:24
  37.3 7.6 %collective-permute-start.7 = (bf16[48,2048]{1,0:T(8,128)(2,1)S(1)}, bf16[48,2048]{1,0:T(8,128)(2,1)S(1)}, u32[]{:S(2)}, u32[]{:S(2)}) collective-permute-start(bf16[48,2048]{1,0:T(8,128)(2,1)S(1)} %get-tuple-element.67.refs_0_), channel_id=1, source_target_pairs={{0,2},{1,3},{2,0},{3,1},{4,6},{5,7},{6,4},{7,5},{8,10},{9,11},{10,... | collective-permute-start | bytes 589832 | tf_op jit(solution)/shard_map/ppermute | solution.py:24
  38.9 8.1 %collective-permute-start.12 = (bf16[48,2048]{1,0:T(8,128)(2,1)S(1)}, bf16[48,2048]{1,0:T(8,128)(2,1)S(1)}, u32[]{:S(2)}, u32[]{:S(2)}) collective-permute-start(bf16[48,2048]{1,0:T(8,128)(2,1)S(1)} %get-tuple-element.71.refs_4_), channel_id=1, source_target_pairs={{0,2},{1,3},{2,0},{3,1},{4,6},{5,7},{6,4},{7,5},{8,10},{9,11},{10,... | collective-permute-start | bytes 589832 | tf_op jit(solution)/shard_map/ppermute | solution.py:24
  45.0 9.6 %collective-permute-start.14 = (bf16[2,576,128]{2,1,0:T(8,128)(2,1)S(1)}, bf16[2,576,128]{2,1,0:T(8,128)(2,1)S(1)}, u32[]{:S(2)}, u32[]{:S(2)}) collective-permute-start(bf16[2,576,128]{2,1,0:T(8,128)(2,1)S(1)} %collective-permute-done.9.refs_2_), channel_id=1, source_target_pairs={{0,4},{4,0},{8,12},{12,8},{1,5},{5,1},{9,13},{13,9},{2,6},{6,2},{1... | collective-permute-start | bytes 884744 | tf_op jit(solution)/shard_map/ppermute | solution.py:24
  47.0 8.6 %collective-permute-start.16 = (bf16[48,2048]{1,0:T(8,128)(2,1)S(1)}, bf16[48,2048]{1,0:T(8,128)(2,1)S(1)}, u32[]{:S(2)}, u32[]{:S(2)}) collective-permute-start(bf16[48,2048]{1,0:T(8,128)(2,1)S(1)} %get-tuple-element.78.refs_0_), channel_id=1, source_target_pairs={{0,2},{1,3},{2,0},{3,1},{4,6},{5,7},{6,4},{7,5},{8,10},{9,11},{10,... | collective-permute-start | bytes 589832 | tf_op jit(solution)/shard_map/ppermute | solution.py:24
  48.5 10.0 %collective-permute-start.19 = (bf16[48,2048]{1,0:T(8,128)(2,1)S(1)}, bf16[48,2048]{1,0:T(8,128)(2,1)S(1)}, u32[]{:S(2)}, u32[]{:S(2)}) collective-permute-start(bf16[48,2048]{1,0:T(8,128)(2,1)S(1)} %get-tuple-element.66.refs_4_), channel_id=1, source_target_pairs={{0,2},{1,3},{2,0},{3,1},{4,6},{5,7},{6,4},{7,5},{8,10},{9,11},{10,... | collective-permute-start | bytes 589832 | tf_op jit(solution)/shard_map/ppermute | solution.py:24
  49.1 9.5 %collective-permute-start.18 = (bf16[48,2048]{1,0:T(8,128)(2,1)S(1)}, bf16[48,2048]{1,0:T(8,128)(2,1)S(1)}, u32[]{:S(2)}, u32[]{:S(2)}) collective-permute-start(bf16[48,2048]{1,0:T(8,128)(2,1)S(1)} %get-tuple-element.66.refs_4_), channel_id=1, source_target_pairs={{0,1},{1,0},{2,3},{3,2},{4,5},{5,4},{6,7},{7,6},{8,9},{9,8},{10,11... | collective-permute-start | bytes 589832 | tf_op jit(solution)/shard_map/ppermute | solution.py:24
  54.7 17.3 %collective-permute-start.21 = (bf16[192,768]{1,0:T(8,128)(2,1)S(1)}, bf16[192,768]{1,0:T(8,128)(2,1)S(1)}, u32[]{:S(2)}, u32[]{:S(2)}) collective-permute-start(bf16[192,768]{1,0:T(8,128)(2,1)S(1)} %get-tuple-element.80), channel_id=1, source_target_pairs={{0,4},{4,0},{8,12},{12,8},{1,5},{5,1},{9,13},{13,9},{2,6},{6,2},{1... | collective-permute-start | bytes 884744 | tf_op jit(solution)/shard_map/ppermute | solution.py:24
  55.4 8.9 %collective-permute-start.15 = (bf16[48,2048]{1,0:T(8,128)(2,1)S(1)}, bf16[48,2048]{1,0:T(8,128)(2,1)S(1)}, u32[]{:S(2)}, u32[]{:S(2)}) collective-permute-start(bf16[48,2048]{1,0:T(8,128)(2,1)S(1)} %get-tuple-element.78.refs_0_), channel_id=1, source_target_pairs={{0,1},{1,0},{2,3},{3,2},{4,5},{5,4},{6,7},{7,6},{8,9},{9,8},{10,11... | collective-permute-start | bytes 589832 | tf_op jit(solution)/shard_map/ppermute | solution.py:24
  55.6 10.2 %collective-permute-start.17 = (bf16[48,2048]{1,0:T(8,128)(2,1)S(1)}, bf16[48,2048]{1,0:T(8,128)(2,1)S(1)}, u32[]{:S(2)}, u32[]{:S(2)}) collective-permute-start(bf16[48,2048]{1,0:T(8,128)(2,1)S(1)} %collective-permute-done.16.refs_2_), channel_id=1, source_target_pairs={{0,1},{1,0},{2,3},{3,2},{4,5},{5,4},{6,7},{7,6},{8,9},{9,8},{10,11... | collective-permute-start | bytes 589832 | tf_op jit(solution)/shard_map/ppermute | solution.py:24
  58.5 7.9 %collective-permute-start.20 = (bf16[48,2048]{1,0:T(8,128)(2,1)S(1)}, bf16[48,2048]{1,0:T(8,128)(2,1)S(1)}, u32[]{:S(2)}, u32[]{:S(2)}) collective-permute-start(bf16[48,2048]{1,0:T(8,128)(2,1)S(1)} %collective-permute-done.19.refs_6_), channel_id=1, source_target_pairs={{0,1},{1,0},{2,3},{3,2},{4,5},{5,4},{6,7},{7,6},{8,9},{9,8},{10,11... | collective-permute-start | bytes 589832 | tf_op jit(solution)/shard_map/ppermute | solution.py:24
  58.6 14.1 %collective-permute-start.22 = (bf16[192,1024]{1,0:T(8,128)(2,1)S(1)}, bf16[192,1024]{1,0:T(8,128)(2,1)S(1)}, u32[]{:S(2)}, u32[]{:S(2)}) collective-permute-start(bf16[192,1024]{1,0:T(8,128)(2,1)S(1)} %get-tuple-element.82), channel_id=1, source_target_pairs={{0,4},{4,0},{8,12},{12,8},{1,5},{5,1},{9,13},{13,9},{2,6},{6,2},{1... | collective-permute-start | bytes 1179656 | tf_op jit(solution)/shard_map/ppermute | solution.py:24
  64.3 11.3 %collective-permute-start.24 = (bf16[48,2048]{1,0:T(8,128)(2,1)S(1)}, bf16[48,2048]{1,0:T(8,128)(2,1)S(1)}, u32[]{:S(2)}, u32[]{:S(2)}) collective-permute-start(bf16[48,2048]{1,0:T(8,128)(2,1)S(1)} %get-tuple-element.85.refs_0_), channel_id=1, source_target_pairs={{0,2},{1,3},{2,0},{3,1},{4,6},{5,7},{6,4},{7,5},{8,10},{9,11},{10,... | collective-permute-start | bytes 589832 | tf_op jit(solution)/shard_map/ppermute | solution.py:24
  65.9 9.8 %collective-permute-start.27 = (bf16[48,2048]{1,0:T(8,128)(2,1)S(1)}, bf16[48,2048]{1,0:T(8,128)(2,1)S(1)}, u32[]{:S(2)}, u32[]{:S(2)}) collective-permute-start(bf16[48,2048]{1,0:T(8,128)(2,1)S(1)} %get-tuple-element.77.refs_4_), channel_id=1, source_target_pairs={{0,2},{1,3},{2,0},{3,1},{4,6},{5,7},{6,4},{7,5},{8,10},{9,11},{10,... | collective-permute-start | bytes 589832 | tf_op jit(solution)/shard_map/ppermute | solution.py:24
  66.4 14.8 %collective-permute-start.26 = (bf16[48,2048]{1,0:T(8,128)(2,1)S(1)}, bf16[48,2048]{1,0:T(8,128)(2,1)S(1)}, u32[]{:S(2)}, u32[]{:S(2)}) collective-permute-start(bf16[48,2048]{1,0:T(8,128)(2,1)S(1)} %get-tuple-element.77.refs_4_), channel_id=1, source_target_pairs={{0,1},{1,0},{2,3},{3,2},{4,5},{5,4},{6,7},{7,6},{8,9},{9,8},{10,11... | collective-permute-start | bytes 589832 | tf_op jit(solution)/shard_map/ppermute | solution.py:24
  72.0 10.7 %collective-permute-start.23 = (bf16[48,2048]{1,0:T(8,128)(2,1)S(1)}, bf16[48,2048]{1,0:T(8,128)(2,1)S(1)}, u32[]{:S(2)}, u32[]{:S(2)}) collective-permute-start(bf16[48,2048]{1,0:T(8,128)(2,1)S(1)} %get-tuple-element.85.refs_0_), channel_id=1, source_target_pairs={{0,1},{1,0},{2,3},{3,2},{4,5},{5,4},{6,7},{7,6},{8,9},{9,8},{10,11... | collective-permute-start | bytes 589832 | tf_op jit(solution)/shard_map/ppermute | solution.py:24
  72.7 17.6 %collective-permute-start.31 = (bf16[192,768]{1,0:T(8,128)(2,1)S(1)}, bf16[192,768]{1,0:T(8,128)(2,1)S(1)}, u32[]{:S(2)}, u32[]{:S(2)}) collective-permute-start(bf16[192,768]{1,0:T(8,128)(2,1)S(1)} %add_convert_fusion.3), channel_id=1, source_target_pairs={{0,8},{4,12},{8,0},{12,4},{1,9},{5,13},{9,1},{13,5},{2,10},{6,14},... | collective-permute-start | bytes 884744 | tf_op jit(solution)/shard_map/ppermute | solution.py:24
  75.6 7.7 %collective-permute-start.25 = (bf16[48,2048]{1,0:T(8,128)(2,1)S(1)}, bf16[48,2048]{1,0:T(8,128)(2,1)S(1)}, u32[]{:S(2)}, u32[]{:S(2)}) collective-permute-start(bf16[48,2048]{1,0:T(8,128)(2,1)S(1)} %collective-permute-done.24.refs_2_), channel_id=1, source_target_pairs={{0,1},{1,0},{2,3},{3,2},{4,5},{5,4},{6,7},{7,6},{8,9},{9,8},{10,11... | collective-permute-start | bytes 589832 | tf_op jit(solution)/shard_map/ppermute | solution.py:24
  75.6 7.7 %collective-permute-start.28 = (bf16[48,2048]{1,0:T(8,128)(2,1)S(1)}, bf16[48,2048]{1,0:T(8,128)(2,1)S(1)}, u32[]{:S(2)}, u32[]{:S(2)}) collective-permute-start(bf16[48,2048]{1,0:T(8,128)(2,1)S(1)} %collective-permute-done.27.refs_6_), channel_id=1, source_target_pairs={{0,1},{1,0},{2,3},{3,2},{4,5},{5,4},{6,7},{7,6},{8,9},{9,8},{10,11... | collective-permute-start | bytes 589832 | tf_op jit(solution)/shard_map/ppermute | solution.py:24
  81.2 9.5 %collective-permute-start.30 = (bf16[48,2048]{1,0:T(8,128)(2,1)S(1)}, bf16[48,2048]{1,0:T(8,128)(2,1)S(1)}, u32[]{:S(2)}, u32[]{:S(2)}) collective-permute-start(bf16[48,2048]{1,0:T(8,128)(2,1)S(1)} %get-tuple-element.92.refs_0_), channel_id=1, source_target_pairs={{0,2},{1,3},{2,0},{3,1},{4,6},{5,7},{6,4},{7,5},{8,10},{9,11},{10,... | collective-permute-start | bytes 589832 | tf_op jit(solution)/shard_map/ppermute | solution.py:24
  82.7 9.5 %collective-permute-start.34 = (bf16[48,2048]{1,0:T(8,128)(2,1)S(1)}, bf16[48,2048]{1,0:T(8,128)(2,1)S(1)}, u32[]{:S(2)}, u32[]{:S(2)}) collective-permute-start(bf16[48,2048]{1,0:T(8,128)(2,1)S(1)} %get-tuple-element.94.refs_4_), channel_id=1, source_target_pairs={{0,2},{1,3},{2,0},{3,1},{4,6},{5,7},{6,4},{7,5},{8,10},{9,11},{10,... | collective-permute-start | bytes 589832 | tf_op jit(solution)/shard_map/ppermute | solution.py:24
  88.8 12.1 %collective-permute-start.36 = (bf16[192,768]{1,0:T(8,128)(2,1)S(1)}, bf16[192,768]{1,0:T(8,128)(2,1)S(1)}, u32[]{:S(2)}, u32[]{:S(2)}) collective-permute-start(bf16[192,768]{1,0:T(8,128)(2,1)S(1)} %get-tuple-element.88), channel_id=1, source_target_pairs={{0,4},{4,0},{8,12},{12,8},{1,5},{5,1},{9,13},{13,9},{2,6},{6,2},{1... | collective-permute-start | bytes 884744 | tf_op jit(solution)/shard_map/ppermute | solution.py:24
  92.3 21.0 %collective-permute-start.41 = (bf16[192,1024]{1,0:T(8,128)(2,1)S(1)}, bf16[192,1024]{1,0:T(8,128)(2,1)S(1)}, u32[]{:S(2)}, u32[]{:S(2)}) collective-permute-start(bf16[192,1024]{1,0:T(8,128)(2,1)S(1)} %add_convert_fusion.1), channel_id=1, source_target_pairs={{0,8},{4,12},{8,0},{12,4},{1,9},{5,13},{9,1},{13,5},{2,10},{6,14},... | collective-permute-start | bytes 1179656 | tf_op jit(solution)/shard_map/ppermute | solution.py:24
  93.6 20.5 %collective-permute-start.40 = (bf16[192,1024]{1,0:T(8,128)(2,1)S(1)}, bf16[192,1024]{1,0:T(8,128)(2,1)S(1)}, u32[]{:S(2)}, u32[]{:S(2)}) collective-permute-start(bf16[192,1024]{1,0:T(8,128)(2,1)S(1)} %get-tuple-element.89), channel_id=1, source_target_pairs={{0,4},{4,0},{8,12},{12,8},{1,5},{5,1},{9,13},{13,9},{2,6},{6,2},{1... | collective-permute-start | bytes 1179656 | tf_op jit(solution)/shard_map/ppermute | solution.py:24
  114.8 6.8 %collective-permute-start.43 = (bf16[48,1024]{1,0:T(8,128)(2,1)S(1)}, bf16[48,1024]{1,0:T(8,128)(2,1)S(1)}, u32[]{:S(2)}, u32[]{:S(2)}) collective-permute-start(bf16[48,1024]{1,0:T(8,128)(2,1)S(1)} %get-tuple-element.103), channel_id=1, source_target_pairs={{0,2},{1,3},{2,0},{3,1},{4,6},{5,7},{6,4},{7,5},{8,10},{9,11},{10,... | collective-permute-start | bytes 294920 | tf_op jit(solution)/shard_map/ppermute | solution.py:24
  (28 other events, 208.0 us)

commit v6 on v5

--- a/solution.py
+++ b/solution.py
@@ -9,13 +9,7 @@
 from jax.sharding import PartitionSpec as P
 
 MIB = 1 << 20
-CFG = {'cost': 0.0, 'near': 'three', 'c': [3], 'b': [3], 'a': [3], 't': [3], 'h': [[4], [4], [4], [4]], 'arr': 3, 'p3r2': 1, 'p3n': 1, 'own3': 1, 't3r2': 1, 'cn': 1, 'cx2': 0, 'r0': 'post', 'core1': 'sums', 'own1': 0, 't1': 'sums', 'core0': 'first', 'own0': 1, 'hand': 'end', 't0': 'none', 'tail': [0, 1], 'tie': 1}
-
-
-def cost(us):
-    return pl.CostEstimate(
-        flops=int(us * CFG["cost"] * 1.15e9) + 1, bytes_accessed=1, transcendentals=0
-    )
+LIGHT = pl.CostEstimate(flops=1, bytes_accessed=1, transcendentals=0)
 
 
 def swap(value, axis, distance, inner=1):
@@ -91,7 +85,7 @@
         out_specs=pl.BlockSpec((step, rows, latent + rotary), lambda h: (h, 0, 0)),
         out_shape=jax.ShapeDtypeStruct((heads, rows, latent + rotary), q_nope.dtype),
         compiler_params=pltpu.CompilerParams(vmem_limit_bytes=8 * MIB),
-        cost_estimate=cost(3),
+        cost_estimate=LIGHT,
         name="absorb",
     )(q_nope, q_rope, w_key)
 
@@ -181,7 +175,7 @@
         out_shape=[jax.ShapeDtypeStruct((stretch, heads // halves * value_width), jnp.bfloat16)]
         * halves,
         compiler_params=pltpu.CompilerParams(vmem_limit_bytes=10 * MIB * max(span // 512, 1)),
-        cost_estimate=cost(5),
+        cost_estimate=LIGHT,
         name=f"attend_{distance}",
     )(ids, prefix_len, stretch_len, full_query, *blocks, w_value)
 
@@ -229,7 +223,7 @@
         out_shape=[jax.ShapeDtypeStruct((rows, columns), dtype) for _, columns in splits],
         scratch_shapes=[pltpu.VMEM((rows, depth), jnp.bfloat16)],
         compiler_params=pltpu.CompilerParams(vmem_limit_bytes=14 * MIB),
-        cost_estimate=cost(5.5),
+        cost_estimate=LIGHT,
         name=name,
     )(*pieces, w_out)
 
@@ -346,9 +340,8 @@
         swap(after(outgoing[k], full_query), "request", k) for k in range(1, rank_count)
     ]
     far_three = swap(after(far_two, far_one, full_query), "tensor", 1, inner)
-    near_gate = [far_three] if CFG["near"] == "three" else [far_two, far_one]
-    near_two = swap(after(far_keys, *near_gate), "tensor", 2, inner)
-    near_one = swap(after(near_keys, *near_gate), "tensor", 1, inner)
+    near_two = swap(after(far_keys, far_three), "tensor", 2, inner)
+    near_one = swap(after(near_keys, far_three), "tensor", 1, inner)
     far_blocks = [far_keys, far_one, far_two, far_three]
     near_blocks = [near_keys, near_one, near_two]
 
@@ -368,62 +361,41 @@
         )
 
     width = w_out.shape[1]
-    split = {k: split_at(width, *[256 * p for p in CFG[k]]) if width == 1792 else [(0, width)] for k in "cbat"}
-    heads = [split_at(head_count, *[head_count * p // 8 for p in CFG["h"][k]]) for k in range(4)]
+    splits = split_at(width, -(-width // 512) * 256) if width % 256 == 0 else split_at(width)
     sent = jnp.bfloat16
 
-    def regroup(arrays, splits):
-        if [x.shape[1] for x in arrays] == [size for _, size in splits]:
-            return arrays
-        whole = jnp.concatenate(arrays, axis=1) if len(arrays) > 1 else arrays[0]
-        return [whole[:, start : start + size] for start, size in splits]
-
-    def terms_of(distance, pieces, dtype, splits, *earlier):
+    def terms_of(distance, pieces, dtype, *earlier):
         pieces = [after(pieces[0], *earlier)] + pieces[1:]
         return project(pieces, w_out, splits, dtype, f"project_{distance}")
 
-    rows_3 = rows_of(3, far_blocks, heads[3], *(arrived if CFG["arr"] == 3 else []))
+    rows_3 = rows_of(3, far_blocks, *arrived)
     cross_3 = cross(rows_3, "request")
-    rows_2 = rows_of(2, far_blocks, heads[2], *rows_3, *(arrived if CFG["arr"] == 2 else []))
+    rows_2 = rows_of(2, far_blocks, *rows_3)
     cross_2 = cross(rows_2, "request")
-    crossed_2 = [piece for pieces in cross_2 for k, piece in pieces.items() if k]
-    gate = [*(rows_2 if CFG["p3r2"] else []), *([near_one, near_two] if CFG["p3n"] else [])]
-    pieces_3 = spread(cross_3, "request", *gate, own=rows_2 if CFG["own3"] else ())
-    terms_3 = terms_of(3, pieces_3, sent, split["c"], *(rows_2 if CFG["t3r2"] else []))
+    pieces_3 = spread(cross_3, "request", *rows_2, near_one, near_two, own=rows_2)
+    terms_3 = terms_of(3, pieces_3, sent, *rows_2)
     near_blocks.append(swap(near_two, "tensor", 1, inner))
-    gate = [*([near_blocks[3]] if CFG["cn"] else []), *(crossed_2 if CFG["cx2"] else [])]
-    opposite = [swap(after(t, *gate), "tensor", 1, inner) for t in terms_3]
-    rows_1 = rows_of(1, near_blocks, heads[1], *terms_3)
+    opposite = [swap(after(t, near_blocks[3]), "tensor", 1, inner) for t in terms_3]
+    rows_1 = rows_of(1, near_blocks, *terms_3)
     cross_1 = cross(rows_1, "request")
-    if CFG["r0"] != "post":
-        rows_0 = rows_of(0, near_blocks, heads[0], *rows_1)
-    pieces_2 = spread(cross_2, "request")
-    terms_2 = terms_of(2, pieces_2, jnp.float32, split["b"], *(rows_0 if CFG["r0"] == "pre" else rows_1))
-    sums = [(t + o).astype(sent) for t, o in zip(terms_2, regroup(opposite, split["b"]))]
+    pieces_2 = spread(cross_2[:1], "request")
+    pieces_2 += spread(cross_2[1:], "request", *rows_1)
+    terms_2 = terms_of(2, pieces_2, jnp.float32, *rows_1)
+    sums = [(t + o).astype(sent) for t, o in zip(terms_2, opposite)]
     across = [swap(t, "tensor", 2, inner) for t in sums]
-    if CFG["r0"] == "post":
-        rows_0 = rows_of(0, near_blocks, heads[0], *sums)
+    rows_0 = rows_of(0, near_blocks, *sums)
     cross_0 = cross(rows_0, "request")
-    gates = {"none": [], "sums": sums, "first": across[:1], "last": across[-1:]}
-    pieces_1 = spread(cross_1, "request", *gates[CFG["core1"]], own=sums if CFG["own1"] else ())
-    terms_1 = terms_of(1, pieces_1, sent, split["a"], *(sums if CFG["t1"] == "sums" else rows_0))
+    pieces_1 = spread(cross_1, "request", *sums)
+    terms_1 = terms_of(1, pieces_1, sent, *sums)
     beside = [swap(t, "tensor", 1, inner) for t in terms_1]
-    gates["beside"] = beside[:1]
-    pieces_0 = spread(cross_0, "request", *gates[CFG["core0"]], own=rows_0 if CFG["own0"] else ())
-    if CFG["hand"] == "t1":
-        handed = place_blocks(after(ids, *terms_1), arrived)
-    elif CFG["hand"] == "r1":
-        handed = place_blocks(after(ids, *rows_1), arrived)
-    terms_0 = terms_of(0, pieces_0, jnp.float32, split["t"], *([handed] if CFG["hand"] != "end" else []), *gates[CFG["t0"]], *terms_1)
-    if CFG["hand"] == "end":
-        handed = place_blocks(after(ids, *terms_0), arrived)
-    across, beside = regroup(across, split["t"]), regroup(beside, split["t"])
-    parts = len(split["t"])
-
-    columns = {}
+    pieces_0 = spread(cross_0, "request", across[0], own=rows_0)
+    terms_0 = terms_of(0, pieces_0, jnp.float32, *terms_1)
+    handed = place_blocks(after(ids, *terms_0), arrived)
+
+    columns = []
     earlier = []
-    for part in CFG['tail'] if parts > 1 else [0]:
-        summed = (after(terms_0[part], *(earlier if CFG['tie'] else [])) + beside[part] + across[part]).astype(sent)
+    for kept_terms, near_terms, far_terms in zip(terms_0, beside, across):
+        summed = (after(kept_terms, *earlier) + near_terms + far_terms).astype(sent)
         if inner > 1:
             summed = summed.reshape(rank_count, inner, share_rows, summed.shape[1]).swapaxes(0, 1)
             summed = lax.psum_scatter(
@@ -431,9 +403,9 @@
             )
         summed = summed.reshape(rank_count, share_rows, summed.shape[-1])
         earlier = [swap(summed[k], "request", k) for k in range(1, rank_count)]
-        columns[part] = [summed[0]] + earlier
-    ordered = [columns[part][k] for k in range(rank_count) for part in range(parts)]
-    mixed = place_columns(ids, ordered, split['t'])[None]
+        columns.append([summed[0]] + earlier)
+    ordered = [part[k] for k in range(rank_count) for part in columns]
+    mixed = place_columns(ids, ordered, splits)[None]
     handed = handed.transpose(0, 2, 1)[None]
     return (mixed, handed)
 

time: 123 us -> 122 us (level)
  waiting for transfers between devices: 27.8 us -> 24.7 us
  starting transfers between devices: 34.8 us -> 36.3 us
    ppermute x45, waiting for transfers between devices: 27.8 us -> 24.7 us  [swap(): return lax.ppermute(value, axis, pairs)]
    ppermute x45, starting transfers between devices: 34.8 us -> 36.3 us  [swap(): return lax.ppermute(value, axis, pairs)]
  transfers between devices with their start and end apart: 45 -> 45, of which waited for: 12 -> 11; matrix products, arithmetic and copies ran while one was open for 0% -> 0% of each run, Pallas kernels for 39% -> 39%
where the time goes in v6:
time: 122 us; the launch traced here: 121 us
  Pallas kernels  49.4 us (40%)
  starting transfers between devices  36.3 us (30%)
  waiting for transfers between devices  24.7 us (20%)
  local copies, waits for them, and re-layouts  9.59 us (8%)
    ppermute x45, starting transfers between devices, swap(): return lax.ppermute(value, axis, pairs)  36.3 us
    ppermute x45, waiting for transfers between devices, swap(): return lax.ppermute(value, axis, pairs)  24.7 us
    pallas_call x4, Pallas kernels, project(): pl.pallas_call(functools.partial(project_kernel, stretch, splits), grid=(...  22.2 us
    pallas_call x4, Pallas kernels, attend(): pl.pallas_call(functools.partial(attend_kernel, distance, scale), grid_sp...  20.2 us
    unnamed x30, local copies, waits for them, and re-layouts  8.44 us
    pallas_call x1, Pallas kernels, absorb(): pl.pallas_call(absorb_kernel, grid=(heads // step,), in_specs=[pl.BlockSp...  3.3 us
  transfers between devices with their start and end apart: 45, of which 11 were waited for; matrix products, arithmetic and copies ran while one was open for 0% of the time, Pallas kernels for 39%

profile of v6, /device:TPU:0, one launch (start us, length us, event | category | flops | bytes accessed | tf_op | source)
XLA Modules:
  0.0 121.4 jit_solution(6422932678379070758)
XLA Ops:
  1.8 4.1 %collective-permute-start.4 = (bf16[2,576,128]{2,1,0:T(8,128)(2,1)S(1)}, bf16[2,576,128]{2,1,0:T(8,128)(2,1)S(1)}, u32[]{:S(2)}, u32[]{:S(2)}) collective-permute-start(bf16[2,576,128]{2,1,0:T(8,128)(2,1)S(1)} %get-tuple-element.69.refs_0_), channel_id=1, source_target_pairs={{0,8},{4,12},{8,0},{12,4},{1,9},{5,13},{9,1},{13,5},{2,10},{6,14},... | collective-permute-start | bytes 884744 | tf_op jit(solution)/shard_map/ppermute | solution.py:18
  5.9 1.6 %collective-permute-start.3 = (bf16[2,576,128]{2,1,0:T(8,128)(2,1)S(1)}, bf16[2,576,128]{2,1,0:T(8,128)(2,1)S(1)}, u32[]{:S(2)}, u32[]{:S(2)}) collective-permute-start(bf16[2,576,128]{2,1,0:T(8,128)(2,1)S(1)} %get-tuple-element.70.refs_0_), channel_id=1, source_target_pairs={{0,4},{4,0},{8,12},{12,8},{1,5},{5,1},{9,13},{13,9},{2,6},{6,2},{1... | collective-permute-start | bytes 884744 | tf_op jit(solution)/shard_map/ppermute | solution.py:18
  12.1 2.2 %copy-done.1 = bf16[32,512,128]{2,1,0:T(8,128)(2,1)S(1)} copy-done((bf16[32,512,128]{2,1,0:T(8,128)(2,1)S(1)}, bf16[32,512,128]{2,1,0:T(8,128)(2,1)}, u32[]{:S(2)}) %copy-start.1) | copy-done | bytes 4194328
  14.3 1.4 %copy-done.3 = bf16[192,4096]{1,0:T(8,128)(2,1)S(1)} copy-done((bf16[192,4096]{1,0:T(8,128)(2,1)S(1)}, bf16[192,4096]{1,0:T(8,128)(2,1)}, u32[]{:S(2)}) %copy-start.3) | copy-done | bytes 1572888
  16.9 3.3 %absorb.1.query_ref = bf16[32,192,576]{2,1,0:T(8,128)(2,1)S(1)} custom-call(bf16[192,4096]{1,0:T(8,128)(2,1)S(1)} %copy-done.3, bf16[192,2048]{1,0:T(8,128)(2,1)S(1)} %copy-done.4, bf16[32,512,128]{2,1,0:T(8,128)(2,1)S(1)} %copy-done.1), custom_call_target="tpu_custom_call" | custom-call | flops 1 | bytes 1 | tf_op jit(solution)/shard_map/absorb/pallas_call | solution.py:77
  21.0 1.5 %collective-permute-start.1 = (bf16[576,128]{1,0:T(8,128)(2,1)S(1)}, bf16[576,128]{1,0:T(8,128)(2,1)S(1)}, u32[]{:S(2)}, u32[]{:S(2)}) collective-permute-start(bf16[576,128]{1,0:T(8,128)(2,1)S(1)} %get-tuple-element.59), channel_id=1, source_target_pairs={{0,2},{1,3},{2,0},{3,1},{4,6},{5,7},{6,4},{7,5},{8,10},{9,11},{10,... | collective-permute-start | bytes 442376 | tf_op jit(solution)/shard_map/ppermute | solution.py:18
  22.8 5.6 %collective-permute-done.5.refs_3_ = bf16[2,576,128]{2,1,0:T(8,128)(2,1)S(1)} collective-permute-done((bf16[2,576,128]{2,1,0:T(8,128)(2,1)S(1)}, bf16[2,576,128]{2,1,0:T(8,128)(2,1)S(1)}, u32[]{:S(2)}, u32[]{:S(2)}) %collective-permute-start.5) | collective-permute-done | bytes 294944 | tf_op jit(solution)/shard_map/ppermute | solution.py:18
  28.5 2.0 %collective-permute-start.9 = (bf16[2,576,128]{2,1,0:T(8,128)(2,1)S(1)}, bf16[2,576,128]{2,1,0:T(8,128)(2,1)S(1)}, u32[]{:S(2)}, u32[]{:S(2)}) collective-permute-start(bf16[2,576,128]{2,1,0:T(8,128)(2,1)S(1)} %get-tuple-element.70.refs_0_), channel_id=1, source_target_pairs={{0,8},{4,12},{8,0},{12,4},{1,9},{5,13},{9,1},{13,5},{2,10},{6,14},... | collective-permute-start | bytes 884744 | tf_op jit(solution)/shard_map/ppermute | solution.py:18
  30.5 1.7 %collective-permute-start.8 = (bf16[2,576,128]{2,1,0:T(8,128)(2,1)S(1)}, bf16[2,576,128]{2,1,0:T(8,128)(2,1)S(1)}, u32[]{:S(2)}, u32[]{:S(2)}) collective-permute-start(bf16[2,576,128]{2,1,0:T(8,128)(2,1)S(1)} %get-tuple-element.69.refs_0_), channel_id=1, source_target_pairs={{0,4},{4,0},{8,12},{12,8},{1,5},{5,1},{9,13},{13,9},{2,6},{6,2},{1... | collective-permute-start | bytes 884744 | tf_op jit(solution)/shard_map/ppermute | solution.py:18
  32.3 5.0 %attend_3.1 = (bf16[48,2048]{1,0:T(8,128)(2,1)S(1)}, bf16[48,2048]{1,0:T(8,128)(2,1)S(1)}) custom-call(s32[3]{0:T(128)S(1)} %pad_add_fusion.ids_ref, s32[4]{0:T(128)S(1)} %copy-done.6, s32[4]{0:T(128)S(1)} %copy-done.8, bf16[32,192,576]{2,1,0:T(8,128)(2,1)S(1)} %absorb.1.query_ref, bf16[2,576,128]{2,1,0:T(8,128)(2,1)S(1)} %get-tuple-element.70.refs_0_, ...), custom_call_target="tpu_custom_call" | custom-call | flops 1 | bytes 1 | tf_op jit(solution)/shard_map/attend_3/pallas_call | solution.py:157
  37.3 1.6 %collective-permute-start.7 = (bf16[48,2048]{1,0:T(8,128)(2,1)S(1)}, bf16[48,2048]{1,0:T(8,128)(2,1)S(1)}, u32[]{:S(2)}, u32[]{:S(2)}) collective-permute-start(bf16[48,2048]{1,0:T(8,128)(2,1)S(1)} %get-tuple-element.68.refs_0_), channel_id=1, source_target_pairs={{0,2},{1,3},{2,0},{3,1},{4,6},{5,7},{6,4},{7,5},{8,10},{9,11},{10,... | collective-permute-start | bytes 589832 | tf_op jit(solution)/shard_map/ppermute | solution.py:18
  39.4 5.0 %attend_2.1 = (bf16[48,2048]{1,0:T(8,128)(2,1)S(1)}, bf16[48,2048]{1,0:T(8,128)(2,1)S(1)}) custom-call(s32[3]{0:T(128)S(1)} %pad_add_fusion.ids_ref, s32[4]{0:T(128)S(1)} %copy-done.6, s32[4]{0:T(128)S(1)} %copy-done.8, bf16[32,192,576]{2,1,0:T(8,128)(2,1)S(1)} %absorb.1.query_ref, bf16[2,576,128]{2,1,0:T(8,128)(2,1)S(1)} %get-tuple-element.70.refs_0_, ...), custom_call_target="tpu_custom_call" | custom-call | flops 1 | bytes 1 | tf_op jit(solution)/shard_map/attend_2/pallas_call | solution.py:157
  47.0 1.5 %collective-permute-start.16 = (bf16[48,2048]{1,0:T(8,128)(2,1)S(1)}, bf16[48,2048]{1,0:T(8,128)(2,1)S(1)}, u32[]{:S(2)}, u32[]{:S(2)}) collective-permute-start(bf16[48,2048]{1,0:T(8,128)(2,1)S(1)} %get-tuple-element.79.refs_0_), channel_id=1, source_target_pairs={{0,2},{1,3},{2,0},{3,1},{4,6},{5,7},{6,4},{7,5},{8,10},{9,11},{10,... | collective-permute-start | bytes 589832 | tf_op jit(solution)/shard_map/ppermute | solution.py:18
  49.1 5.5 %project_3.1 = (bf16[192,1024]{1,0:T(8,128)(2,1)S(1)}, bf16[192,768]{1,0:T(8,128)(2,1)S(1)}) custom-call(bf16[48,2048]{1,0:T(8,128)(2,1)S(1)} %get-tuple-element.68.refs_0_, bf16[48,2048]{1,0:T(8,128)(2,1)S(1)} %collective-permute-done.6.refs_1_, bf16[48,2048]{1,0:T(8,128)(2,1)S(1)} %collective-permute-done.7.refs_2_, ...), custom_call_target="tpu_custom_call" | custom-call | flops 1 | bytes 1 | tf_op jit(solution)/shard_map/project_3/pallas_call | solution.py:217
  55.9 5.0 %attend_1.1 = (bf16[48,2048]{1,0:T(8,128)(2,1)S(1)}, bf16[48,2048]{1,0:T(8,128)(2,1)S(1)}) custom-call(s32[3]{0:T(128)S(1)} %pad_add_fusion.ids_ref, s32[4]{0:T(128)S(1)} %copy-done.6, s32[4]{0:T(128)S(1)} %copy-done.8, bf16[32,192,576]{2,1,0:T(8,128)(2,1)S(1)} %absorb.1.query_ref, bf16[2,576,128]{2,1,0:T(8,128)(2,1)S(1)} %get-tuple-element.69.refs_0_, ...), custom_call_target="tpu_custom_call" | custom-call | flops 1 | bytes 1 | tf_op jit(solution)/shard_map/attend_1/pallas_call | solution.py:157
  62.6 1.5 %collective-permute-start.24 = (bf16[48,2048]{1,0:T(8,128)(2,1)S(1)}, bf16[48,2048]{1,0:T(8,128)(2,1)S(1)}, u32[]{:S(2)}, u32[]{:S(2)}) collective-permute-start(bf16[48,2048]{1,0:T(8,128)(2,1)S(1)} %get-tuple-element.87.refs_0_), channel_id=1, source_target_pairs={{0,2},{1,3},{2,0},{3,1},{4,6},{5,7},{6,4},{7,5},{8,10},{9,11},{10,... | collective-permute-start | bytes 589832 | tf_op jit(solution)/shard_map/ppermute | solution.py:18
  64.7 5.6 %project_2.1 = (f32[192,1024]{1,0:T(8,128)S(1)}, f32[192,768]{1,0:T(8,128)S(1)}) custom-call(bf16[48,2048]{1,0:T(8,128)(2,1)S(1)} %get-tuple-element.79.refs_0_, bf16[48,2048]{1,0:T(8,128)(2,1)S(1)} %collective-permute-done.15.refs_1_, bf16[48,2048]{1,0:T(8,128)(2,1)S(1)} %collective-permute-done.16.refs_2_, ...), custom_call_target="tpu_custom_call" | custom-call | flops 1 | bytes 1 | tf_op jit(solution)/shard_map/project_2/pallas_call | solution.py:217
  70.9 1.7 %collective-permute-done.21 = bf16[192,1024]{1,0:T(8,128)(2,1)S(1)} collective-permute-done((bf16[192,1024]{1,0:T(8,128)(2,1)S(1)}, bf16[192,1024]{1,0:T(8,128)(2,1)S(1)}, u32[]{:S(2)}, u32[]{:S(2)}) %collective-permute-start.21) | collective-permute-done | bytes 393248 | tf_op jit(solution)/shard_map/ppermute | solution.py:18
  72.7 1.7 %collective-permute-start.31 = (bf16[192,1024]{1,0:T(8,128)(2,1)S(1)}, bf16[192,1024]{1,0:T(8,128)(2,1)S(1)}, u32[]{:S(2)}, u32[]{:S(2)}) collective-permute-start(bf16[192,1024]{1,0:T(8,128)(2,1)S(1)} %add_convert_fusion.1), channel_id=1, source_target_pairs={{0,8},{4,12},{8,0},{12,4},{1,9},{5,13},{9,1},{13,5},{2,10},{6,14},... | collective-permute-start | bytes 1179656 | tf_op jit(solution)/shard_map/ppermute | solution.py:18
  74.9 5.0 %attend_0.1 = (bf16[48,2048]{1,0:T(8,128)(2,1)S(1)}, bf16[48,2048]{1,0:T(8,128)(2,1)S(1)}) custom-call(s32[3]{0:T(128)S(1)} %pad_add_fusion.ids_ref, s32[4]{0:T(128)S(1)} %copy-done.6, s32[4]{0:T(128)S(1)} %copy-done.8, bf16[32,192,576]{2,1,0:T(8,128)(2,1)S(1)} %absorb.1.query_ref, bf16[2,576,128]{2,1,0:T(8,128)(2,1)S(1)} %get-tuple-element.69.refs_0_, ...), custom_call_target="tpu_custom_call" | custom-call | flops 1 | bytes 1 | tf_op jit(solution)/shard_map/attend_0/pallas_call | solution.py:157
  80.0 1.5 %collective-permute-start.34 = (bf16[48,2048]{1,0:T(8,128)(2,1)S(1)}, bf16[48,2048]{1,0:T(8,128)(2,1)S(1)}, u32[]{:S(2)}, u32[]{:S(2)}) collective-permute-start(bf16[48,2048]{1,0:T(8,128)(2,1)S(1)} %get-tuple-element.96.refs_4_), channel_id=1, source_target_pairs={{0,2},{1,3},{2,0},{3,1},{4,6},{5,7},{6,4},{7,5},{8,10},{9,11},{10,... | collective-permute-start | bytes 589832 | tf_op jit(solution)/shard_map/ppermute | solution.py:18
  82.1 5.5 %project_1.1 = (bf16[192,1024]{1,0:T(8,128)(2,1)S(1)}, bf16[192,768]{1,0:T(8,128)(2,1)S(1)}) custom-call(bf16[48,2048]{1,0:T(8,128)(2,1)S(1)} %get-tuple-element.87.refs_0_, bf16[48,2048]{1,0:T(8,128)(2,1)S(1)} %collective-permute-done.23.refs_1_, bf16[48,2048]{1,0:T(8,128)(2,1)S(1)} %collective-permute-done.24.refs_2_, ...), custom_call_target="tpu_custom_call" | custom-call | flops 1 | bytes 1 | tf_op jit(solution)/shard_map/project_1/pallas_call | solution.py:217
  87.6 1.5 %collective-permute-start.36 = (bf16[192,1024]{1,0:T(8,128)(2,1)S(1)}, bf16[192,1024]{1,0:T(8,128)(2,1)S(1)}, u32[]{:S(2)}, u32[]{:S(2)}) collective-permute-start(bf16[192,1024]{1,0:T(8,128)(2,1)S(1)} %get-tuple-element.90), channel_id=1, source_target_pairs={{0,4},{4,0},{8,12},{12,8},{1,5},{5,1},{9,13},{13,9},{2,6},{6,2},{1... | collective-permute-start | bytes 1179656 | tf_op jit(solution)/shard_map/ppermute | solution.py:18
  89.6 3.1 %collective-permute-done.31 = bf16[192,1024]{1,0:T(8,128)(2,1)S(1)} collective-permute-done((bf16[192,1024]{1,0:T(8,128)(2,1)S(1)}, bf16[192,1024]{1,0:T(8,128)(2,1)S(1)}, u32[]{:S(2)}, u32[]{:S(2)}) %collective-permute-start.31) | collective-permute-done | bytes 393248 | tf_op jit(solution)/shard_map/ppermute | solution.py:18
  93.2 3.0 %collective-permute-start.40 = (bf16[192,768]{1,0:T(8,128)(2,1)S(1)}, bf16[192,768]{1,0:T(8,128)(2,1)S(1)}, u32[]{:S(2)}, u32[]{:S(2)}) collective-permute-start(bf16[192,768]{1,0:T(8,128)(2,1)S(1)} %get-tuple-element.91), channel_id=1, source_target_pairs={{0,4},{4,0},{8,12},{12,8},{1,5},{5,1},{9,13},{13,9},{2,6},{6,2},{1... | collective-permute-start | bytes 884744 | tf_op jit(solution)/shard_map/ppermute | solution.py:18
  96.2 5.6 %project_0.1 = (f32[192,1024]{1,0:T(8,128)S(1)}, f32[192,768]{1,0:T(8,128)S(1)}) custom-call(bf16[48,2048]{1,0:T(8,128)(2,1)S(1)} %get-tuple-element.94.refs_0_, bf16[48,2048]{1,0:T(8,128)(2,1)S(1)} %collective-permute-done.29.refs_1_, bf16[48,2048]{1,0:T(8,128)(2,1)S(1)} %collective-permute-done.30.refs_2_, ...), custom_call_target="tpu_custom_call" | custom-call | flops 1 | bytes 1 | tf_op jit(solution)/shard_map/project_0/pallas_call | solution.py:217
  101.8 1.6 %collective-permute-done.36 = bf16[192,1024]{1,0:T(8,128)(2,1)S(1)} collective-permute-done((bf16[192,1024]{1,0:T(8,128)(2,1)S(1)}, bf16[192,1024]{1,0:T(8,128)(2,1)S(1)}, u32[]{:S(2)}, u32[]{:S(2)}) %collective-permute-start.36) | collective-permute-done | bytes 393248 | tf_op jit(solution)/shard_map/ppermute | solution.py:18
  105.6 3.1 %collective-permute-done.39.refs_6_ = bf16[48,1024]{1,0:T(8,128)(2,1)S(1)} collective-permute-done((bf16[48,1024]{1,0:T(8,128)(2,1)S(1)}, bf16[48,1024]{1,0:T(8,128)(2,1)S(1)}, u32[]{:S(2)}, u32[]{:S(2)}) %collective-permute-start.39) | collective-permute-done | bytes 98336 | tf_op jit(solution)/shard_map/ppermute | solution.py:18
  108.7 2.2 %collective-permute-done.38.refs_4_ = bf16[48,1024]{1,0:T(8,128)(2,1)S(1)} collective-permute-done((bf16[48,1024]{1,0:T(8,128)(2,1)S(1)}, bf16[48,1024]{1,0:T(8,128)(2,1)S(1)}, u32[]{:S(2)}, u32[]{:S(2)}) %collective-permute-start.38) | collective-permute-done | bytes 98336 | tf_op jit(solution)/shard_map/ppermute | solution.py:18
  110.9 2.7 %collective-permute-done.40 = bf16[192,768]{1,0:T(8,128)(2,1)S(1)} collective-permute-done((bf16[192,768]{1,0:T(8,128)(2,1)S(1)}, bf16[192,768]{1,0:T(8,128)(2,1)S(1)}, u32[]{:S(2)}, u32[]{:S(2)}) %collective-permute-start.40) | collective-permute-done | bytes 294944 | tf_op jit(solution)/shard_map/ppermute | solution.py:18
  118.2 1.8 %collective-permute-done.43.refs_5_ = bf16[48,768]{1,0:T(8,128)(2,1)S(1)} collective-permute-done((bf16[48,768]{1,0:T(8,128)(2,1)S(1)}, bf16[48,768]{1,0:T(8,128)(2,1)S(1)}, u32[]{:S(2)}, u32[]{:S(2)}) %collective-permute-start.43) | collective-permute-done | bytes 73760 | tf_op jit(solution)/shard_map/ppermute | solution.py:18
  120.0 1.4 %place_columns.1 = bf16[48,7168]{1,0:T(8,128)(2,1)} custom-call(s32[3]{0:T(128)S(1)} %pad_add_fusion.ids_ref, bf16[48,1024]{1,0:T(8,128)(2,1)S(1)} %get-tuple-element.107.refs_0_, bf16[48,768]{1,0:T(8,128)(2,1)S(1)} %get-tuple-element.111.refs_1_, bf16[48,1024]{1,0:T(8,128)(2,1)S(1)} %collective-permute-done.37.refs_2_, ...), custom_call_target="tpu_custom_call" | custom-call | tf_op jit(solution)/shard_map/place_columns/pallas_call | solution.py:288
  (109 shorter events, 24.7 us)
Async XLA Ops:
  1.8 18.4 %collective-permute-start.4 = (bf16[2,576,128]{2,1,0:T(8,128)(2,1)S(1)}, bf16[2,576,128]{2,1,0:T(8,128)(2,1)S(1)}, u32[]{:S(2)}, u32[]{:S(2)}) collective-permute-start(bf16[2,576,128]{2,1,0:T(8,128)(2,1)S(1)} %get-tuple-element.69.refs_0_), channel_id=1, source_target_pairs={{0,8},{4,12},{8,0},{12,4},{1,9},{5,13},{9,1},{13,5},{2,10},{6,14},... | collective-permute-start | bytes 884744 | tf_op jit(solution)/shard_map/ppermute | solution.py:18
  5.9 14.3 %collective-permute-start.3 = (bf16[2,576,128]{2,1,0:T(8,128)(2,1)S(1)}, bf16[2,576,128]{2,1,0:T(8,128)(2,1)S(1)}, u32[]{:S(2)}, u32[]{:S(2)}) collective-permute-start(bf16[2,576,128]{2,1,0:T(8,128)(2,1)S(1)} %get-tuple-element.70.refs_0_), channel_id=1, source_target_pairs={{0,4},{4,0},{8,12},{12,8},{1,5},{5,1},{9,13},{13,9},{2,6},{6,2},{1... | collective-permute-start | bytes 884744 | tf_op jit(solution)/shard_map/ppermute | solution.py:18
  20.2 8.3 %collective-permute-start.5 = (bf16[2,576,128]{2,1,0:T(8,128)(2,1)S(1)}, bf16[2,576,128]{2,1,0:T(8,128)(2,1)S(1)}, u32[]{:S(2)}, u32[]{:S(2)}) collective-permute-start(bf16[2,576,128]{2,1,0:T(8,128)(2,1)S(1)} %collective-permute-done.4.refs_2_), channel_id=1, source_target_pairs={{0,4},{4,0},{8,12},{12,8},{1,5},{5,1},{9,13},{13,9},{2,6},{6,2},{1... | collective-permute-start | bytes 884744 | tf_op jit(solution)/shard_map/ppermute | solution.py:18
  21.0 11.3 %collective-permute-start = (bf16[576,128]{1,0:T(8,128)(2,1)S(1)}, bf16[576,128]{1,0:T(8,128)(2,1)S(1)}, u32[]{:S(2)}, u32[]{:S(2)}) collective-permute-start(bf16[576,128]{1,0:T(8,128)(2,1)S(1)} %get-tuple-element.58), channel_id=1, source_target_pairs={{0,1},{1,0},{2,3},{3,2},{4,5},{5,4},{6,7},{7,6},{8,9},{9,8},{10,11... | collective-permute-start | bytes 442376 | tf_op jit(solution)/shard_map/ppermute | solution.py:18
  21.0 11.3 %collective-permute-start.1 = (bf16[576,128]{1,0:T(8,128)(2,1)S(1)}, bf16[576,128]{1,0:T(8,128)(2,1)S(1)}, u32[]{:S(2)}, u32[]{:S(2)}) collective-permute-start(bf16[576,128]{1,0:T(8,128)(2,1)S(1)} %get-tuple-element.59), channel_id=1, source_target_pairs={{0,2},{1,3},{2,0},{3,1},{4,6},{5,7},{6,4},{7,5},{8,10},{9,11},{10,... | collective-permute-start | bytes 442376 | tf_op jit(solution)/shard_map/ppermute | solution.py:18
  22.5 9.8 %collective-permute-start.2 = (bf16[576,128]{1,0:T(8,128)(2,1)S(1)}, bf16[576,128]{1,0:T(8,128)(2,1)S(1)}, u32[]{:S(2)}, u32[]{:S(2)}) collective-permute-start(bf16[576,128]{1,0:T(8,128)(2,1)S(1)} %get-tuple-element.60), channel_id=1, source_target_pairs={{0,3},{1,2},{2,1},{3,0},{4,7},{5,6},{6,5},{7,4},{8,11},{9,10},{10,... | collective-permute-start | bytes 442376 | tf_op jit(solution)/shard_map/ppermute | solution.py:18
  28.5 16.6 %collective-permute-start.9 = (bf16[2,576,128]{2,1,0:T(8,128)(2,1)S(1)}, bf16[2,576,128]{2,1,0:T(8,128)(2,1)S(1)}, u32[]{:S(2)}, u32[]{:S(2)}) collective-permute-start(bf16[2,576,128]{2,1,0:T(8,128)(2,1)S(1)} %get-tuple-element.70.refs_0_), channel_id=1, source_target_pairs={{0,8},{4,12},{8,0},{12,4},{1,9},{5,13},{9,1},{13,5},{2,10},{6,14},... | collective-permute-start | bytes 884744 | tf_op jit(solution)/shard_map/ppermute | solution.py:18
  30.5 15.1 %collective-permute-start.8 = (bf16[2,576,128]{2,1,0:T(8,128)(2,1)S(1)}, bf16[2,576,128]{2,1,0:T(8,128)(2,1)S(1)}, u32[]{:S(2)}, u32[]{:S(2)}) collective-permute-start(bf16[2,576,128]{2,1,0:T(8,128)(2,1)S(1)} %get-tuple-element.69.refs_0_), channel_id=1, source_target_pairs={{0,4},{4,0},{8,12},{12,8},{1,5},{5,1},{9,13},{13,9},{2,6},{6,2},{1... | collective-permute-start | bytes 884744 | tf_op jit(solution)/shard_map/ppermute | solution.py:18
  37.3 7.6 %collective-permute-start.7 = (bf16[48,2048]{1,0:T(8,128)(2,1)S(1)}, bf16[48,2048]{1,0:T(8,128)(2,1)S(1)}, u32[]{:S(2)}, u32[]{:S(2)}) collective-permute-start(bf16[48,2048]{1,0:T(8,128)(2,1)S(1)} %get-tuple-element.68.refs_0_), channel_id=1, source_target_pairs={{0,2},{1,3},{2,0},{3,1},{4,6},{5,7},{6,4},{7,5},{8,10},{9,11},{10,... | collective-permute-start | bytes 589832 | tf_op jit(solution)/shard_map/ppermute | solution.py:18
  38.9 8.1 %collective-permute-start.12 = (bf16[48,2048]{1,0:T(8,128)(2,1)S(1)}, bf16[48,2048]{1,0:T(8,128)(2,1)S(1)}, u32[]{:S(2)}, u32[]{:S(2)}) collective-permute-start(bf16[48,2048]{1,0:T(8,128)(2,1)S(1)} %get-tuple-element.72.refs_4_), channel_id=1, source_target_pairs={{0,2},{1,3},{2,0},{3,1},{4,6},{5,7},{6,4},{7,5},{8,10},{9,11},{10,... | collective-permute-start | bytes 589832 | tf_op jit(solution)/shard_map/ppermute | solution.py:18
  45.0 9.6 %collective-permute-start.14 = (bf16[2,576,128]{2,1,0:T(8,128)(2,1)S(1)}, bf16[2,576,128]{2,1,0:T(8,128)(2,1)S(1)}, u32[]{:S(2)}, u32[]{:S(2)}) collective-permute-start(bf16[2,576,128]{2,1,0:T(8,128)(2,1)S(1)} %collective-permute-done.9.refs_2_), channel_id=1, source_target_pairs={{0,4},{4,0},{8,12},{12,8},{1,5},{5,1},{9,13},{13,9},{2,6},{6,2},{1... | collective-permute-start | bytes 884744 | tf_op jit(solution)/shard_map/ppermute | solution.py:18
  47.0 8.6 %collective-permute-start.16 = (bf16[48,2048]{1,0:T(8,128)(2,1)S(1)}, bf16[48,2048]{1,0:T(8,128)(2,1)S(1)}, u32[]{:S(2)}, u32[]{:S(2)}) collective-permute-start(bf16[48,2048]{1,0:T(8,128)(2,1)S(1)} %get-tuple-element.79.refs_0_), channel_id=1, source_target_pairs={{0,2},{1,3},{2,0},{3,1},{4,6},{5,7},{6,4},{7,5},{8,10},{9,11},{10,... | collective-permute-start | bytes 589832 | tf_op jit(solution)/shard_map/ppermute | solution.py:18
  48.5 12.5 %collective-permute-start.19 = (bf16[48,2048]{1,0:T(8,128)(2,1)S(1)}, bf16[48,2048]{1,0:T(8,128)(2,1)S(1)}, u32[]{:S(2)}, u32[]{:S(2)}) collective-permute-start(bf16[48,2048]{1,0:T(8,128)(2,1)S(1)} %get-tuple-element.67.refs_4_), channel_id=1, source_target_pairs={{0,2},{1,3},{2,0},{3,1},{4,6},{5,7},{6,4},{7,5},{8,10},{9,11},{10,... | collective-permute-start | bytes 589832 | tf_op jit(solution)/shard_map/ppermute | solution.py:18
  49.1 12.2 %collective-permute-start.18 = (bf16[48,2048]{1,0:T(8,128)(2,1)S(1)}, bf16[48,2048]{1,0:T(8,128)(2,1)S(1)}, u32[]{:S(2)}, u32[]{:S(2)}) collective-permute-start(bf16[48,2048]{1,0:T(8,128)(2,1)S(1)} %get-tuple-element.67.refs_4_), channel_id=1, source_target_pairs={{0,1},{1,0},{2,3},{3,2},{4,5},{5,4},{6,7},{7,6},{8,9},{9,8},{10,11... | collective-permute-start | bytes 589832 | tf_op jit(solution)/shard_map/ppermute | solution.py:18
  54.7 15.6 %collective-permute-start.22 = (bf16[192,768]{1,0:T(8,128)(2,1)S(1)}, bf16[192,768]{1,0:T(8,128)(2,1)S(1)}, u32[]{:S(2)}, u32[]{:S(2)}) collective-permute-start(bf16[192,768]{1,0:T(8,128)(2,1)S(1)} %get-tuple-element.84), channel_id=1, source_target_pairs={{0,4},{4,0},{8,12},{12,8},{1,5},{5,1},{9,13},{13,9},{2,6},{6,2},{1... | collective-permute-start | bytes 884744 | tf_op jit(solution)/shard_map/ppermute | solution.py:18
  55.4 7.2 %collective-permute-start.15 = (bf16[48,2048]{1,0:T(8,128)(2,1)S(1)}, bf16[48,2048]{1,0:T(8,128)(2,1)S(1)}, u32[]{:S(2)}, u32[]{:S(2)}) collective-permute-start(bf16[48,2048]{1,0:T(8,128)(2,1)S(1)} %get-tuple-element.79.refs_0_), channel_id=1, source_target_pairs={{0,1},{1,0},{2,3},{3,2},{4,5},{5,4},{6,7},{7,6},{8,9},{9,8},{10,11... | collective-permute-start | bytes 589832 | tf_op jit(solution)/shard_map/ppermute | solution.py:18
  55.6 8.5 %collective-permute-start.17 = (bf16[48,2048]{1,0:T(8,128)(2,1)S(1)}, bf16[48,2048]{1,0:T(8,128)(2,1)S(1)}, u32[]{:S(2)}, u32[]{:S(2)}) collective-permute-start(bf16[48,2048]{1,0:T(8,128)(2,1)S(1)} %collective-permute-done.16.refs_2_), channel_id=1, source_target_pairs={{0,1},{1,0},{2,3},{3,2},{4,5},{5,4},{6,7},{7,6},{8,9},{9,8},{10,11... | collective-permute-start | bytes 589832 | tf_op jit(solution)/shard_map/ppermute | solution.py:18
  61.3 11.3 %collective-permute-start.21 = (bf16[192,1024]{1,0:T(8,128)(2,1)S(1)}, bf16[192,1024]{1,0:T(8,128)(2,1)S(1)}, u32[]{:S(2)}, u32[]{:S(2)}) collective-permute-start(bf16[192,1024]{1,0:T(8,128)(2,1)S(1)} %get-tuple-element.82), channel_id=1, source_target_pairs={{0,4},{4,0},{8,12},{12,8},{1,5},{5,1},{9,13},{13,9},{2,6},{6,2},{1... | collective-permute-start | bytes 1179656 | tf_op jit(solution)/shard_map/ppermute | solution.py:18
  62.6 11.8 %collective-permute-start.24 = (bf16[48,2048]{1,0:T(8,128)(2,1)S(1)}, bf16[48,2048]{1,0:T(8,128)(2,1)S(1)}, u32[]{:S(2)}, u32[]{:S(2)}) collective-permute-start(bf16[48,2048]{1,0:T(8,128)(2,1)S(1)} %get-tuple-element.87.refs_0_), channel_id=1, source_target_pairs={{0,2},{1,3},{2,0},{3,1},{4,6},{5,7},{6,4},{7,5},{8,10},{9,11},{10,... | collective-permute-start | bytes 589832 | tf_op jit(solution)/shard_map/ppermute | solution.py:18
  64.1 10.3 %collective-permute-start.27 = (bf16[48,2048]{1,0:T(8,128)(2,1)S(1)}, bf16[48,2048]{1,0:T(8,128)(2,1)S(1)}, u32[]{:S(2)}, u32[]{:S(2)}) collective-permute-start(bf16[48,2048]{1,0:T(8,128)(2,1)S(1)} %get-tuple-element.78.refs_4_), channel_id=1, source_target_pairs={{0,2},{1,3},{2,0},{3,1},{4,6},{5,7},{6,4},{7,5},{8,10},{9,11},{10,... | collective-permute-start | bytes 589832 | tf_op jit(solution)/shard_map/ppermute | solution.py:18
  64.7 15.3 %collective-permute-start.26 = (bf16[48,2048]{1,0:T(8,128)(2,1)S(1)}, bf16[48,2048]{1,0:T(8,128)(2,1)S(1)}, u32[]{:S(2)}, u32[]{:S(2)}) collective-permute-start(bf16[48,2048]{1,0:T(8,128)(2,1)S(1)} %get-tuple-element.78.refs_4_), channel_id=1, source_target_pairs={{0,1},{1,0},{2,3},{3,2},{4,5},{5,4},{6,7},{7,6},{8,9},{9,8},{10,11... | collective-permute-start | bytes 589832 | tf_op jit(solution)/shard_map/ppermute | solution.py:18
  70.3 11.3 %collective-permute-start.23 = (bf16[48,2048]{1,0:T(8,128)(2,1)S(1)}, bf16[48,2048]{1,0:T(8,128)(2,1)S(1)}, u32[]{:S(2)}, u32[]{:S(2)}) collective-permute-start(bf16[48,2048]{1,0:T(8,128)(2,1)S(1)} %get-tuple-element.87.refs_0_), channel_id=1, source_target_pairs={{0,1},{1,0},{2,3},{3,2},{4,5},{5,4},{6,7},{7,6},{8,9},{9,8},{10,11... | collective-permute-start | bytes 589832 | tf_op jit(solution)/shard_map/ppermute | solution.py:18
  72.7 20.0 %collective-permute-start.31 = (bf16[192,1024]{1,0:T(8,128)(2,1)S(1)}, bf16[192,1024]{1,0:T(8,128)(2,1)S(1)}, u32[]{:S(2)}, u32[]{:S(2)}) collective-permute-start(bf16[192,1024]{1,0:T(8,128)(2,1)S(1)} %add_convert_fusion.1), channel_id=1, source_target_pairs={{0,8},{4,12},{8,0},{12,4},{1,9},{5,13},{9,1},{13,5},{2,10},{6,14},... | collective-permute-start | bytes 1179656 | tf_op jit(solution)/shard_map/ppermute | solution.py:18
  74.4 7.7 %collective-permute-start.25 = (bf16[48,2048]{1,0:T(8,128)(2,1)S(1)}, bf16[48,2048]{1,0:T(8,128)(2,1)S(1)}, u32[]{:S(2)}, u32[]{:S(2)}) collective-permute-start(bf16[48,2048]{1,0:T(8,128)(2,1)S(1)} %collective-permute-done.24.refs_2_), channel_id=1, source_target_pairs={{0,1},{1,0},{2,3},{3,2},{4,5},{5,4},{6,7},{7,6},{8,9},{9,8},{10,11... | collective-permute-start | bytes 589832 | tf_op jit(solution)/shard_map/ppermute | solution.py:18
  74.4 7.7 %collective-permute-start.28 = (bf16[48,2048]{1,0:T(8,128)(2,1)S(1)}, bf16[48,2048]{1,0:T(8,128)(2,1)S(1)}, u32[]{:S(2)}, u32[]{:S(2)}) collective-permute-start(bf16[48,2048]{1,0:T(8,128)(2,1)S(1)} %collective-permute-done.27.refs_6_), channel_id=1, source_target_pairs={{0,1},{1,0},{2,3},{3,2},{4,5},{5,4},{6,7},{7,6},{8,9},{9,8},{10,11... | collective-permute-start | bytes 589832 | tf_op jit(solution)/shard_map/ppermute | solution.py:18
  80.0 9.1 %collective-permute-start.34 = (bf16[48,2048]{1,0:T(8,128)(2,1)S(1)}, bf16[48,2048]{1,0:T(8,128)(2,1)S(1)}, u32[]{:S(2)}, u32[]{:S(2)}) collective-permute-start(bf16[48,2048]{1,0:T(8,128)(2,1)S(1)} %get-tuple-element.96.refs_4_), channel_id=1, source_target_pairs={{0,2},{1,3},{2,0},{3,1},{4,6},{5,7},{6,4},{7,5},{8,10},{9,11},{10,... | collective-permute-start | bytes 589832 | tf_op jit(solution)/shard_map/ppermute | solution.py:18
  81.5 11.2 %collective-permute-start.30 = (bf16[48,2048]{1,0:T(8,128)(2,1)S(1)}, bf16[48,2048]{1,0:T(8,128)(2,1)S(1)}, u32[]{:S(2)}, u32[]{:S(2)}) collective-permute-start(bf16[48,2048]{1,0:T(8,128)(2,1)S(1)} %get-tuple-element.94.refs_0_), channel_id=1, source_target_pairs={{0,2},{1,3},{2,0},{3,1},{4,6},{5,7},{6,4},{7,5},{8,10},{9,11},{10,... | collective-permute-start | bytes 589832 | tf_op jit(solution)/shard_map/ppermute | solution.py:18
  87.6 15.8 %collective-permute-start.36 = (bf16[192,1024]{1,0:T(8,128)(2,1)S(1)}, bf16[192,1024]{1,0:T(8,128)(2,1)S(1)}, u32[]{:S(2)}, u32[]{:S(2)}) collective-permute-start(bf16[192,1024]{1,0:T(8,128)(2,1)S(1)} %get-tuple-element.90), channel_id=1, source_target_pairs={{0,4},{4,0},{8,12},{12,8},{1,5},{5,1},{9,13},{13,9},{2,6},{6,2},{1... | collective-permute-start | bytes 1179656 | tf_op jit(solution)/shard_map/ppermute | solution.py:18
  93.2 17.7 %collective-permute-start.41 = (bf16[192,768]{1,0:T(8,128)(2,1)S(1)}, bf16[192,768]{1,0:T(8,128)(2,1)S(1)}, u32[]{:S(2)}, u32[]{:S(2)}) collective-permute-start(bf16[192,768]{1,0:T(8,128)(2,1)S(1)} %add_convert_fusion.3), channel_id=1, source_target_pairs={{0,8},{4,12},{8,0},{12,4},{1,9},{5,13},{9,1},{13,5},{2,10},{6,14},... | collective-permute-start | bytes 884744 | tf_op jit(solution)/shard_map/ppermute | solution.py:18
  93.2 20.4 %collective-permute-start.40 = (bf16[192,768]{1,0:T(8,128)(2,1)S(1)}, bf16[192,768]{1,0:T(8,128)(2,1)S(1)}, u32[]{:S(2)}, u32[]{:S(2)}) collective-permute-start(bf16[192,768]{1,0:T(8,128)(2,1)S(1)} %get-tuple-element.91), channel_id=1, source_target_pairs={{0,4},{4,0},{8,12},{12,8},{1,5},{5,1},{9,13},{13,9},{2,6},{6,2},{1... | collective-permute-start | bytes 884744 | tf_op jit(solution)/shard_map/ppermute | solution.py:18
  104.7 6.2 %collective-permute-start.38 = (bf16[48,1024]{1,0:T(8,128)(2,1)S(1)}, bf16[48,1024]{1,0:T(8,128)(2,1)S(1)}, u32[]{:S(2)}, u32[]{:S(2)}) collective-permute-start(bf16[48,1024]{1,0:T(8,128)(2,1)S(1)} %get-tuple-element.105), channel_id=1, source_target_pairs={{0,2},{1,3},{2,0},{3,1},{4,6},{5,7},{6,4},{7,5},{8,10},{9,11},{10,... | collective-permute-start | bytes 294920 | tf_op jit(solution)/shard_map/ppermute | solution.py:18
  105.3 5.6 %collective-permute-start.37 = (bf16[48,1024]{1,0:T(8,128)(2,1)S(1)}, bf16[48,1024]{1,0:T(8,128)(2,1)S(1)}, u32[]{:S(2)}, u32[]{:S(2)}) collective-permute-start(bf16[48,1024]{1,0:T(8,128)(2,1)S(1)} %get-tuple-element.106), channel_id=1, source_target_pairs={{0,1},{1,0},{2,3},{3,2},{4,5},{5,4},{6,7},{7,6},{8,9},{9,8},{10,11... | collective-permute-start | bytes 294920 | tf_op jit(solution)/shard_map/ppermute | solution.py:18
  (28 other events, 208.1 us)

commit v7 on v6

--- a/solution.py
+++ b/solution.py
@@ -376,7 +376,7 @@
     terms_3 = terms_of(3, pieces_3, sent, *rows_2)
     near_blocks.append(swap(near_two, "tensor", 1, inner))
     opposite = [swap(after(t, near_blocks[3]), "tensor", 1, inner) for t in terms_3]
-    rows_1 = rows_of(1, near_blocks, *terms_3)
+    rows_1 = rows_of(1, near_blocks, *terms_3, *cross_2[0].values())
     cross_1 = cross(rows_1, "request")
     pieces_2 = spread(cross_2[:1], "request")
     pieces_2 += spread(cross_2[1:], "request", *rows_1)
@@ -389,7 +389,7 @@
     terms_1 = terms_of(1, pieces_1, sent, *sums)
     beside = [swap(t, "tensor", 1, inner) for t in terms_1]
     pieces_0 = spread(cross_0, "request", across[0], own=rows_0)
-    terms_0 = terms_of(0, pieces_0, jnp.float32, *terms_1)
+    terms_0 = terms_of(0, pieces_0, jnp.float32)
     handed = place_blocks(after(ids, *terms_0), arrived)
 
     columns = []

time: 122 us -> 122 us (level)
  no operation moved by 1% of the time
where the time goes in v7:
time: 122 us; the launch traced here: 121 us
  Pallas kernels  49.4 us (40%)
  starting transfers between devices  36.3 us (30%)
  waiting for transfers between devices  24.7 us (20%)
  local copies, waits for them, and re-layouts  9.59 us (8%)
    ppermute x45, starting transfers between devices, swap(): return lax.ppermute(value, axis, pairs)  36.3 us
    ppermute x45, waiting for transfers between devices, swap(): return lax.ppermute(value, axis, pairs)  24.7 us
    pallas_call x4, Pallas kernels, project(): pl.pallas_call(functools.partial(project_kernel, stretch, splits), grid=(...  22.2 us
    pallas_call x4, Pallas kernels, attend(): pl.pallas_call(functools.partial(attend_kernel, distance, scale), grid_sp...  20.2 us
    unnamed x30, local copies, waits for them, and re-layouts  8.44 us
    pallas_call x1, Pallas kernels, absorb(): pl.pallas_call(absorb_kernel, grid=(heads // step,), in_specs=[pl.BlockSp...  3.3 us
  transfers between devices with their start and end apart: 45, of which 11 were waited for; matrix products, arithmetic and copies ran while one was open for 0% of the time, Pallas kernels for 39%

profile of v7, /device:TPU:0, one launch (start us, length us, event | category | flops | bytes accessed | tf_op | source)
XLA Modules:
  0.0 121.4 jit_solution(11637086213097680686)
XLA Ops:
  1.8 4.1 %collective-permute-start.4 = (bf16[2,576,128]{2,1,0:T(8,128)(2,1)S(1)}, bf16[2,576,128]{2,1,0:T(8,128)(2,1)S(1)}, u32[]{:S(2)}, u32[]{:S(2)}) collective-permute-start(bf16[2,576,128]{2,1,0:T(8,128)(2,1)S(1)} %get-tuple-element.68.refs_0_), channel_id=1, source_target_pairs={{0,8},{4,12},{8,0},{12,4},{1,9},{5,13},{9,1},{13,5},{2,10},{6,14},... | collective-permute-start | bytes 884744 | tf_op jit(solution)/shard_map/ppermute | solution.py:18
  5.9 1.6 %collective-permute-start.3 = (bf16[2,576,128]{2,1,0:T(8,128)(2,1)S(1)}, bf16[2,576,128]{2,1,0:T(8,128)(2,1)S(1)}, u32[]{:S(2)}, u32[]{:S(2)}) collective-permute-start(bf16[2,576,128]{2,1,0:T(8,128)(2,1)S(1)} %get-tuple-element.69.refs_0_), channel_id=1, source_target_pairs={{0,4},{4,0},{8,12},{12,8},{1,5},{5,1},{9,13},{13,9},{2,6},{6,2},{1... | collective-permute-start | bytes 884744 | tf_op jit(solution)/shard_map/ppermute | solution.py:18
  12.1 2.2 %copy-done.1 = bf16[32,512,128]{2,1,0:T(8,128)(2,1)S(1)} copy-done((bf16[32,512,128]{2,1,0:T(8,128)(2,1)S(1)}, bf16[32,512,128]{2,1,0:T(8,128)(2,1)}, u32[]{:S(2)}) %copy-start.1) | copy-done | bytes 4194328
  14.3 1.4 %copy-done.3 = bf16[192,4096]{1,0:T(8,128)(2,1)S(1)} copy-done((bf16[192,4096]{1,0:T(8,128)(2,1)S(1)}, bf16[192,4096]{1,0:T(8,128)(2,1)}, u32[]{:S(2)}) %copy-start.3) | copy-done | bytes 1572888
  16.9 3.3 %absorb.1.query_ref = bf16[32,192,576]{2,1,0:T(8,128)(2,1)S(1)} custom-call(bf16[192,4096]{1,0:T(8,128)(2,1)S(1)} %copy-done.3, bf16[192,2048]{1,0:T(8,128)(2,1)S(1)} %copy-done.4, bf16[32,512,128]{2,1,0:T(8,128)(2,1)S(1)} %copy-done.1), custom_call_target="tpu_custom_call" | custom-call | flops 1 | bytes 1 | tf_op jit(solution)/shard_map/absorb/pallas_call | solution.py:77
  21.0 1.5 %collective-permute-start.1 = (bf16[576,128]{1,0:T(8,128)(2,1)S(1)}, bf16[576,128]{1,0:T(8,128)(2,1)S(1)}, u32[]{:S(2)}, u32[]{:S(2)}) collective-permute-start(bf16[576,128]{1,0:T(8,128)(2,1)S(1)} %get-tuple-element.58), channel_id=1, source_target_pairs={{0,2},{1,3},{2,0},{3,1},{4,6},{5,7},{6,4},{7,5},{8,10},{9,11},{10,... | collective-permute-start | bytes 442376 | tf_op jit(solution)/shard_map/ppermute | solution.py:18
  22.8 5.6 %collective-permute-done.5.refs_3_ = bf16[2,576,128]{2,1,0:T(8,128)(2,1)S(1)} collective-permute-done((bf16[2,576,128]{2,1,0:T(8,128)(2,1)S(1)}, bf16[2,576,128]{2,1,0:T(8,128)(2,1)S(1)}, u32[]{:S(2)}, u32[]{:S(2)}) %collective-permute-start.5) | collective-permute-done | bytes 294944 | tf_op jit(solution)/shard_map/ppermute | solution.py:18
  28.5 2.0 %collective-permute-start.9 = (bf16[2,576,128]{2,1,0:T(8,128)(2,1)S(1)}, bf16[2,576,128]{2,1,0:T(8,128)(2,1)S(1)}, u32[]{:S(2)}, u32[]{:S(2)}) collective-permute-start(bf16[2,576,128]{2,1,0:T(8,128)(2,1)S(1)} %get-tuple-element.69.refs_0_), channel_id=1, source_target_pairs={{0,8},{4,12},{8,0},{12,4},{1,9},{5,13},{9,1},{13,5},{2,10},{6,14},... | collective-permute-start | bytes 884744 | tf_op jit(solution)/shard_map/ppermute | solution.py:18
  30.5 1.7 %collective-permute-start.8 = (bf16[2,576,128]{2,1,0:T(8,128)(2,1)S(1)}, bf16[2,576,128]{2,1,0:T(8,128)(2,1)S(1)}, u32[]{:S(2)}, u32[]{:S(2)}) collective-permute-start(bf16[2,576,128]{2,1,0:T(8,128)(2,1)S(1)} %get-tuple-element.68.refs_0_), channel_id=1, source_target_pairs={{0,4},{4,0},{8,12},{12,8},{1,5},{5,1},{9,13},{13,9},{2,6},{6,2},{1... | collective-permute-start | bytes 884744 | tf_op jit(solution)/shard_map/ppermute | solution.py:18
  32.3 5.0 %attend_3.1 = (bf16[48,2048]{1,0:T(8,128)(2,1)S(1)}, bf16[48,2048]{1,0:T(8,128)(2,1)S(1)}) custom-call(s32[3]{0:T(128)S(1)} %pad_add_fusion.ids_ref, s32[4]{0:T(128)S(1)} %copy-done.6, s32[4]{0:T(128)S(1)} %copy-done.8, bf16[32,192,576]{2,1,0:T(8,128)(2,1)S(1)} %absorb.1.query_ref, bf16[2,576,128]{2,1,0:T(8,128)(2,1)S(1)} %get-tuple-element.69.refs_0_, ...), custom_call_target="tpu_custom_call" | custom-call | flops 1 | bytes 1 | tf_op jit(solution)/shard_map/attend_3/pallas_call | solution.py:157
  37.3 1.6 %collective-permute-start.7 = (bf16[48,2048]{1,0:T(8,128)(2,1)S(1)}, bf16[48,2048]{1,0:T(8,128)(2,1)S(1)}, u32[]{:S(2)}, u32[]{:S(2)}) collective-permute-start(bf16[48,2048]{1,0:T(8,128)(2,1)S(1)} %get-tuple-element.67.refs_0_), channel_id=1, source_target_pairs={{0,2},{1,3},{2,0},{3,1},{4,6},{5,7},{6,4},{7,5},{8,10},{9,11},{10,... | collective-permute-start | bytes 589832 | tf_op jit(solution)/shard_map/ppermute | solution.py:18
  39.4 5.0 %attend_2.1 = (bf16[48,2048]{1,0:T(8,128)(2,1)S(1)}, bf16[48,2048]{1,0:T(8,128)(2,1)S(1)}) custom-call(s32[3]{0:T(128)S(1)} %pad_add_fusion.ids_ref, s32[4]{0:T(128)S(1)} %copy-done.6, s32[4]{0:T(128)S(1)} %copy-done.8, bf16[32,192,576]{2,1,0:T(8,128)(2,1)S(1)} %absorb.1.query_ref, bf16[2,576,128]{2,1,0:T(8,128)(2,1)S(1)} %get-tuple-element.69.refs_0_, ...), custom_call_target="tpu_custom_call" | custom-call | flops 1 | bytes 1 | tf_op jit(solution)/shard_map/attend_2/pallas_call | solution.py:157
  47.0 1.5 %collective-permute-start.14 = (bf16[48,2048]{1,0:T(8,128)(2,1)S(1)}, bf16[48,2048]{1,0:T(8,128)(2,1)S(1)}, u32[]{:S(2)}, u32[]{:S(2)}) collective-permute-start(bf16[48,2048]{1,0:T(8,128)(2,1)S(1)} %get-tuple-element.78.refs_0_), channel_id=1, source_target_pairs={{0,2},{1,3},{2,0},{3,1},{4,6},{5,7},{6,4},{7,5},{8,10},{9,11},{10,... | collective-permute-start | bytes 589832 | tf_op jit(solution)/shard_map/ppermute | solution.py:18
  49.1 5.5 %project_3.1 = (bf16[192,1024]{1,0:T(8,128)(2,1)S(1)}, bf16[192,768]{1,0:T(8,128)(2,1)S(1)}) custom-call(bf16[48,2048]{1,0:T(8,128)(2,1)S(1)} %get-tuple-element.67.refs_0_, bf16[48,2048]{1,0:T(8,128)(2,1)S(1)} %collective-permute-done.6.refs_1_, bf16[48,2048]{1,0:T(8,128)(2,1)S(1)} %collective-permute-done.7.refs_2_, ...), custom_call_target="tpu_custom_call" | custom-call | flops 1 | bytes 1 | tf_op jit(solution)/shard_map/project_3/pallas_call | solution.py:217
  55.9 5.0 %attend_1.1 = (bf16[48,2048]{1,0:T(8,128)(2,1)S(1)}, bf16[48,2048]{1,0:T(8,128)(2,1)S(1)}) custom-call(s32[3]{0:T(128)S(1)} %pad_add_fusion.ids_ref, s32[4]{0:T(128)S(1)} %copy-done.6, s32[4]{0:T(128)S(1)} %copy-done.8, bf16[32,192,576]{2,1,0:T(8,128)(2,1)S(1)} %absorb.1.query_ref, bf16[2,576,128]{2,1,0:T(8,128)(2,1)S(1)} %get-tuple-element.68.refs_0_, ...), custom_call_target="tpu_custom_call" | custom-call | flops 1 | bytes 1 | tf_op jit(solution)/shard_map/attend_1/pallas_call | solution.py:157
  62.6 1.5 %collective-permute-start.31 = (bf16[48,2048]{1,0:T(8,128)(2,1)S(1)}, bf16[48,2048]{1,0:T(8,128)(2,1)S(1)}, u32[]{:S(2)}, u32[]{:S(2)}) collective-permute-start(bf16[48,2048]{1,0:T(8,128)(2,1)S(1)} %get-tuple-element.92.refs_0_), channel_id=1, source_target_pairs={{0,2},{1,3},{2,0},{3,1},{4,6},{5,7},{6,4},{7,5},{8,10},{9,11},{10,... | collective-permute-start | bytes 589832 | tf_op jit(solution)/shard_map/ppermute | solution.py:18
  64.7 5.6 %project_2.1 = (f32[192,1024]{1,0:T(8,128)S(1)}, f32[192,768]{1,0:T(8,128)S(1)}) custom-call(bf16[48,2048]{1,0:T(8,128)(2,1)S(1)} %get-tuple-element.78.refs_0_, bf16[48,2048]{1,0:T(8,128)(2,1)S(1)} %collective-permute-done.16.refs_1_, bf16[48,2048]{1,0:T(8,128)(2,1)S(1)} %collective-permute-done.14.refs_2_, ...), custom_call_target="tpu_custom_call" | custom-call | flops 1 | bytes 1 | tf_op jit(solution)/shard_map/project_2/pallas_call | solution.py:217
  70.9 1.7 %collective-permute-done.21 = bf16[192,1024]{1,0:T(8,128)(2,1)S(1)} collective-permute-done((bf16[192,1024]{1,0:T(8,128)(2,1)S(1)}, bf16[192,1024]{1,0:T(8,128)(2,1)S(1)}, u32[]{:S(2)}, u32[]{:S(2)}) %collective-permute-start.21) | collective-permute-done | bytes 393248 | tf_op jit(solution)/shard_map/ppermute | solution.py:18
  72.7 1.7 %collective-permute-start.25 = (bf16[192,1024]{1,0:T(8,128)(2,1)S(1)}, bf16[192,1024]{1,0:T(8,128)(2,1)S(1)}, u32[]{:S(2)}, u32[]{:S(2)}) collective-permute-start(bf16[192,1024]{1,0:T(8,128)(2,1)S(1)} %add_convert_fusion.1), channel_id=1, source_target_pairs={{0,8},{4,12},{8,0},{12,4},{1,9},{5,13},{9,1},{13,5},{2,10},{6,14},... | collective-permute-start | bytes 1179656 | tf_op jit(solution)/shard_map/ppermute | solution.py:18
  74.9 5.0 %attend_0.1 = (bf16[48,2048]{1,0:T(8,128)(2,1)S(1)}, bf16[48,2048]{1,0:T(8,128)(2,1)S(1)}) custom-call(s32[3]{0:T(128)S(1)} %pad_add_fusion.ids_ref, s32[4]{0:T(128)S(1)} %copy-done.6, s32[4]{0:T(128)S(1)} %copy-done.8, bf16[32,192,576]{2,1,0:T(8,128)(2,1)S(1)} %absorb.1.query_ref, bf16[2,576,128]{2,1,0:T(8,128)(2,1)S(1)} %get-tuple-element.68.refs_0_, ...), custom_call_target="tpu_custom_call" | custom-call | flops 1 | bytes 1 | tf_op jit(solution)/shard_map/attend_0/pallas_call | solution.py:157
  80.0 1.5 %collective-permute-start.28 = (bf16[48,2048]{1,0:T(8,128)(2,1)S(1)}, bf16[48,2048]{1,0:T(8,128)(2,1)S(1)}, u32[]{:S(2)}, u32[]{:S(2)}) collective-permute-start(bf16[48,2048]{1,0:T(8,128)(2,1)S(1)} %get-tuple-element.89.refs_4_), channel_id=1, source_target_pairs={{0,2},{1,3},{2,0},{3,1},{4,6},{5,7},{6,4},{7,5},{8,10},{9,11},{10,... | collective-permute-start | bytes 589832 | tf_op jit(solution)/shard_map/ppermute | solution.py:18
  82.1 5.5 %project_1.1 = (bf16[192,1024]{1,0:T(8,128)(2,1)S(1)}, bf16[192,768]{1,0:T(8,128)(2,1)S(1)}) custom-call(bf16[48,2048]{1,0:T(8,128)(2,1)S(1)} %get-tuple-element.92.refs_0_, bf16[48,2048]{1,0:T(8,128)(2,1)S(1)} %collective-permute-done.30.refs_1_, bf16[48,2048]{1,0:T(8,128)(2,1)S(1)} %collective-permute-done.31.refs_2_, ...), custom_call_target="tpu_custom_call" | custom-call | flops 1 | bytes 1 | tf_op jit(solution)/shard_map/project_1/pallas_call | solution.py:217
  87.6 1.5 %collective-permute-start.36 = (bf16[192,1024]{1,0:T(8,128)(2,1)S(1)}, bf16[192,1024]{1,0:T(8,128)(2,1)S(1)}, u32[]{:S(2)}, u32[]{:S(2)}) collective-permute-start(bf16[192,1024]{1,0:T(8,128)(2,1)S(1)} %get-tuple-element.95), channel_id=1, source_target_pairs={{0,4},{4,0},{8,12},{12,8},{1,5},{5,1},{9,13},{13,9},{2,6},{6,2},{1... | collective-permute-start | bytes 1179656 | tf_op jit(solution)/shard_map/ppermute | solution.py:18
  89.6 3.1 %collective-permute-done.25 = bf16[192,1024]{1,0:T(8,128)(2,1)S(1)} collective-permute-done((bf16[192,1024]{1,0:T(8,128)(2,1)S(1)}, bf16[192,1024]{1,0:T(8,128)(2,1)S(1)}, u32[]{:S(2)}, u32[]{:S(2)}) %collective-permute-start.25) | collective-permute-done | bytes 393248 | tf_op jit(solution)/shard_map/ppermute | solution.py:18
  93.2 3.0 %collective-permute-start.40 = (bf16[192,768]{1,0:T(8,128)(2,1)S(1)}, bf16[192,768]{1,0:T(8,128)(2,1)S(1)}, u32[]{:S(2)}, u32[]{:S(2)}) collective-permute-start(bf16[192,768]{1,0:T(8,128)(2,1)S(1)} %get-tuple-element.98), channel_id=1, source_target_pairs={{0,4},{4,0},{8,12},{12,8},{1,5},{5,1},{9,13},{13,9},{2,6},{6,2},{1... | collective-permute-start | bytes 884744 | tf_op jit(solution)/shard_map/ppermute | solution.py:18
  96.2 5.6 %project_0.1 = (f32[192,1024]{1,0:T(8,128)S(1)}, f32[192,768]{1,0:T(8,128)S(1)}) custom-call(bf16[48,2048]{1,0:T(8,128)(2,1)S(1)} %get-tuple-element.87.refs_0_, bf16[48,2048]{1,0:T(8,128)(2,1)S(1)} %collective-permute-done.23.refs_1_, bf16[48,2048]{1,0:T(8,128)(2,1)S(1)} %collective-permute-done.24.refs_2_, ...), custom_call_target="tpu_custom_call" | custom-call | flops 1 | bytes 1 | tf_op jit(solution)/shard_map/project_0/pallas_call | solution.py:217
  101.8 1.6 %collective-permute-done.36 = bf16[192,1024]{1,0:T(8,128)(2,1)S(1)} collective-permute-done((bf16[192,1024]{1,0:T(8,128)(2,1)S(1)}, bf16[192,1024]{1,0:T(8,128)(2,1)S(1)}, u32[]{:S(2)}, u32[]{:S(2)}) %collective-permute-start.36) | collective-permute-done | bytes 393248 | tf_op jit(solution)/shard_map/ppermute | solution.py:18
  105.6 3.1 %collective-permute-done.39.refs_6_ = bf16[48,1024]{1,0:T(8,128)(2,1)S(1)} collective-permute-done((bf16[48,1024]{1,0:T(8,128)(2,1)S(1)}, bf16[48,1024]{1,0:T(8,128)(2,1)S(1)}, u32[]{:S(2)}, u32[]{:S(2)}) %collective-permute-start.39) | collective-permute-done | bytes 98336 | tf_op jit(solution)/shard_map/ppermute | solution.py:18
  108.7 2.2 %collective-permute-done.38.refs_4_ = bf16[48,1024]{1,0:T(8,128)(2,1)S(1)} collective-permute-done((bf16[48,1024]{1,0:T(8,128)(2,1)S(1)}, bf16[48,1024]{1,0:T(8,128)(2,1)S(1)}, u32[]{:S(2)}, u32[]{:S(2)}) %collective-permute-start.38) | collective-permute-done | bytes 98336 | tf_op jit(solution)/shard_map/ppermute | solution.py:18
  110.9 2.7 %collective-permute-done.40 = bf16[192,768]{1,0:T(8,128)(2,1)S(1)} collective-permute-done((bf16[192,768]{1,0:T(8,128)(2,1)S(1)}, bf16[192,768]{1,0:T(8,128)(2,1)S(1)}, u32[]{:S(2)}, u32[]{:S(2)}) %collective-permute-start.40) | collective-permute-done | bytes 294944 | tf_op jit(solution)/shard_map/ppermute | solution.py:18
  118.2 1.8 %collective-permute-done.43.refs_5_ = bf16[48,768]{1,0:T(8,128)(2,1)S(1)} collective-permute-done((bf16[48,768]{1,0:T(8,128)(2,1)S(1)}, bf16[48,768]{1,0:T(8,128)(2,1)S(1)}, u32[]{:S(2)}, u32[]{:S(2)}) %collective-permute-start.43) | collective-permute-done | bytes 73760 | tf_op jit(solution)/shard_map/ppermute | solution.py:18
  120.0 1.4 %place_columns.1 = bf16[48,7168]{1,0:T(8,128)(2,1)} custom-call(s32[3]{0:T(128)S(1)} %pad_add_fusion.ids_ref, bf16[48,1024]{1,0:T(8,128)(2,1)S(1)} %get-tuple-element.105.refs_0_, bf16[48,768]{1,0:T(8,128)(2,1)S(1)} %get-tuple-element.109.refs_1_, bf16[48,1024]{1,0:T(8,128)(2,1)S(1)} %collective-permute-done.37.refs_2_, ...), custom_call_target="tpu_custom_call" | custom-call | tf_op jit(solution)/shard_map/place_columns/pallas_call | solution.py:288
  (109 shorter events, 24.7 us)
Async XLA Ops:
  1.8 18.4 %collective-permute-start.4 = (bf16[2,576,128]{2,1,0:T(8,128)(2,1)S(1)}, bf16[2,576,128]{2,1,0:T(8,128)(2,1)S(1)}, u32[]{:S(2)}, u32[]{:S(2)}) collective-permute-start(bf16[2,576,128]{2,1,0:T(8,128)(2,1)S(1)} %get-tuple-element.68.refs_0_), channel_id=1, source_target_pairs={{0,8},{4,12},{8,0},{12,4},{1,9},{5,13},{9,1},{13,5},{2,10},{6,14},... | collective-permute-start | bytes 884744 | tf_op jit(solution)/shard_map/ppermute | solution.py:18
  5.9 14.3 %collective-permute-start.3 = (bf16[2,576,128]{2,1,0:T(8,128)(2,1)S(1)}, bf16[2,576,128]{2,1,0:T(8,128)(2,1)S(1)}, u32[]{:S(2)}, u32[]{:S(2)}) collective-permute-start(bf16[2,576,128]{2,1,0:T(8,128)(2,1)S(1)} %get-tuple-element.69.refs_0_), channel_id=1, source_target_pairs={{0,4},{4,0},{8,12},{12,8},{1,5},{5,1},{9,13},{13,9},{2,6},{6,2},{1... | collective-permute-start | bytes 884744 | tf_op jit(solution)/shard_map/ppermute | solution.py:18
  20.2 8.3 %collective-permute-start.5 = (bf16[2,576,128]{2,1,0:T(8,128)(2,1)S(1)}, bf16[2,576,128]{2,1,0:T(8,128)(2,1)S(1)}, u32[]{:S(2)}, u32[]{:S(2)}) collective-permute-start(bf16[2,576,128]{2,1,0:T(8,128)(2,1)S(1)} %collective-permute-done.4.refs_2_), channel_id=1, source_target_pairs={{0,4},{4,0},{8,12},{12,8},{1,5},{5,1},{9,13},{13,9},{2,6},{6,2},{1... | collective-permute-start | bytes 884744 | tf_op jit(solution)/shard_map/ppermute | solution.py:18
  21.0 11.3 %collective-permute-start = (bf16[576,128]{1,0:T(8,128)(2,1)S(1)}, bf16[576,128]{1,0:T(8,128)(2,1)S(1)}, u32[]{:S(2)}, u32[]{:S(2)}) collective-permute-start(bf16[576,128]{1,0:T(8,128)(2,1)S(1)} %get-tuple-element.57), channel_id=1, source_target_pairs={{0,1},{1,0},{2,3},{3,2},{4,5},{5,4},{6,7},{7,6},{8,9},{9,8},{10,11... | collective-permute-start | bytes 442376 | tf_op jit(solution)/shard_map/ppermute | solution.py:18
  21.0 11.3 %collective-permute-start.1 = (bf16[576,128]{1,0:T(8,128)(2,1)S(1)}, bf16[576,128]{1,0:T(8,128)(2,1)S(1)}, u32[]{:S(2)}, u32[]{:S(2)}) collective-permute-start(bf16[576,128]{1,0:T(8,128)(2,1)S(1)} %get-tuple-element.58), channel_id=1, source_target_pairs={{0,2},{1,3},{2,0},{3,1},{4,6},{5,7},{6,4},{7,5},{8,10},{9,11},{10,... | collective-permute-start | bytes 442376 | tf_op jit(solution)/shard_map/ppermute | solution.py:18
  22.5 9.8 %collective-permute-start.2 = (bf16[576,128]{1,0:T(8,128)(2,1)S(1)}, bf16[576,128]{1,0:T(8,128)(2,1)S(1)}, u32[]{:S(2)}, u32[]{:S(2)}) collective-permute-start(bf16[576,128]{1,0:T(8,128)(2,1)S(1)} %get-tuple-element.59), channel_id=1, source_target_pairs={{0,3},{1,2},{2,1},{3,0},{4,7},{5,6},{6,5},{7,4},{8,11},{9,10},{10,... | collective-permute-start | bytes 442376 | tf_op jit(solution)/shard_map/ppermute | solution.py:18
  28.5 16.6 %collective-permute-start.9 = (bf16[2,576,128]{2,1,0:T(8,128)(2,1)S(1)}, bf16[2,576,128]{2,1,0:T(8,128)(2,1)S(1)}, u32[]{:S(2)}, u32[]{:S(2)}) collective-permute-start(bf16[2,576,128]{2,1,0:T(8,128)(2,1)S(1)} %get-tuple-element.69.refs_0_), channel_id=1, source_target_pairs={{0,8},{4,12},{8,0},{12,4},{1,9},{5,13},{9,1},{13,5},{2,10},{6,14},... | collective-permute-start | bytes 884744 | tf_op jit(solution)/shard_map/ppermute | solution.py:18
  30.5 15.1 %collective-permute-start.8 = (bf16[2,576,128]{2,1,0:T(8,128)(2,1)S(1)}, bf16[2,576,128]{2,1,0:T(8,128)(2,1)S(1)}, u32[]{:S(2)}, u32[]{:S(2)}) collective-permute-start(bf16[2,576,128]{2,1,0:T(8,128)(2,1)S(1)} %get-tuple-element.68.refs_0_), channel_id=1, source_target_pairs={{0,4},{4,0},{8,12},{12,8},{1,5},{5,1},{9,13},{13,9},{2,6},{6,2},{1... | collective-permute-start | bytes 884744 | tf_op jit(solution)/shard_map/ppermute | solution.py:18
  37.3 7.6 %collective-permute-start.7 = (bf16[48,2048]{1,0:T(8,128)(2,1)S(1)}, bf16[48,2048]{1,0:T(8,128)(2,1)S(1)}, u32[]{:S(2)}, u32[]{:S(2)}) collective-permute-start(bf16[48,2048]{1,0:T(8,128)(2,1)S(1)} %get-tuple-element.67.refs_0_), channel_id=1, source_target_pairs={{0,2},{1,3},{2,0},{3,1},{4,6},{5,7},{6,4},{7,5},{8,10},{9,11},{10,... | collective-permute-start | bytes 589832 | tf_op jit(solution)/shard_map/ppermute | solution.py:18
  38.9 8.1 %collective-permute-start.12 = (bf16[48,2048]{1,0:T(8,128)(2,1)S(1)}, bf16[48,2048]{1,0:T(8,128)(2,1)S(1)}, u32[]{:S(2)}, u32[]{:S(2)}) collective-permute-start(bf16[48,2048]{1,0:T(8,128)(2,1)S(1)} %get-tuple-element.71.refs_4_), channel_id=1, source_target_pairs={{0,2},{1,3},{2,0},{3,1},{4,6},{5,7},{6,4},{7,5},{8,10},{9,11},{10,... | collective-permute-start | bytes 589832 | tf_op jit(solution)/shard_map/ppermute | solution.py:18
  45.0 9.6 %collective-permute-start.15 = (bf16[2,576,128]{2,1,0:T(8,128)(2,1)S(1)}, bf16[2,576,128]{2,1,0:T(8,128)(2,1)S(1)}, u32[]{:S(2)}, u32[]{:S(2)}) collective-permute-start(bf16[2,576,128]{2,1,0:T(8,128)(2,1)S(1)} %collective-permute-done.9.refs_2_), channel_id=1, source_target_pairs={{0,4},{4,0},{8,12},{12,8},{1,5},{5,1},{9,13},{13,9},{2,6},{6,2},{1... | collective-permute-start | bytes 884744 | tf_op jit(solution)/shard_map/ppermute | solution.py:18
  47.0 8.6 %collective-permute-start.14 = (bf16[48,2048]{1,0:T(8,128)(2,1)S(1)}, bf16[48,2048]{1,0:T(8,128)(2,1)S(1)}, u32[]{:S(2)}, u32[]{:S(2)}) collective-permute-start(bf16[48,2048]{1,0:T(8,128)(2,1)S(1)} %get-tuple-element.78.refs_0_), channel_id=1, source_target_pairs={{0,2},{1,3},{2,0},{3,1},{4,6},{5,7},{6,4},{7,5},{8,10},{9,11},{10,... | collective-permute-start | bytes 589832 | tf_op jit(solution)/shard_map/ppermute | solution.py:18
  48.5 12.5 %collective-permute-start.19 = (bf16[48,2048]{1,0:T(8,128)(2,1)S(1)}, bf16[48,2048]{1,0:T(8,128)(2,1)S(1)}, u32[]{:S(2)}, u32[]{:S(2)}) collective-permute-start(bf16[48,2048]{1,0:T(8,128)(2,1)S(1)} %get-tuple-element.66.refs_4_), channel_id=1, source_target_pairs={{0,2},{1,3},{2,0},{3,1},{4,6},{5,7},{6,4},{7,5},{8,10},{9,11},{10,... | collective-permute-start | bytes 589832 | tf_op jit(solution)/shard_map/ppermute | solution.py:18
  49.1 12.2 %collective-permute-start.16 = (bf16[48,2048]{1,0:T(8,128)(2,1)S(1)}, bf16[48,2048]{1,0:T(8,128)(2,1)S(1)}, u32[]{:S(2)}, u32[]{:S(2)}) collective-permute-start(bf16[48,2048]{1,0:T(8,128)(2,1)S(1)} %get-tuple-element.78.refs_0_), channel_id=1, source_target_pairs={{0,1},{1,0},{2,3},{3,2},{4,5},{5,4},{6,7},{7,6},{8,9},{9,8},{10,11... | collective-permute-start | bytes 589832 | tf_op jit(solution)/shard_map/ppermute | solution.py:18
  54.7 15.6 %collective-permute-start.22 = (bf16[192,768]{1,0:T(8,128)(2,1)S(1)}, bf16[192,768]{1,0:T(8,128)(2,1)S(1)}, u32[]{:S(2)}, u32[]{:S(2)}) collective-permute-start(bf16[192,768]{1,0:T(8,128)(2,1)S(1)} %get-tuple-element.83), channel_id=1, source_target_pairs={{0,4},{4,0},{8,12},{12,8},{1,5},{5,1},{9,13},{13,9},{2,6},{6,2},{1... | collective-permute-start | bytes 884744 | tf_op jit(solution)/shard_map/ppermute | solution.py:18
  55.4 7.2 %collective-permute-start.18 = (bf16[48,2048]{1,0:T(8,128)(2,1)S(1)}, bf16[48,2048]{1,0:T(8,128)(2,1)S(1)}, u32[]{:S(2)}, u32[]{:S(2)}) collective-permute-start(bf16[48,2048]{1,0:T(8,128)(2,1)S(1)} %get-tuple-element.66.refs_4_), channel_id=1, source_target_pairs={{0,1},{1,0},{2,3},{3,2},{4,5},{5,4},{6,7},{7,6},{8,9},{9,8},{10,11... | collective-permute-start | bytes 589832 | tf_op jit(solution)/shard_map/ppermute | solution.py:18
  55.6 8.5 %collective-permute-start.17 = (bf16[48,2048]{1,0:T(8,128)(2,1)S(1)}, bf16[48,2048]{1,0:T(8,128)(2,1)S(1)}, u32[]{:S(2)}, u32[]{:S(2)}) collective-permute-start(bf16[48,2048]{1,0:T(8,128)(2,1)S(1)} %collective-permute-done.14.refs_2_), channel_id=1, source_target_pairs={{0,1},{1,0},{2,3},{3,2},{4,5},{5,4},{6,7},{7,6},{8,9},{9,8},{10,11... | collective-permute-start | bytes 589832 | tf_op jit(solution)/shard_map/ppermute | solution.py:18
  61.3 11.3 %collective-permute-start.21 = (bf16[192,1024]{1,0:T(8,128)(2,1)S(1)}, bf16[192,1024]{1,0:T(8,128)(2,1)S(1)}, u32[]{:S(2)}, u32[]{:S(2)}) collective-permute-start(bf16[192,1024]{1,0:T(8,128)(2,1)S(1)} %get-tuple-element.81), channel_id=1, source_target_pairs={{0,4},{4,0},{8,12},{12,8},{1,5},{5,1},{9,13},{13,9},{2,6},{6,2},{1... | collective-permute-start | bytes 1179656 | tf_op jit(solution)/shard_map/ppermute | solution.py:18
  62.6 11.8 %collective-permute-start.31 = (bf16[48,2048]{1,0:T(8,128)(2,1)S(1)}, bf16[48,2048]{1,0:T(8,128)(2,1)S(1)}, u32[]{:S(2)}, u32[]{:S(2)}) collective-permute-start(bf16[48,2048]{1,0:T(8,128)(2,1)S(1)} %get-tuple-element.92.refs_0_), channel_id=1, source_target_pairs={{0,2},{1,3},{2,0},{3,1},{4,6},{5,7},{6,4},{7,5},{8,10},{9,11},{10,... | collective-permute-start | bytes 589832 | tf_op jit(solution)/shard_map/ppermute | solution.py:18
  64.1 10.3 %collective-permute-start.34 = (bf16[48,2048]{1,0:T(8,128)(2,1)S(1)}, bf16[48,2048]{1,0:T(8,128)(2,1)S(1)}, u32[]{:S(2)}, u32[]{:S(2)}) collective-permute-start(bf16[48,2048]{1,0:T(8,128)(2,1)S(1)} %get-tuple-element.77.refs_4_), channel_id=1, source_target_pairs={{0,2},{1,3},{2,0},{3,1},{4,6},{5,7},{6,4},{7,5},{8,10},{9,11},{10,... | collective-permute-start | bytes 589832 | tf_op jit(solution)/shard_map/ppermute | solution.py:18
  64.7 15.3 %collective-permute-start.33 = (bf16[48,2048]{1,0:T(8,128)(2,1)S(1)}, bf16[48,2048]{1,0:T(8,128)(2,1)S(1)}, u32[]{:S(2)}, u32[]{:S(2)}) collective-permute-start(bf16[48,2048]{1,0:T(8,128)(2,1)S(1)} %get-tuple-element.77.refs_4_), channel_id=1, source_target_pairs={{0,1},{1,0},{2,3},{3,2},{4,5},{5,4},{6,7},{7,6},{8,9},{9,8},{10,11... | collective-permute-start | bytes 589832 | tf_op jit(solution)/shard_map/ppermute | solution.py:18
  70.3 11.3 %collective-permute-start.30 = (bf16[48,2048]{1,0:T(8,128)(2,1)S(1)}, bf16[48,2048]{1,0:T(8,128)(2,1)S(1)}, u32[]{:S(2)}, u32[]{:S(2)}) collective-permute-start(bf16[48,2048]{1,0:T(8,128)(2,1)S(1)} %get-tuple-element.92.refs_0_), channel_id=1, source_target_pairs={{0,1},{1,0},{2,3},{3,2},{4,5},{5,4},{6,7},{7,6},{8,9},{9,8},{10,11... | collective-permute-start | bytes 589832 | tf_op jit(solution)/shard_map/ppermute | solution.py:18
  72.7 20.0 %collective-permute-start.25 = (bf16[192,1024]{1,0:T(8,128)(2,1)S(1)}, bf16[192,1024]{1,0:T(8,128)(2,1)S(1)}, u32[]{:S(2)}, u32[]{:S(2)}) collective-permute-start(bf16[192,1024]{1,0:T(8,128)(2,1)S(1)} %add_convert_fusion.1), channel_id=1, source_target_pairs={{0,8},{4,12},{8,0},{12,4},{1,9},{5,13},{9,1},{13,5},{2,10},{6,14},... | collective-permute-start | bytes 1179656 | tf_op jit(solution)/shard_map/ppermute | solution.py:18
  74.4 7.7 %collective-permute-start.32 = (bf16[48,2048]{1,0:T(8,128)(2,1)S(1)}, bf16[48,2048]{1,0:T(8,128)(2,1)S(1)}, u32[]{:S(2)}, u32[]{:S(2)}) collective-permute-start(bf16[48,2048]{1,0:T(8,128)(2,1)S(1)} %collective-permute-done.31.refs_2_), channel_id=1, source_target_pairs={{0,1},{1,0},{2,3},{3,2},{4,5},{5,4},{6,7},{7,6},{8,9},{9,8},{10,11... | collective-permute-start | bytes 589832 | tf_op jit(solution)/shard_map/ppermute | solution.py:18
  74.4 7.7 %collective-permute-start.35 = (bf16[48,2048]{1,0:T(8,128)(2,1)S(1)}, bf16[48,2048]{1,0:T(8,128)(2,1)S(1)}, u32[]{:S(2)}, u32[]{:S(2)}) collective-permute-start(bf16[48,2048]{1,0:T(8,128)(2,1)S(1)} %collective-permute-done.34.refs_6_), channel_id=1, source_target_pairs={{0,1},{1,0},{2,3},{3,2},{4,5},{5,4},{6,7},{7,6},{8,9},{9,8},{10,11... | collective-permute-start | bytes 589832 | tf_op jit(solution)/shard_map/ppermute | solution.py:18
  80.0 9.1 %collective-permute-start.28 = (bf16[48,2048]{1,0:T(8,128)(2,1)S(1)}, bf16[48,2048]{1,0:T(8,128)(2,1)S(1)}, u32[]{:S(2)}, u32[]{:S(2)}) collective-permute-start(bf16[48,2048]{1,0:T(8,128)(2,1)S(1)} %get-tuple-element.89.refs_4_), channel_id=1, source_target_pairs={{0,2},{1,3},{2,0},{3,1},{4,6},{5,7},{6,4},{7,5},{8,10},{9,11},{10,... | collective-permute-start | bytes 589832 | tf_op jit(solution)/shard_map/ppermute | solution.py:18
  81.5 11.2 %collective-permute-start.24 = (bf16[48,2048]{1,0:T(8,128)(2,1)S(1)}, bf16[48,2048]{1,0:T(8,128)(2,1)S(1)}, u32[]{:S(2)}, u32[]{:S(2)}) collective-permute-start(bf16[48,2048]{1,0:T(8,128)(2,1)S(1)} %get-tuple-element.87.refs_0_), channel_id=1, source_target_pairs={{0,2},{1,3},{2,0},{3,1},{4,6},{5,7},{6,4},{7,5},{8,10},{9,11},{10,... | collective-permute-start | bytes 589832 | tf_op jit(solution)/shard_map/ppermute | solution.py:18
  87.6 15.8 %collective-permute-start.36 = (bf16[192,1024]{1,0:T(8,128)(2,1)S(1)}, bf16[192,1024]{1,0:T(8,128)(2,1)S(1)}, u32[]{:S(2)}, u32[]{:S(2)}) collective-permute-start(bf16[192,1024]{1,0:T(8,128)(2,1)S(1)} %get-tuple-element.95), channel_id=1, source_target_pairs={{0,4},{4,0},{8,12},{12,8},{1,5},{5,1},{9,13},{13,9},{2,6},{6,2},{1... | collective-permute-start | bytes 1179656 | tf_op jit(solution)/shard_map/ppermute | solution.py:18
  93.2 17.7 %collective-permute-start.41 = (bf16[192,768]{1,0:T(8,128)(2,1)S(1)}, bf16[192,768]{1,0:T(8,128)(2,1)S(1)}, u32[]{:S(2)}, u32[]{:S(2)}) collective-permute-start(bf16[192,768]{1,0:T(8,128)(2,1)S(1)} %add_convert_fusion.3), channel_id=1, source_target_pairs={{0,8},{4,12},{8,0},{12,4},{1,9},{5,13},{9,1},{13,5},{2,10},{6,14},... | collective-permute-start | bytes 884744 | tf_op jit(solution)/shard_map/ppermute | solution.py:18
  93.2 20.4 %collective-permute-start.40 = (bf16[192,768]{1,0:T(8,128)(2,1)S(1)}, bf16[192,768]{1,0:T(8,128)(2,1)S(1)}, u32[]{:S(2)}, u32[]{:S(2)}) collective-permute-start(bf16[192,768]{1,0:T(8,128)(2,1)S(1)} %get-tuple-element.98), channel_id=1, source_target_pairs={{0,4},{4,0},{8,12},{12,8},{1,5},{5,1},{9,13},{13,9},{2,6},{6,2},{1... | collective-permute-start | bytes 884744 | tf_op jit(solution)/shard_map/ppermute | solution.py:18
  104.7 6.2 %collective-permute-start.38 = (bf16[48,1024]{1,0:T(8,128)(2,1)S(1)}, bf16[48,1024]{1,0:T(8,128)(2,1)S(1)}, u32[]{:S(2)}, u32[]{:S(2)}) collective-permute-start(bf16[48,1024]{1,0:T(8,128)(2,1)S(1)} %get-tuple-element.103), channel_id=1, source_target_pairs={{0,2},{1,3},{2,0},{3,1},{4,6},{5,7},{6,4},{7,5},{8,10},{9,11},{10,... | collective-permute-start | bytes 294920 | tf_op jit(solution)/shard_map/ppermute | solution.py:18
  105.3 5.6 %collective-permute-start.37 = (bf16[48,1024]{1,0:T(8,128)(2,1)S(1)}, bf16[48,1024]{1,0:T(8,128)(2,1)S(1)}, u32[]{:S(2)}, u32[]{:S(2)}) collective-permute-start(bf16[48,1024]{1,0:T(8,128)(2,1)S(1)} %get-tuple-element.104), channel_id=1, source_target_pairs={{0,1},{1,0},{2,3},{3,2},{4,5},{5,4},{6,7},{7,6},{8,9},{9,8},{10,11... | collective-permute-start | bytes 294920 | tf_op jit(solution)/shard_map/ppermute | solution.py:18
  (28 other events, 208.1 us)
